TPU v7x, 256 devices: a whole 4x4x8 slice. The times are simulated.
256 devices in a mesh: block: 8 (over x, core), space: 32 (over y, z).
Axes of the slice: x: 4, y: 4, z: 8, core: 2. Of those that a mesh axis runs over, the one named last changes fastest.
Arguments:
- snapshots: bfloat16 [32, 32, 2, 256, 3, 256], P('space', None, None, 'block'), may hold values from -6 to 6
- slot_line: int32 [32, 32, 2], replicated, may hold values from -1 to 31, as said below
- freq_ids: int32 [24], replicated, may hold values from 0 to 128, as said below
- metrics: float32 [4, 128, 256], P(None, 'space'), may hold values from -1.5 to 1.5
- weights: float32 [128, 256], P('space'), may hold values from 0.25 to 12, as said below
- stored_spectra: bfloat16 [24, 2, 2, 3, 128, 8, 256], P('block', None, None, None, 'space'), may hold values from -6 to 6
Outputs:
- spectra: bfloat16 [24, 2, 3, 128, 8, 256], P('block', None, None, 'space')
- gram: float32 [24, 2, 3, 3], P('block')
Inputs may be any that keep to these rules, and one draw needn't show every extreme that they name: slot_line[h, d, s] is the local index (pitch-major, 8 per pitch line) of the owner d line that holder h keeps in slot s, or -1 for an empty slot. Each of an owner's 32 lines stands in exactly one slot; for every owner some holder fills all 2 of its slots. `freq_ids`: distinct values. `weights`: Positive.
All inputs are finite; a program needn't handle non-finite values.
Results may differ from a plain program's by a relative error of at most 0.008.
Values may be sent and summed in bfloat16 or wider, within the bound.
No kernel may reach another device: no remote copies, remote signals or barrier semaphores. Data moves between devices by JAX's collectives and lax.ppermute only.
A program may use at most 320 MiB of HBM per device.

v0:
```python
import math

import jax
import jax.numpy as jnp
from jax import lax
from jax.sharding import PartitionSpec as P

P_SIZE = 256
NT = 256
NF = 24
NK = 8
JD = 4


span_metric = 1.0


def extended(block, sides, width):
    for axis, dim in sides:
        count = lax.axis_size(axis)
        forward = [(i, i + 1) for i in range(count - 1)]
        forward.append((count - 1, 0))
        backward = [(target, source) for source, target in forward]
        low = lax.ppermute(
            lax.slice_in_dim(block, block.shape[dim] - width, None, axis=dim), axis, forward
        )
        high = lax.ppermute(lax.slice_in_dim(block, 0, width, axis=dim), axis, backward)
        block = jnp.concatenate([low, block, high], axis=dim)
    return block


def fourier_table(freq_ids, times, total):
    turns = times[:, None] * freq_ids[None, :] % total
    theta = 2.0 * math.pi / total * turns.astype(jnp.float32)
    window = 0.5 - 0.5 * jnp.cos(2.0 * math.pi / total * times.astype(jnp.float32))
    scale = 1.0 / math.sqrt(0.375 * total)
    cosine = scale * window[:, None] * jnp.cos(theta)
    sine = -scale * window[:, None] * jnp.sin(theta)
    table = jnp.stack([cosine, sine], axis=-1)
    return table.reshape(times.shape[0], -1).astype(jnp.bfloat16)


def line_derivative(field):
    inner = (
        field[..., :-4] - 8.0 * field[..., 1:-3] + 8.0 * field[..., 3:-1] - field[..., 4:]
    ) / 12.0
    first = (
        -25.0 * field[..., 0]
        + 48.0 * field[..., 1]
        - 36.0 * field[..., 2]
        + 16.0 * field[..., 3]
        - 3.0 * field[..., 4]
    ) / 12.0
    second = (
        -3.0 * field[..., 0]
        - 10.0 * field[..., 1]
        + 18.0 * field[..., 2]
        - 6.0 * field[..., 3]
        + field[..., 4]
    ) / 12.0
    penult = (
        3.0 * field[..., -1]
        + 10.0 * field[..., -2]
        - 18.0 * field[..., -3]
        + 6.0 * field[..., -4]
        - field[..., -5]
    ) / 12.0
    final = (
        25.0 * field[..., -1]
        - 48.0 * field[..., -2]
        + 36.0 * field[..., -3]
        - 16.0 * field[..., -4]
        + 3.0 * field[..., -5]
    ) / 12.0
    return jnp.concatenate(
        [first[..., None], second[..., None], inner, penult[..., None], final[..., None]], axis=-1
    )


def vorticity(padded, metric):
    center = padded[2:-2]
    along_line = line_derivative(center)
    along_pitch = (padded[:-4] - 8.0 * padded[1:-3] + 8.0 * padded[3:-1] - padded[4:]) / 12.0
    along_span = (
        jnp.roll(center, 2, axis=1)
        - 8.0 * jnp.roll(center, 1, axis=1)
        + 8.0 * jnp.roll(center, -1, axis=1)
        - jnp.roll(center, -2, axis=1)
    ) * (span_metric / 12.0)
    shape = (metric.shape[1], 1, 1, 1, metric.shape[2])
    xi_x = metric[0].reshape(shape)
    xi_y = metric[1].reshape(shape)
    eta_x = metric[2].reshape(shape)
    eta_y = metric[3].reshape(shape)
    d_x = xi_x * along_line + eta_x * along_pitch
    d_y = xi_y * along_line + eta_y * along_pitch
    omega_x = d_y[:, :, :, 2] - along_span[:, :, :, 1]
    omega_y = along_span[:, :, :, 0] - d_x[:, :, :, 2]
    omega_z = d_x[:, :, :, 1] - d_y[:, :, :, 0]
    return jnp.stack([omega_x, omega_y, omega_z], axis=0)


def per_device(snapshots, slot_line, freq_ids, metrics, weights, stored_spectra):
    holders = lax.axis_size("space")
    capacity = snapshots.shape[2]
    local_times = snapshots.shape[3]
    slot_count = holders * capacity
    arrived = lax.all_to_all(snapshots, "space", split_axis=1, concat_axis=0, tiled=True)
    arrived = arrived.reshape(slot_count, local_times, 3, P_SIZE)
    owner = lax.axis_index("space")
    slot_ids = lax.dynamic_index_in_dim(slot_line, owner, 1, keepdims=False).reshape(slot_count)
    line_index = jnp.arange(JD * NK, dtype=jnp.int32)
    slot_index = jnp.arange(slot_count, dtype=jnp.int32)
    position = jnp.sum(
        jnp.where(slot_ids[None, :] == line_index[:, None], slot_index[None, :], 0), axis=1
    )
    owned = jnp.take(arrived, position, axis=0).reshape(JD, NK, local_times, 3, P_SIZE)
    groups = lax.axis_size("block")
    freq_local = NF // groups
    times = lax.axis_index("block") * local_times + jnp.arange(local_times, dtype=jnp.int32)
    table = fourier_table(freq_ids, times, NT)
    summed = lax.psum_scatter(
        jnp.einsum("tq,jktcp->qjkcp", table, owned, preferred_element_type=jnp.float32),
        "block",
        scatter_dimension=0,
        tiled=True,
    )
    velocity_rows = summed.astype(jnp.bfloat16)
    padded = extended(velocity_rows, (("space", 1),), 2)
    padded = jnp.transpose(padded, (1, 2, 0, 3, 4)).astype(jnp.float32)
    vort = vorticity(padded, metrics).astype(jnp.bfloat16)
    spectra = jnp.transpose(vort, (3, 0, 1, 2, 4)).reshape(freq_local, 2, 3, JD, NK, P_SIZE)
    columns = jnp.concatenate([spectra[:, None], stored_spectra], axis=1).astype(jnp.float32)
    weighted = columns * weights[:, None, :]
    ncolumns = columns.shape[1]
    flat_cols = columns.reshape(freq_local, 2 * ncolumns, -1)
    flat_weighted = weighted.reshape(freq_local, 2 * ncolumns, -1)
    full = jnp.einsum(
        "fam,fbm->fab", flat_cols, flat_weighted, precision=lax.Precision.HIGHEST
    ).reshape(freq_local, ncolumns, 2, ncolumns, 2)
    real_part = full[:, :, 0, :, 0] + full[:, :, 1, :, 1]
    imag_part = full[:, :, 0, :, 1] - full[:, :, 1, :, 0]
    npoints = 3.0 * JD * holders * NK * P_SIZE
    local_gram = jnp.stack([real_part, imag_part], axis=1) / npoints
    gram = lax.psum(local_gram, "space")
    return (spectra, gram)


def solution(mesh):
    return jax.shard_map(
        per_device,
        mesh=mesh,
        in_specs=(
            P("space", None, None, "block", None, None),
            P(),
            P(),
            P(None, "space", None),
            P("space", None),
            P("block", None, None, None, "space", None, None),
        ),
        out_specs=(P("block", None, None, "space", None, None), P("block", None, None, None)),
        check_vma=False,
    )
```

profile of v0, /device:TPU:6, one launch (start us, length us, event | category | flops | bytes accessed | tf_op | source)
XLA Modules:
  0.0 249.0 jit_solution(6603422752489882813)
XLA Ops:
  7.2 11.6 %all-to-all-start = ((bf16[1,32,2,32,3,256]{5,3,4,2,0,1:T(8,128)(2,1)}), bf16[1,32,2,32,3,256]{5,3,4,2,0,1:T(8,128)(2,1)S(1)}, u32[]{:S(2)}, u32[]{:S(2)}) async-start(bf16[1,32,2,32,3,256]{5,3,4,2,0,1:T(8,128)(2,1)} %bitcast.50), calls=%async_computation | async-start | bytes 6291456 | tf_op jit(solution)/shard_map/all_to_all | solution.py:108
  18.9 0.7 dynamic-slice_reduce_fusion
  19.8 0.1 multiply_convert_fusion.1
  20.1 73.4 %all-to-all-done = bf16[1,32,2,32,3,256]{5,3,4,2,0,1:T(8,128)(2,1)S(1)} async-done(((bf16[1,32,2,32,3,256]{5,3,4,2,0,1:T(8,128)(2,1)}), bf16[1,32,2,32,3,256]{5,3,4,2,0,1:T(8,128)(2,1)S(1)}, u32[]{:S(2)}, u32[]{:S(2)}) %all-to-all-start) | async-done | bytes 3145760 | tf_op jit(solution)/shard_map/all_to_all | solution.py:108
  93.5 1.8 gather_fusion
  95.3 1.6 broadcast_select_fusion
  96.9 0.8 fusion.27
  97.7 4.9 %copy.97 = f32[48,4,8,3,256]{4,2,3,1,0:T(8,128)} copy(f32[48,4,8,3,256]{4,0,3,2,1:T(8,128)S(1)} %fusion.27) | data formatting | bytes 9437184 | tf_op jit(solution)/shard_map/tq,jktcp->qjkcp/dot_general | solution.py:123
  102.6 0.7 copy-done.9
  103.2 0.7 copy.107
  104.0 33.9 %reduce-scatter.2.cloned.1.call-done = f32[6,4,8,3,256]{4,2,3,1,0:T(8,128)} async-done(((f32[48,4,8,3,256]{4,2,3,1,0:T(8,128)}), f32[6,4,8,3,256]{4,2,3,1,0:T(8,128)}) %reduce-scatter.2.cloned.1.call-update) | async-done | bytes 589840 | tf_op jit(solution)/shard_map/reduce_scatter | solution.py:122
  137.8 1.1 fusion.26
  138.9 1.5 collective-permute-start
  140.4 4.4 %collective-permute-start.1 = (bf16[6,2,8,3,256]{4,2,1,0,3:T(8,128)(2,1)S(1)}, bf16[6,2,8,3,256]{4,2,1,0,3:T(8,128)(2,1)S(1)}, u32[]{:S(2)}, u32[]{:S(2)}) collective-permute-start(bf16[6,2,8,3,256]{4,2,1,0,3:T(8,128)(2,1)S(1)} %get-tuple-element.21), channel_id=1, source_target_pairs={{1,0},{2,1},{3,2},{4,3},{5,4},{6,5},{7,6},{8,7},{9,8},{10,9},{11,1... | collective-permute-start | bytes 442376 | tf_op jit(solution)/shard_map/ppermute | solution.py:27
  144.7 2.9 %collective-permute-done = bf16[6,2,8,3,256]{4,2,1,0,3:T(8,128)(2,1)S(1)} collective-permute-done((bf16[6,2,8,3,256]{4,2,1,0,3:T(8,128)(2,1)S(1)}, bf16[6,2,8,3,256]{4,2,1,0,3:T(8,128)(2,1)S(1)}, u32[]{:S(2)}, u32[]{:S(2)}) %collective-permute-start) | collective-permute-done | bytes 147488 | tf_op jit(solution)/shard_map/ppermute | solution.py:24
  147.6 0.1 collective-permute-done.1
  147.7 1.2 convert_bitcast_fusion
  148.9 1.7 add_multiply_fusion
  150.6 1.4 fusion.6
  152.0 0.4 add_multiply_fusion.1
  152.5 1.2 fusion.22
  153.7 0.8 fusion.23
  154.4 0.7 fusion.25
  155.1 1.8 concatenate.26
  156.9 0.2 multiply_add_fusion
  157.3 0.9 copy-done.1
  158.2 0.2 copy-done.2
  158.4 0.5 fusion.11
  159.1 0.9 copy-done.4
  160.1 0.9 reshape.365
  161.0 2.6 %fusion = f32[3,6,6]{2,1,0:T(8,128)S(1)} fusion(bf16[3,6,24576]{2,1,0:T(8,128)(2,1)S(1)} %reshape.365, f32[24576]{0:T(1024)S(1)} %bitcast.54), kind=kOutput, calls=%fused_computation.1 | convolution fusion | flops 32735232 | bytes 983472 | tf_op jit(solution)/shard_map/fam,fbm->fab/dot_general | solution.py:138
  164.1 78.0 %psum.7 = f32[3,2,3,3]{3,1,2,0:T(2,128)} all-reduce(f32[3,2,3,3]{3,1,2,0:T(2,128)S(1)} %maximum_multiply_fusion.2), channel_id=1, replica_groups=mesh['block'=8,'space'=32] {'space'}, use_global_device_ids=true, to_apply=%region_2.3 | all-reduce | flops 54 | bytes 432 | tf_op jit(solution)/shard_map/psum | solution.py:145
  (42 shorter events, 1.3 us)
Async XLA Ops:
  7.2 11.7 %copy-start = (s32[32,32,2]{1,2,0:T(2,128)S(1)}, s32[32,32,2]{1,2,0:T(2,128)}, u32[]{:S(2)}) copy-start(s32[32,32,2]{1,2,0:T(2,128)} %param.7) | copy-start | bytes 24580
  7.2 12.6 %copy-start.10 = (s32[24]{0:T(128)S(1)}, s32[24]{0:T(128)}, u32[]{:S(2)}) copy-start(s32[24]{0:T(128)} %param.8) | copy-start | bytes 292
  7.2 86.3 %all-to-all-start = ((bf16[1,32,2,32,3,256]{5,3,4,2,0,1:T(8,128)(2,1)}), bf16[1,32,2,32,3,256]{5,3,4,2,0,1:T(8,128)(2,1)S(1)}, u32[]{:S(2)}, u32[]{:S(2)}) async-start(bf16[1,32,2,32,3,256]{5,3,4,2,0,1:T(8,128)(2,1)} %bitcast.50), calls=%async_computation | async-start | bytes 6291456 | tf_op jit(solution)/shard_map/all_to_all | solution.py:108
  18.8 119.0 %reduce-scatter.2.cloned.1.call-start = ((), (), s32[]{:S(2)}) async-start(), calls=%async_computation.2 | async-start | bytes 5308416 | tf_op jit(solution)/shard_map/reduce_scatter | solution.py:122
  102.5 0.7 copy-start.9
  102.5 42.2 %copy-start.8 = (f32[4,4,256]{2,1,0:T(4,128)S(1)}, f32[4,4,256]{2,1,0:T(4,128)}, u32[]{:S(2)}) copy-start(f32[4,4,256]{2,1,0:T(4,128)} %param.9) | copy-start | bytes 49156
  138.9 8.7 %collective-permute-start = (bf16[6,2,8,3,256]{4,2,1,0,3:T(8,128)(2,1)S(1)}, bf16[6,2,8,3,256]{4,2,1,0,3:T(8,128)(2,1)S(1)}, u32[]{:S(2)}, u32[]{:S(2)}) collective-permute-start(bf16[6,2,8,3,256]{4,2,1,0,3:T(8,128)(2,1)S(1)} %get-tuple-element.20), channel_id=1, source_target_pairs={{0,1},{1,2},{2,3},{3,4},{4,5},{5,6},{6,7},{7,8},{8,9},{9,10},{10,1... | collective-permute-start | bytes 442376 | tf_op jit(solution)/shard_map/ppermute | solution.py:24
  140.4 7.3 %collective-permute-start.1 = (bf16[6,2,8,3,256]{4,2,1,0,3:T(8,128)(2,1)S(1)}, bf16[6,2,8,3,256]{4,2,1,0,3:T(8,128)(2,1)S(1)}, u32[]{:S(2)}, u32[]{:S(2)}) collective-permute-start(bf16[6,2,8,3,256]{4,2,1,0,3:T(8,128)(2,1)S(1)} %get-tuple-element.21), channel_id=1, source_target_pairs={{1,0},{2,1},{3,2},{4,3},{5,4},{6,5},{7,6},{8,7},{9,8},{10,9},{11,1... | collective-permute-start | bytes 442376 | tf_op jit(solution)/shard_map/ppermute | solution.py:27
  157.1 1.1 copy-start.1
  157.1 1.2 copy-start.2
  157.1 1.2 copy-start.5
  157.2 1.3 copy-start.6
  158.9 1.1 copy-start.4
  159.1 1.9 copy-start.3
  160.0 1.0 copy-start.7
Sparse Core Ops, SparseCore 0:
  102.7 35.0 reduce-scatter.1
where the time goes:
time: 251 us; the launch traced here: 249 us
  waiting for transfers between devices  110 us (44%)
  blocking collectives  78 us (31%)
  local copies, waits for them, and re-layouts  17.8 us (7%)
  starting transfers between devices  17.5 us (7%)
  between operations  14.3 us (6%)
  other arithmetic  7.62 us (3%)
  matrix products  3.39 us (1%)
    psum x1, blocking collectives, per_device(): gram = lax.psum(local_gram, 'space')  78 us
    all_to_all x1, waiting for transfers between devices, per_device(): lax.all_to_all(snapshots, 'space', split_axis=1, concat_axis=0, tiled=True)  73.4 us
    reduce_scatter x1, waiting for transfers between devices, per_device(): lax.psum_scatter(jnp.einsum('tq,jktcp->qjkcp', table, owned, preferred_el...  33.9 us
    all_to_all x1, starting transfers between devices, per_device(): lax.all_to_all(snapshots, 'space', split_axis=1, concat_axis=0, tiled=True)  11.6 us
  transfers between devices with their start and end apart: 4, of which 4 were waited for; matrix products, arithmetic and copies ran while one was open for 1% of the time, Pallas kernels for 0%

commit v1 on v0

v1 whole, which is shorter than its diff:
```python
import functools
import math

import jax
import jax.numpy as jnp
import numpy as np
from jax import lax
from jax.experimental import pallas as pl
from jax.experimental.pallas import tpu as pltpu
from jax.sharding import PartitionSpec as P

P_SIZE = 256
NT = 256
NF = 24
NK = 8
JD = 4
LD = JD * NK
ROWS = 40
VMEM = pl.BlockSpec(memory_space=pltpu.VMEM)
PARAMS = pltpu.CompilerParams(vmem_limit_bytes=32 * 1024 * 1024)


def fourier_table(freq_ids, times, total):
    turns = times[:, None] * freq_ids[None, :] % total
    theta = 2.0 * math.pi / total * turns.astype(jnp.float32)
    window = 0.5 - 0.5 * jnp.cos(2.0 * math.pi / total * times.astype(jnp.float32))
    scale = 1.0 / math.sqrt(0.375 * total)
    cosine = scale * window[:, None] * jnp.cos(theta)
    sine = -scale * window[:, None] * jnp.sin(theta)
    table = jnp.stack([cosine, sine], axis=-1)
    return table.reshape(times.shape[0], -1).astype(jnp.bfloat16)


def line_matrix():
    d = np.zeros((P_SIZE, P_SIZE), np.float32)
    for p in range(2, P_SIZE - 2):
        d[p - 2, p], d[p - 1, p], d[p + 1, p], d[p + 2, p] = 1, -8, 8, -1
    first, second = (-25, 48, -36, 16, -3), (-3, -10, 18, -6, 1)
    for i in range(5):
        d[i, 0], d[i, 1] = first[i], second[i]
        d[P_SIZE - 1 - i, P_SIZE - 1], d[P_SIZE - 1 - i, P_SIZE - 2] = -first[i], -second[i]
    return jnp.asarray(d, jnp.bfloat16)


def dft_kernel(raw_ref, table_ref, out_ref):
    blocks, owners = raw_ref.shape[:2]
    for d in range(owners):
        total = None
        for s in range(2):
            for c in range(3):
                lines = raw_ref[:, d, s, c].reshape(NT, P_SIZE)
                term = jnp.dot(
                    table_ref[3 * s + c], lines, preferred_element_type=jnp.float32
                )
                total = term if total is None else total + term
        out_ref[:, d] = total.astype(jnp.bfloat16).reshape(blocks, ROWS, P_SIZE)


def place_kernel(place_ref, held_ref, own_ref, low_ref, high_ref):
    held = held_ref[...].reshape(-1, P_SIZE)
    rows = jnp.dot(place_ref[...], held, preferred_element_type=jnp.float32)
    rows = rows.astype(jnp.bfloat16).reshape(own_ref.shape)
    own_ref[...] = rows
    low_ref[...] = rows[:, :, JD - 2 :]
    high_ref[...] = rows[:, :, :2]


def vorticity_kernel(
    own_ref, low_ref, high_ref, line_ref, metric_ref, weight_ref, stored_ref, spectra_ref, gram_ref
):
    gram_ref[...] = jnp.zeros_like(gram_ref)
    nf = stored_ref.shape[0]
    xi_x, xi_y, eta_x, eta_y = (metric_ref[i].reshape(JD, 1, P_SIZE) for i in range(4))
    weight = weight_ref[...].reshape(1, JD, 1, P_SIZE)
    twelfth = 1.0 / 12.0

    for f in range(nf):
        new = []
        for r in range(2):
            q = 2 * f + r
            d_x, d_y, d_z = [], [], []
            for c in range(3):
                line = own_ref[q, c].reshape(LD, P_SIZE)
                along = jnp.dot(line, line_ref[...], preferred_element_type=jnp.float32)
                along = (along * twelfth).reshape(JD, NK, P_SIZE)
                center = own_ref[q, c].astype(jnp.float32)
                padded = jnp.concatenate(
                    [
                        low_ref[q, c].astype(jnp.float32),
                        center,
                        high_ref[q, c].astype(jnp.float32),
                    ],
                    axis=0,
                )
                pitch = (
                    padded[:-4] - 8.0 * padded[1:-3] + 8.0 * padded[3:-1] - padded[4:]
                ) * twelfth
                span = (
                    pltpu.roll(center, 2, 1)
                    - 8.0 * pltpu.roll(center, 1, 1)
                    + 8.0 * pltpu.roll(center, NK - 1, 1)
                    - pltpu.roll(center, NK - 2, 1)
                ) * twelfth
                d_x.append(xi_x * along + eta_x * pitch)
                d_y.append(xi_y * along + eta_y * pitch)
                d_z.append(span)
            vort = [d_y[2] - d_z[1], d_z[0] - d_x[2], d_x[1] - d_y[0]]
            vort = [v.astype(jnp.bfloat16) for v in vort]
            for c in range(3):
                spectra_ref[f, r, c] = vort[c]
            new.append(jnp.stack([v.astype(jnp.float32) for v in vort], axis=0))
        columns = [tuple(new)] + [
            tuple(stored_ref[f, a, r].astype(jnp.float32) for r in range(2)) for a in range(2)
        ]

        def put(part, a, b, value):
            total = jnp.sum(value, axis=(0, 1, 2)).reshape(1, P_SIZE)
            total = total[:, :128] + total[:, 128:]
            row = ((f * 2 + part) * 3 + a) * 3 + b
            gram_ref[row : row + 1, :] = total
            if a != b:
                row = ((f * 2 + part) * 3 + b) * 3 + a
                gram_ref[row : row + 1, :] = total if part == 0 else -total

        for a in range(3):
            real, imag = (weight * v for v in columns[a])
            for b in range(a, 3):
                put(0, a, b, real * columns[b][0] + imag * columns[b][1])
                if a != b:
                    put(1, a, b, real * columns[b][1] - imag * columns[b][0])


def ring_sum(value, axis, shifts):
    count = lax.axis_size(axis)
    arrived = [lax.ppermute(value, axis, pairs(count)) for pairs in shifts]
    return functools.reduce(lambda a, b: a + b, arrived, value)


def shift_y(k):
    return lambda n: [(i, (i + 8 * k) % n) for i in range(n)]


def shift_z(k):
    return lambda n: [(i, i // 8 * 8 + (i + k) % 8) for i in range(n)]


def per_device(snapshots, slot_line, freq_ids, metrics, weights, stored_spectra):
    groups = lax.axis_size("block")
    holders = lax.axis_size("space")
    owners = holders // groups
    raw = jnp.transpose(snapshots[0], (0, 1, 3, 2, 4))
    raw = raw.reshape((groups, owners) + raw.shape[1:])
    raw = lax.all_to_all(raw, "block", split_axis=0, concat_axis=0, tiled=True)

    table = fourier_table(freq_ids, jnp.arange(NT, dtype=jnp.int32), NT).T
    table = table.reshape(groups, 1, NF // groups * 2, NT)
    table = jnp.broadcast_to(table, (groups, 6, NF // groups * 2, NT)).reshape(groups, 36, NT)
    table = jnp.pad(table, ((0, 0), (0, ROWS - 36), (0, 0)))
    part = jnp.arange(6, dtype=jnp.int32)[:, None, None, None]
    row = jnp.arange(ROWS, dtype=jnp.int32)[None, None, :, None]
    table = jnp.where(row // 6 == part, table[None], 0).reshape(6, groups * ROWS, NT)

    velocity = pl.pallas_call(
        dft_kernel,
        out_shape=jax.ShapeDtypeStruct((groups, owners, ROWS, P_SIZE), jnp.bfloat16),
        in_specs=[VMEM, VMEM],
        out_specs=VMEM,
        compiler_params=PARAMS,
        name="dft",
    )(raw, table)
    velocity = lax.all_to_all(velocity, "block", split_axis=0, concat_axis=0, tiled=True)
    velocity = velocity.reshape(holders, ROWS, P_SIZE)
    velocity = lax.all_to_all(velocity, "space", split_axis=0, concat_axis=0, tiled=True)

    me = lax.axis_index("space")
    ids = lax.dynamic_index_in_dim(slot_line, me, 1, keepdims=False)
    in_row = jnp.arange(ROWS, dtype=jnp.int32)
    held = jnp.where(in_row[None, :] < 18, ids[:, 0:1], ids[:, 1:2])
    inner = in_row % 18
    source = (inner % 6 * 3 + inner // 6)[None, :] * LD + held
    source = jnp.where((held >= 0) & (in_row[None, :] < 36), source, -1).reshape(1, -1)
    target = jnp.arange(18 * LD, dtype=jnp.int32)[:, None]
    place = (source == target).astype(jnp.bfloat16)

    nq = NF // groups * 2
    own, low, high = pl.pallas_call(
        place_kernel,
        out_shape=[
            jax.ShapeDtypeStruct((nq, 3, JD, NK, P_SIZE), jnp.bfloat16),
            jax.ShapeDtypeStruct((nq, 3, 2, NK, P_SIZE), jnp.bfloat16),
            jax.ShapeDtypeStruct((nq, 3, 2, NK, P_SIZE), jnp.bfloat16),
        ],
        in_specs=[VMEM, VMEM],
        out_specs=[VMEM, VMEM, VMEM],
        compiler_params=PARAMS,
        name="place",
    )(place, velocity)
    forward = [(i, (i + 1) % holders) for i in range(holders)]
    backward = [(target, source) for source, target in forward]
    low = lax.ppermute(low, "space", forward)
    high = lax.ppermute(high, "space", backward)

    spectra, gram = pl.pallas_call(
        vorticity_kernel,
        out_shape=[
            jax.ShapeDtypeStruct((NF // groups, 2, 3, JD, NK, P_SIZE), jnp.bfloat16),
            jax.ShapeDtypeStruct((56, 128), jnp.float32),
        ],
        in_specs=[VMEM] * 7,
        out_specs=[VMEM, VMEM],
        compiler_params=PARAMS,
        name="vorticity",
    )(own, low, high, line_matrix(), metrics, weights, stored_spectra)
    gram = jnp.sum(gram, axis=1) * (1.0 / (3.0 * JD * holders * NK * P_SIZE))
    gram = ring_sum(gram, "space", [shift_y(k) for k in range(1, 4)])
    gram = ring_sum(gram, "space", [shift_z(k) for k in range(1, 8)])
    gram = gram[: NF // groups * 18].reshape(NF // groups, 2, 3, 3)
    return (spectra, gram)


def solution(mesh):
    return jax.shard_map(
        per_device,
        mesh=mesh,
        in_specs=(
            P("space", None, None, "block", None, None),
            P(),
            P(),
            P(None, "space", None),
            P("space", None),
            P("block", None, None, None, "space", None, None),
        ),
        out_specs=(P("block", None, None, "space", None, None), P("block", None, None, None)),
        check_vma=False,
    )
```

time: 251 us -> 130 us (0.52)
  blocking collectives: 78 us -> 0 us
  waiting for transfers between devices: 110 us -> 74.6 us
  starting transfers between devices: 17.5 us -> 44.4 us
  local copies, waits for them, and re-layouts: 17.8 us -> 3.29 us
  between operations: 14.3 us -> 0.88 us
  other arithmetic: 7.62 us -> 2.2 us
  Pallas kernels: 0 us -> 3.55 us
  matrix products: 3.39 us -> 0 us
    psum x1 -> x0, blocking collectives: 78 us -> none  [per_device(): gram = lax.psum(local_gram, 'space')]
    reduce_scatter x1 -> x0, waiting for transfers between devices: 33.9 us -> none  [per_device(): lax.psum_scatter(jnp.einsum('tq,jktcp->qjkcp', table, owned, preferred_el...]
    ppermute x2 -> x12, starting transfers between devices: 5.83 us -> 21.6 us  [the longest x10 16.2 us: ring_sum(): arrived = [lax.ppermute(value, axis, pairs(count)) for pairs in shifts]]
    all_to_all x1 -> x3, starting transfers between devices: 11.6 us -> 22.8 us  [the longest x1 10.5 us: per_device(): lax.all_to_all(velocity, 'space', split_axis=0, concat_axis=0, tiled=True)]
    all_to_all x1 -> x3, waiting for transfers between devices: 73.4 us -> 63.8 us  [the longest x1 34.5 us: per_device(): raw = lax.all_to_all(raw, 'block', split_axis=0, concat_axis=0, tiled=True)]
    ppermute x2 -> x12, waiting for transfers between devices: 2.99 us -> 10.8 us  [the longest x10 7.68 us: ring_sum(): arrived = [lax.ppermute(value, axis, pairs(count)) for pairs in shifts]]
    dot_general x2 -> x0, local copies, waits for them, and re-layouts: 4.98 us -> none  [the longest x1 4.86 us: per_device(): jnp.einsum('tq,jktcp->qjkcp', table, owned, preferred_element_type=jnp.fl...]
    slice x5 -> x0, local copies, waits for them, and re-layouts: 3.87 us -> none  [the longest x2 1.94 us: vorticity(): jnp.roll(center, -2, axis=1)]
  transfers between devices with their start and end apart: 4 -> 15, of which waited for: 4 -> 8; matrix products, arithmetic and copies ran while one was open for 1% -> 2% of each run, Pallas kernels for 0% -> 0%
where the time goes in v1:
time: 130 us; the launch traced here: 129 us
  waiting for transfers between devices  74.6 us (57%)
  starting transfers between devices  44.4 us (34%)
  Pallas kernels  3.55 us (3%)
  local copies, waits for them, and re-layouts  3.29 us (3%)
  other arithmetic  2.2 us (2%)
    all_to_all x1, waiting for transfers between devices, per_device(): raw = lax.all_to_all(raw, 'block', split_axis=0, concat_axis=0, tiled=True)  34.5 us
    all_to_all x1, waiting for transfers between devices, per_device(): lax.all_to_all(velocity, 'space', split_axis=0, concat_axis=0, tiled=True)  19.5 us
    ppermute x10, starting transfers between devices, ring_sum(): arrived = [lax.ppermute(value, axis, pairs(count)) for pairs in shifts]  16.2 us
    all_to_all x1, starting transfers between devices, per_device(): lax.all_to_all(velocity, 'space', split_axis=0, concat_axis=0, tiled=True)  10.5 us
    all_to_all x1, waiting for transfers between devices, per_device(): lax.all_to_all(velocity, 'block', split_axis=0, concat_axis=0, tiled=True)  9.77 us
    ppermute x10, waiting for transfers between devices, ring_sum(): arrived = [lax.ppermute(value, axis, pairs(count)) for pairs in shifts]  7.68 us
    all_to_all x1, starting transfers between devices, per_device(): lax.all_to_all(velocity, 'block', split_axis=0, concat_axis=0, tiled=True)  6.33 us
    all_to_all x1, starting transfers between devices, per_device(): raw = lax.all_to_all(raw, 'block', split_axis=0, concat_axis=0, tiled=True)  5.94 us
  transfers between devices with their start and end apart: 15, of which 8 were waited for; matrix products, arithmetic and copies ran while one was open for 2% of the time, Pallas kernels for 0%

profile of v1, /device:TPU:6, one launch (start us, length us, event | category | flops | bytes accessed | tf_op | source)
XLA Modules:
  0.0 128.9 jit_solution(6702646242857976295)
XLA Ops:
  0.7 5.9 %all-to-all-start = ((bf16[8,4,2,3,32,256]{5,4,3,2,1,0:T(8,128)(2,1)}), bf16[8,4,2,3,32,256]{5,4,3,2,1,0:T(8,128)(2,1)S(1)}, u32[]{:S(2)}, u32[]{:S(2)}) async-start(bf16[8,4,2,3,32,256]{5,4,3,2,1,0:T(8,128)(2,1)} %bitcast.17), calls=%async_computation | async-start | bytes 6291456 | tf_op jit(solution)/shard_map/all_to_all | solution.py:153
  6.8 0.2 multiply_convert_fusion.1
  7.2 1.3 %broadcast_select_fusion.table_ref = bf16[6,320,256]{2,1,0:T(8,128)(2,1)} fusion(pred[6,320]{1,0:T(8,128)(4,1)S(1)} %broadcast_in_dim.83, bf16[320,256]{1,0:T(8,128)(2,1)S(1)} %bitcast.18), kind=kLoop, calls=%fused_computation.2 | loop fusion | flops 491520 | bytes 1148800 | tf_op jit(solution)/shard_map/jit(_where)/select_n | solution.py:161
  8.4 34.5 %all-to-all-done.raw_ref = bf16[8,4,2,3,32,256]{5,4,3,2,1,0:T(8,128)(2,1)S(1)} async-done(((bf16[8,4,2,3,32,256]{5,4,3,2,1,0:T(8,128)(2,1)}), bf16[8,4,2,3,32,256]{5,4,3,2,1,0:T(8,128)(2,1)S(1)}, u32[]{:S(2)}, u32[]{:S(2)}) %all-to-all-start) | async-done | bytes 3145760 | tf_op jit(solution)/shard_map/all_to_all | solution.py:153
  42.9 1.2 copy-done.1
  44.1 1.2 dft.1
  45.3 0.9 copy-done.2
  46.2 6.3 %all-to-all-start.1 = ((bf16[8,4,40,256]{3,2,1,0:T(8,128)(2,1)}), bf16[8,4,40,256]{3,2,1,0:T(8,128)(2,1)}, u32[]{:S(2)}, u32[]{:S(2)}) async-start(bf16[8,4,40,256]{3,2,1,0:T(8,128)(2,1)} %copy-done.2), calls=%async_computation.1 | async-start | bytes 1310720 | tf_op jit(solution)/shard_map/all_to_all | solution.py:171
  52.6 9.8 %all-to-all-done.1 = bf16[8,4,40,256]{3,2,1,0:T(8,128)(2,1)} async-done(((bf16[8,4,40,256]{3,2,1,0:T(8,128)(2,1)}), bf16[8,4,40,256]{3,2,1,0:T(8,128)(2,1)}, u32[]{:S(2)}, u32[]{:S(2)}) %all-to-all-start.1) | async-done | bytes 655392 | tf_op jit(solution)/shard_map/all_to_all | solution.py:171
  62.3 10.5 %all-to-all-start.2 = ((bf16[32,40,256]{2,1,0:T(8,128)(2,1)}), bf16[32,40,256]{2,1,0:T(8,128)(2,1)S(1)}, u32[]{:S(2)}, u32[]{:S(2)}) async-start(bf16[32,40,256]{2,1,0:T(8,128)(2,1)} %bitcast.9), calls=%async_computation.2 | async-start | bytes 1310720 | tf_op jit(solution)/shard_map/all_to_all | solution.py:173
  72.8 0.1 constant_dynamic-slice_fusion
  73.2 0.4 fusion.place_ref
  73.7 19.5 %all-to-all-done.2.held_ref = bf16[32,40,256]{2,1,0:T(8,128)(2,1)S(1)} async-done(((bf16[32,40,256]{2,1,0:T(8,128)(2,1)}), bf16[32,40,256]{2,1,0:T(8,128)(2,1)S(1)}, u32[]{:S(2)}, u32[]{:S(2)}) %all-to-all-start.2) | async-done | bytes 655392 | tf_op jit(solution)/shard_map/all_to_all | solution.py:173
  93.2 0.5 place.1
  93.7 1.5 %collective-permute-start = (bf16[6,3,2,8,256]{4,3,2,1,0:T(8,128)(2,1)S(1)}, bf16[6,3,2,8,256]{4,3,2,1,0:T(8,128)(2,1)S(1)}, u32[]{:S(2)}, u32[]{:S(2)}) collective-permute-start(bf16[6,3,2,8,256]{4,3,2,1,0:T(8,128)(2,1)S(1)} %get-tuple-element.8), channel_id=1, source_target_pairs={{0,1},{1,2},{2,3},{3,4},{4,5},{5,6},{6,7},{7,8},{8,9},{9,10},{10,1... | collective-permute-start | bytes 442376 | tf_op jit(solution)/shard_map/ppermute | solution.py:200
  95.3 3.9 %collective-permute-start.1 = (bf16[6,3,2,8,256]{4,3,2,1,0:T(8,128)(2,1)S(1)}, bf16[6,3,2,8,256]{4,3,2,1,0:T(8,128)(2,1)S(1)}, u32[]{:S(2)}, u32[]{:S(2)}) collective-permute-start(bf16[6,3,2,8,256]{4,3,2,1,0:T(8,128)(2,1)S(1)} %get-tuple-element.9), channel_id=1, source_target_pairs={{1,0},{2,1},{3,2},{4,3},{5,4},{6,5},{7,6},{8,7},{9,8},{10,9},{11,1... | collective-permute-start | bytes 442376 | tf_op jit(solution)/shard_map/ppermute | solution.py:201
  99.2 3.1 %collective-permute-done.low_ref = bf16[6,3,2,8,256]{4,3,2,1,0:T(8,128)(2,1)S(1)} collective-permute-done((bf16[6,3,2,8,256]{4,3,2,1,0:T(8,128)(2,1)S(1)}, bf16[6,3,2,8,256]{4,3,2,1,0:T(8,128)(2,1)S(1)}, u32[]{:S(2)}, u32[]{:S(2)}) %collective-permute-start) | collective-permute-done | bytes 147488 | tf_op jit(solution)/shard_map/ppermute | solution.py:200
  102.3 1.8 %vorticity.1 = (bf16[3,2,3,4,8,256]{5,4,3,2,1,0:T(8,128)(2,1)}, f32[56,128]{1,0:T(8,128)S(1)}) custom-call(bf16[6,3,4,8,256]{4,3,2,1,0:T(8,128)(2,1)S(1)} %get-tuple-element.7.own_ref, bf16[6,3,2,8,256]{4,3,2,1,0:T(8,128)(2,1)S(1)} %collective-permute-done.low_ref, bf16[6,3,2,8,256]{4,3,2,1,0:T(8,128)(2,1)S(1)} %collective-permute-done.1.high_ref, ...), custom_call_target="tpu_custom_call" | custom-call | tf_op jit(solution)/shard_map/vorticity/pallas_call | solution.py:203
  104.1 0.1 reduce_sum.9
  104.3 0.1 collective-permute-start.3
  104.4 1.4 %collective-permute-start.4 = (f32[56]{0:T(128)S(1)}, f32[56]{0:T(128)S(1)}, u32[]{:S(2)}, u32[]{:S(2)}) collective-permute-start(f32[56]{0:T(128)S(1)} %broadcast_multiply_fusion), channel_id=1, source_target_pairs={{0,24},{1,25},{2,26},{3,27},{4,28},{5,29},{6,30},{7,31},{8,0},{9,1... | collective-permute-start | bytes 680 | tf_op jit(solution)/shard_map/ppermute | solution.py:135
  105.8 0.7 collective-permute-start.2
  106.5 2.9 %collective-permute-done.3 = f32[56]{0:T(128)S(1)} collective-permute-done((f32[56]{0:T(128)S(1)}, f32[56]{0:T(128)S(1)}, u32[]{:S(2)}, u32[]{:S(2)}) %collective-permute-start.3) | collective-permute-done | bytes 256 | tf_op jit(solution)/shard_map/ppermute | solution.py:135
  109.4 1.1 collective-permute-done.2
  110.5 4.6 %collective-permute-start.11 = (f32[56]{0:T(128)S(1)}, f32[56]{0:T(128)S(1)}, u32[]{:S(2)}, u32[]{:S(2)}) collective-permute-start(f32[56]{0:T(128)S(1)} %add_add_fusion.1), channel_id=1, source_target_pairs={{0,7},{1,0},{2,1},{3,2},{4,3},{5,4},{6,5},{7,6},{8,15},{9,8},{10,9... | collective-permute-start | bytes 680 | tf_op jit(solution)/shard_map/ppermute | solution.py:135
  115.1 0.8 collective-permute-start.9
  115.9 5.2 %collective-permute-start.8 = (f32[56]{0:T(128)S(1)}, f32[56]{0:T(128)S(1)}, u32[]{:S(2)}, u32[]{:S(2)}) collective-permute-start(f32[56]{0:T(128)S(1)} %add_add_fusion.1), channel_id=1, source_target_pairs={{0,4},{1,5},{2,6},{3,7},{4,0},{5,1},{6,2},{7,3},{8,12},{9,13},{10,... | collective-permute-start | bytes 680 | tf_op jit(solution)/shard_map/ppermute | solution.py:135
  121.1 2.0 %collective-permute-start.6 = (f32[56]{0:T(128)S(1)}, f32[56]{0:T(128)S(1)}, u32[]{:S(2)}, u32[]{:S(2)}) collective-permute-start(f32[56]{0:T(128)S(1)} %add_add_fusion.1), channel_id=1, source_target_pairs={{0,2},{1,3},{2,4},{3,5},{4,6},{5,7},{6,0},{7,1},{8,10},{9,11},{10,... | collective-permute-start | bytes 680 | tf_op jit(solution)/shard_map/ppermute | solution.py:135
  123.2 1.4 %collective-permute-start.5 = (f32[56]{0:T(128)S(1)}, f32[56]{0:T(128)S(1)}, u32[]{:S(2)}, u32[]{:S(2)}) collective-permute-start(f32[56]{0:T(128)S(1)} %add_add_fusion.1), channel_id=1, source_target_pairs={{0,1},{1,2},{2,3},{3,4},{4,5},{5,6},{6,7},{7,0},{8,9},{9,10},{10,1... | collective-permute-start | bytes 680 | tf_op jit(solution)/shard_map/ppermute | solution.py:135
  124.5 3.1 %collective-permute-done.7 = f32[56]{0:T(128)S(1)} collective-permute-done((f32[56]{0:T(128)S(1)}, f32[56]{0:T(128)S(1)}, u32[]{:S(2)}, u32[]{:S(2)}) %collective-permute-start.7) | collective-permute-done | bytes 256 | tf_op jit(solution)/shard_map/ppermute | solution.py:135
  127.7 0.5 collective-permute-done.6
  128.3 0.6 copy.26
  (46 shorter events, 0.7 us)
Async XLA Ops:
  0.6 72.2 %copy-start = (s32[32,32,2]{1,2,0:T(2,128)S(1)}, s32[32,32,2]{1,2,0:T(2,128)}, u32[]{:S(2)}) copy-start(s32[32,32,2]{1,2,0:T(2,128)} %param.8) | copy-start | bytes 24580
  0.6 6.1 %copy-start.7 = (s32[24]{0:T(128)S(1)}, s32[24]{0:T(128)}, u32[]{:S(2)}) copy-start(s32[24]{0:T(128)} %param.9) | copy-start | bytes 292
  0.7 42.3 %all-to-all-start = ((bf16[8,4,2,3,32,256]{5,4,3,2,1,0:T(8,128)(2,1)}), bf16[8,4,2,3,32,256]{5,4,3,2,1,0:T(8,128)(2,1)S(1)}, u32[]{:S(2)}, u32[]{:S(2)}) async-start(bf16[8,4,2,3,32,256]{5,4,3,2,1,0:T(8,128)(2,1)} %bitcast.17), calls=%async_computation | async-start | bytes 6291456 | tf_op jit(solution)/shard_map/all_to_all | solution.py:153
  42.9 1.2 copy-start.1
  45.3 0.9 copy-start.2
  46.2 56.1 %copy-start.3 = (bf16[3,2,2,3,4,8,256]{6,5,4,3,2,1,0:T(8,128)(2,1)S(1)}, bf16[3,2,2,3,4,8,256]{6,5,4,3,2,1,0:T(8,128)(2,1)}, u32[]{:S(2)}) copy-start(bf16[3,2,2,3,4,8,256]{6,5,4,3,2,1,0:T(8,128)(2,1)} %stored_ref.1) | copy-start | bytes 1769476
  46.2 56.1 %copy-start.4 = (bf16[256,256]{1,0:T(8,128)(2,1)S(1)}, bf16[256,256]{1,0:T(8,128)(2,1)}, u32[]{:S(2)}) copy-start(bf16[256,256]{1,0:T(8,128)(2,1)} %constant.82.clone.line_ref) | copy-start | bytes 393220
  46.2 56.1 %copy-start.5 = (f32[4,4,256]{2,1,0:T(4,128)S(1)}, f32[4,4,256]{2,1,0:T(4,128)}, u32[]{:S(2)}) copy-start(f32[4,4,256]{2,1,0:T(4,128)} %metric_ref.1) | copy-start | bytes 49156
  46.2 56.1 %copy-start.6 = (f32[4,256]{1,0:T(4,128)S(1)}, f32[4,256]{1,0:T(4,128)}, u32[]{:S(2)}) copy-start(f32[4,256]{1,0:T(4,128)} %weight_ref.1) | copy-start | bytes 12292
  46.2 16.1 %all-to-all-start.1 = ((bf16[8,4,40,256]{3,2,1,0:T(8,128)(2,1)}), bf16[8,4,40,256]{3,2,1,0:T(8,128)(2,1)}, u32[]{:S(2)}, u32[]{:S(2)}) async-start(bf16[8,4,40,256]{3,2,1,0:T(8,128)(2,1)} %copy-done.2), calls=%async_computation.1 | async-start | bytes 1310720 | tf_op jit(solution)/shard_map/all_to_all | solution.py:171
  62.3 30.9 %all-to-all-start.2 = ((bf16[32,40,256]{2,1,0:T(8,128)(2,1)}), bf16[32,40,256]{2,1,0:T(8,128)(2,1)S(1)}, u32[]{:S(2)}, u32[]{:S(2)}) async-start(bf16[32,40,256]{2,1,0:T(8,128)(2,1)} %bitcast.9), calls=%async_computation.2 | async-start | bytes 1310720 | tf_op jit(solution)/shard_map/all_to_all | solution.py:173
  93.7 8.5 %collective-permute-start = (bf16[6,3,2,8,256]{4,3,2,1,0:T(8,128)(2,1)S(1)}, bf16[6,3,2,8,256]{4,3,2,1,0:T(8,128)(2,1)S(1)}, u32[]{:S(2)}, u32[]{:S(2)}) collective-permute-start(bf16[6,3,2,8,256]{4,3,2,1,0:T(8,128)(2,1)S(1)} %get-tuple-element.8), channel_id=1, source_target_pairs={{0,1},{1,2},{2,3},{3,4},{4,5},{5,6},{6,7},{7,8},{8,9},{9,10},{10,1... | collective-permute-start | bytes 442376 | tf_op jit(solution)/shard_map/ppermute | solution.py:200
  95.3 7.0 %collective-permute-start.1 = (bf16[6,3,2,8,256]{4,3,2,1,0:T(8,128)(2,1)S(1)}, bf16[6,3,2,8,256]{4,3,2,1,0:T(8,128)(2,1)S(1)}, u32[]{:S(2)}, u32[]{:S(2)}) collective-permute-start(bf16[6,3,2,8,256]{4,3,2,1,0:T(8,128)(2,1)S(1)} %get-tuple-element.9), channel_id=1, source_target_pairs={{1,0},{2,1},{3,2},{4,3},{5,4},{6,5},{7,6},{8,7},{9,8},{10,9},{11,1... | collective-permute-start | bytes 442376 | tf_op jit(solution)/shard_map/ppermute | solution.py:201
  104.3 5.1 %collective-permute-start.3 = (f32[56]{0:T(128)S(1)}, f32[56]{0:T(128)S(1)}, u32[]{:S(2)}, u32[]{:S(2)}) collective-permute-start(f32[56]{0:T(128)S(1)} %broadcast_multiply_fusion), channel_id=1, source_target_pairs={{0,16},{1,17},{2,18},{3,19},{4,20},{5,21},{6,22},{7,23},{8,24},{9,... | collective-permute-start | bytes 680 | tf_op jit(solution)/shard_map/ppermute | solution.py:135
  104.4 5.0 %collective-permute-start.4 = (f32[56]{0:T(128)S(1)}, f32[56]{0:T(128)S(1)}, u32[]{:S(2)}, u32[]{:S(2)}) collective-permute-start(f32[56]{0:T(128)S(1)} %broadcast_multiply_fusion), channel_id=1, source_target_pairs={{0,24},{1,25},{2,26},{3,27},{4,28},{5,29},{6,30},{7,31},{8,0},{9,1... | collective-permute-start | bytes 680 | tf_op jit(solution)/shard_map/ppermute | solution.py:135
  105.8 4.8 %collective-permute-start.2 = (f32[56]{0:T(128)S(1)}, f32[56]{0:T(128)S(1)}, u32[]{:S(2)}, u32[]{:S(2)}) collective-permute-start(f32[56]{0:T(128)S(1)} %broadcast_multiply_fusion), channel_id=1, source_target_pairs={{0,8},{1,9},{2,10},{3,11},{4,12},{5,13},{6,14},{7,15},{8,16},{9,17... | collective-permute-start | bytes 680 | tf_op jit(solution)/shard_map/ppermute | solution.py:135
  110.5 10.6 %collective-permute-start.11 = (f32[56]{0:T(128)S(1)}, f32[56]{0:T(128)S(1)}, u32[]{:S(2)}, u32[]{:S(2)}) collective-permute-start(f32[56]{0:T(128)S(1)} %add_add_fusion.1), channel_id=1, source_target_pairs={{0,7},{1,0},{2,1},{3,2},{4,3},{5,4},{6,5},{7,6},{8,15},{9,8},{10,9... | collective-permute-start | bytes 680 | tf_op jit(solution)/shard_map/ppermute | solution.py:135
  115.1 8.1 %collective-permute-start.10 = (f32[56]{0:T(128)S(1)}, f32[56]{0:T(128)S(1)}, u32[]{:S(2)}, u32[]{:S(2)}) collective-permute-start(f32[56]{0:T(128)S(1)} %add_add_fusion.1), channel_id=1, source_target_pairs={{0,6},{1,7},{2,0},{3,1},{4,2},{5,3},{6,4},{7,5},{8,14},{9,15},{10,... | collective-permute-start | bytes 680 | tf_op jit(solution)/shard_map/ppermute | solution.py:135
  115.1 9.4 %collective-permute-start.9 = (f32[56]{0:T(128)S(1)}, f32[56]{0:T(128)S(1)}, u32[]{:S(2)}, u32[]{:S(2)}) collective-permute-start(f32[56]{0:T(128)S(1)} %add_add_fusion.1), channel_id=1, source_target_pairs={{0,5},{1,6},{2,7},{3,0},{4,1},{5,2},{6,3},{7,4},{8,13},{9,14},{10,... | collective-permute-start | bytes 680 | tf_op jit(solution)/shard_map/ppermute | solution.py:135
  115.9 8.6 %collective-permute-start.8 = (f32[56]{0:T(128)S(1)}, f32[56]{0:T(128)S(1)}, u32[]{:S(2)}, u32[]{:S(2)}) collective-permute-start(f32[56]{0:T(128)S(1)} %add_add_fusion.1), channel_id=1, source_target_pairs={{0,4},{1,5},{2,6},{3,7},{4,0},{5,1},{6,2},{7,3},{8,12},{9,13},{10,... | collective-permute-start | bytes 680 | tf_op jit(solution)/shard_map/ppermute | solution.py:135
  121.1 6.5 %collective-permute-start.7 = (f32[56]{0:T(128)S(1)}, f32[56]{0:T(128)S(1)}, u32[]{:S(2)}, u32[]{:S(2)}) collective-permute-start(f32[56]{0:T(128)S(1)} %add_add_fusion.1), channel_id=1, source_target_pairs={{0,3},{1,4},{2,5},{3,6},{4,7},{5,0},{6,1},{7,2},{8,11},{9,12},{10,... | collective-permute-start | bytes 680 | tf_op jit(solution)/shard_map/ppermute | solution.py:135
  121.1 7.0 %collective-permute-start.6 = (f32[56]{0:T(128)S(1)}, f32[56]{0:T(128)S(1)}, u32[]{:S(2)}, u32[]{:S(2)}) collective-permute-start(f32[56]{0:T(128)S(1)} %add_add_fusion.1), channel_id=1, source_target_pairs={{0,2},{1,3},{2,4},{3,5},{4,6},{5,7},{6,0},{7,1},{8,10},{9,11},{10,... | collective-permute-start | bytes 680 | tf_op jit(solution)/shard_map/ppermute | solution.py:135
  123.2 5.0 %collective-permute-start.5 = (f32[56]{0:T(128)S(1)}, f32[56]{0:T(128)S(1)}, u32[]{:S(2)}, u32[]{:S(2)}) collective-permute-start(f32[56]{0:T(128)S(1)} %add_add_fusion.1), channel_id=1, source_target_pairs={{0,1},{1,2},{2,3},{3,4},{4,5},{5,6},{6,7},{7,0},{8,9},{9,10},{10,1... | collective-permute-start | bytes 680 | tf_op jit(solution)/shard_map/ppermute | solution.py:135

commit v2 on v1

v2 whole, which is shorter than its diff:
```python
import functools
import math

import jax
import jax.numpy as jnp
import numpy as np
from jax import lax
from jax.experimental import pallas as pl
from jax.experimental.pallas import tpu as pltpu
from jax.sharding import PartitionSpec as P

P_SIZE = 256
NT = 256
NF = 24
NK = 8
JD = 4
LD = JD * NK
ROWS = 40
PAIR = 72
PARTS = 2
VMEM = pl.BlockSpec(memory_space=pltpu.VMEM)
PARAMS = pltpu.CompilerParams(vmem_limit_bytes=32 * 1024 * 1024)


def fourier_table(freq_ids, times, total):
    turns = times[:, None] * freq_ids[None, :] % total
    theta = 2.0 * math.pi / total * turns.astype(jnp.float32)
    window = 0.5 - 0.5 * jnp.cos(2.0 * math.pi / total * times.astype(jnp.float32))
    scale = 1.0 / math.sqrt(0.375 * total)
    cosine = scale * window[:, None] * jnp.cos(theta)
    sine = -scale * window[:, None] * jnp.sin(theta)
    table = jnp.stack([cosine, sine], axis=-1)
    return table.reshape(times.shape[0], -1).astype(jnp.bfloat16)


def line_matrix():
    d = np.zeros((P_SIZE, P_SIZE), np.float32)
    for p in range(2, P_SIZE - 2):
        d[p - 2, p], d[p - 1, p], d[p + 1, p], d[p + 2, p] = 1, -8, 8, -1
    first, second = (-25, 48, -36, 16, -3), (-3, -10, 18, -6, 1)
    for i in range(5):
        d[i, 0], d[i, 1] = first[i], second[i]
        d[P_SIZE - 1 - i, P_SIZE - 1], d[P_SIZE - 1 - i, P_SIZE - 2] = -first[i], -second[i]
    return jnp.asarray(d, jnp.bfloat16)


def dft_kernel(mine_ref, other_ref, table_ref, own_ref, next_ref, across_ref, last_ref):
    def share(d):
        lines = jnp.concatenate(
            [mine_ref[d].reshape(-1, P_SIZE), other_ref[d].reshape(-1, P_SIZE)], axis=0
        )
        return jnp.dot(table_ref[d % 2], lines, preferred_element_type=jnp.float32)

    for pair in range(own_ref.shape[0]):
        even, odd = share(2 * pair), share(2 * pair + 1)
        for k, ref in enumerate((own_ref, next_ref, across_ref, last_ref)):
            first, second = even[k * ROWS : (k + 1) * ROWS], odd[k * ROWS : (k + 1) * ROWS]
            both = jnp.concatenate(
                [first[: ROWS - 8], first[ROWS - 8 :] + second[:8], second[8:]], axis=0
            )
            ref[pair] = both.astype(ref.dtype)


def sum_kernel(parts, *refs):
    out_ref = refs[-1]
    pair = 0
    for part in range(parts):
        own, a, b, c = refs[4 * part : 4 * part + 4]
        for i in range(own.shape[0]):
            total = own[i] + a[i].astype(jnp.float32)
            total = total + b[i].astype(jnp.float32) + c[i].astype(jnp.float32)
            total = total.astype(jnp.bfloat16)
            out_ref[2 * pair] = total[:ROWS]
            out_ref[2 * pair + 1] = total[PAIR - ROWS :]
            pair += 1


def place_kernel(place_ref, held_ref, own_ref, low_ref, high_ref):
    held = held_ref[...].reshape(-1, P_SIZE)
    rows = jnp.dot(place_ref[...], held, preferred_element_type=jnp.float32)
    rows = rows.astype(jnp.bfloat16).reshape(own_ref.shape)
    own_ref[...] = rows
    low_ref[...] = rows[:, :, JD - 2 :]
    high_ref[...] = rows[:, :, :2]


def vorticity_kernel(
    scale,
    own_ref,
    low_ref,
    high_ref,
    line_ref,
    metric_ref,
    weight_ref,
    stored_ref,
    spectra_ref,
    gram_ref,
    sums_ref,
):
    sums_ref[...] = jnp.zeros_like(sums_ref)
    nf = stored_ref.shape[0]
    xi_x, xi_y, eta_x, eta_y = (metric_ref[i].reshape(JD, 1, P_SIZE) for i in range(4))
    weight = weight_ref[...].reshape(1, JD, 1, P_SIZE)
    twelfth = 1.0 / 12.0

    for f in range(nf):
        new = []
        for r in range(2):
            q = 2 * f + r
            d_x, d_y, d_z = [], [], []
            for c in range(3):
                line = own_ref[q, c].reshape(LD, P_SIZE)
                along = jnp.dot(line, line_ref[...], preferred_element_type=jnp.float32)
                along = (along * twelfth).reshape(JD, NK, P_SIZE)
                center = own_ref[q, c].astype(jnp.float32)
                padded = jnp.concatenate(
                    [
                        low_ref[q, c].astype(jnp.float32),
                        center,
                        high_ref[q, c].astype(jnp.float32),
                    ],
                    axis=0,
                )
                pitch = (
                    padded[:-4] - 8.0 * padded[1:-3] + 8.0 * padded[3:-1] - padded[4:]
                ) * twelfth
                span = (
                    pltpu.roll(center, 2, 1)
                    - 8.0 * pltpu.roll(center, 1, 1)
                    + 8.0 * pltpu.roll(center, NK - 1, 1)
                    - pltpu.roll(center, NK - 2, 1)
                ) * twelfth
                d_x.append(xi_x * along + eta_x * pitch)
                d_y.append(xi_y * along + eta_y * pitch)
                d_z.append(span)
            vort = [d_y[2] - d_z[1], d_z[0] - d_x[2], d_x[1] - d_y[0]]
            vort = [v.astype(jnp.bfloat16) for v in vort]
            for c in range(3):
                spectra_ref[f, r, c] = vort[c]
            new.append(jnp.stack([v.astype(jnp.float32) for v in vort], axis=0))
        columns = [tuple(new)] + [
            tuple(stored_ref[f, a, r].astype(jnp.float32) for r in range(2)) for a in range(2)
        ]

        def put(part, a, b, value):
            total = jnp.sum(value, axis=(0, 1, 2)).reshape(1, P_SIZE)
            total = total[:, :128] + total[:, 128:]
            row = ((f * 2 + part) * 3 + a) * 3 + b
            sums_ref[row : row + 1, :] = total
            if a != b:
                row = ((f * 2 + part) * 3 + b) * 3 + a
                sums_ref[row : row + 1, :] = total if part == 0 else -total

        for a in range(3):
            real, imag = (weight * v for v in columns[a])
            for b in range(a, 3):
                put(0, a, b, real * columns[b][0] + imag * columns[b][1])
                if a != b:
                    put(1, a, b, real * columns[b][1] - imag * columns[b][0])

    total = lax.dot_general(
        jnp.full((8, 128), scale, jnp.float32),
        sums_ref[...],
        (((1,), (1,)), ((), ())),
        precision=lax.Precision.HIGHEST,
        preferred_element_type=jnp.float32,
    )
    gram_ref[...] = jnp.broadcast_to(total[:1].reshape(1, 1, 128), gram_ref.shape)


def shares(snapshots, freq_ids):
    groups = lax.axis_size("block")
    block = lax.axis_index("block")
    held = jnp.transpose(snapshots[0], (0, 1, 3, 2, 4))
    step = held.shape[0] // PARTS
    mine = [held[i * step : (i + 1) * step] for i in range(PARTS)]
    other = [lax.ppermute(v, "block", [(i, i ^ 1) for i in range(groups)]) for v in mine]

    local = held.shape[3]
    both = jnp.stack([block, block ^ 1])[:, None]
    times = (both * local + jnp.arange(local, dtype=jnp.int32)).reshape(-1)
    chips = groups // 2
    target = (block // 2 + jnp.arange(chips, dtype=jnp.int32)) % chips * 2 + block % 2
    ids = jnp.take(freq_ids.reshape(groups, -1), target, axis=0).reshape(-1)
    nq = 2 * NF // groups
    table = fourier_table(ids, times, NT).reshape(2, local, chips, nq)
    table = jnp.transpose(table, (2, 3, 0, 1))
    table = jnp.broadcast_to(table[:, None], (chips, 6, nq, 2, local))
    table = table.reshape(chips, 6 * nq, 2, 1, local)
    row = jnp.arange(6 * nq, dtype=jnp.int32)[:, None, None, None]
    line = jnp.arange(6, dtype=jnp.int32)[:, None]
    table = jnp.where(row // nq == line, table, 0).reshape(chips, 6 * nq, 12 * local)
    pad = ROWS - 6 * nq
    table = jnp.stack(
        [jnp.pad(table, ((0, 0), (0, pad), (0, 0))), jnp.pad(table, ((0, 0), (pad, 0), (0, 0)))]
    ).reshape(2, chips * ROWS, 12 * local)

    operands = []
    for i in range(PARTS):
        own, *sends = pl.pallas_call(
            dft_kernel,
            out_shape=[
                jax.ShapeDtypeStruct(
                    (step // 2, PAIR, P_SIZE), jnp.bfloat16 if k else jnp.float32
                )
                for k in range(chips)
            ],
            in_specs=[VMEM] * 3,
            out_specs=[VMEM] * chips,
            compiler_params=PARAMS,
            name="dft",
        )(mine[i], other[i], table)
        operands.append(own)
        for k, send in enumerate(sends, 1):
            route = [(j, (j + 2 * k) % groups) for j in range(groups)]
            operands.append(lax.ppermute(send, "block", route))
    return pl.pallas_call(
        functools.partial(sum_kernel, PARTS),
        out_shape=jax.ShapeDtypeStruct((held.shape[0], ROWS, P_SIZE), jnp.bfloat16),
        in_specs=[VMEM] * len(operands),
        out_specs=VMEM,
        compiler_params=PARAMS,
        name="sum",
    )(*operands)


def placing(slot_line):
    me = lax.axis_index("space")
    ids = lax.dynamic_index_in_dim(slot_line, me, 1, keepdims=False)
    in_row = jnp.arange(ROWS, dtype=jnp.int32) - (ROWS - 36) * (me % 2)
    held = jnp.where(in_row[None, :] < 18, ids[:, 0:1], ids[:, 1:2])
    inner = in_row % 18
    source = (inner % 6 * 3 + inner // 6)[None, :] * LD + held
    real = (in_row >= 0) & (in_row < 36)
    source = jnp.where((held >= 0) & real[None, :], source, -1).reshape(1, -1)
    target = jnp.arange(18 * LD, dtype=jnp.int32)[:, None]
    return (source == target).astype(jnp.bfloat16)


def per_device(snapshots, slot_line, freq_ids, metrics, weights, stored_spectra):
    groups = lax.axis_size("block")
    holders = lax.axis_size("space")
    velocity = shares(snapshots, freq_ids)
    velocity = lax.all_to_all(velocity, "space", split_axis=0, concat_axis=0, tiled=True)

    nf = NF // groups
    own, low, high = pl.pallas_call(
        place_kernel,
        out_shape=[
            jax.ShapeDtypeStruct((2 * nf, 3, JD, NK, P_SIZE), jnp.bfloat16),
            jax.ShapeDtypeStruct((2 * nf, 3, 2, NK, P_SIZE), jnp.bfloat16),
            jax.ShapeDtypeStruct((2 * nf, 3, 2, NK, P_SIZE), jnp.bfloat16),
        ],
        in_specs=[VMEM, VMEM],
        out_specs=[VMEM, VMEM, VMEM],
        compiler_params=PARAMS,
        name="place",
    )(placing(slot_line), velocity)
    forward = [(i, (i + 1) % holders) for i in range(holders)]
    backward = [(target, source) for source, target in forward]
    low = lax.ppermute(low, "space", forward)
    high = lax.ppermute(high, "space", backward)

    spectra, gram = pl.pallas_call(
        functools.partial(vorticity_kernel, 1.0 / (3.0 * JD * holders * NK * P_SIZE)),
        out_shape=[
            jax.ShapeDtypeStruct((nf, 2, 3, JD, NK, P_SIZE), jnp.bfloat16),
            jax.ShapeDtypeStruct((holders, 1, 128), jnp.float32),
        ],
        in_specs=[VMEM] * 7,
        out_specs=[VMEM, VMEM],
        scratch_shapes=[pltpu.VMEM((128, 128), jnp.float32)],
        compiler_params=PARAMS,
        name="vorticity",
    )(own, low, high, line_matrix(), metrics, weights, stored_spectra)
    gram = lax.all_to_all(gram, "space", split_axis=0, concat_axis=0, tiled=True)
    gram = jnp.sum(gram, axis=(0, 1))[: nf * 18].reshape(nf, 2, 3, 3)
    return (spectra, gram)


def solution(mesh):
    return jax.shard_map(
        per_device,
        mesh=mesh,
        in_specs=(
            P("space", None, None, "block", None, None),
            P(),
            P(),
            P(None, "space", None),
            P("space", None),
            P("block", None, None, None, "space", None, None),
        ),
        out_specs=(P("block", None, None, "space", None, None), P("block", None, None, None)),
        check_vma=False,
    )
```

time: 130 us -> 105 us (0.81)
  waiting for transfers between devices: 74.6 us -> 43.2 us
  starting transfers between devices: 44.4 us -> 23.5 us
  blocking collectives: 0 us -> 16.6 us
  Pallas kernels: 3.55 us -> 10.6 us
  local copies, waits for them, and re-layouts: 3.29 us -> 7.83 us
    all_to_all x2 -> x0, waiting for transfers between devices: 44.3 us -> none  [the longest x1 34.5 us: per_device(): raw = lax.all_to_all(raw, 'block', split_axis=0, concat_axis=0, tiled=True)]
    all_to_all x0 -> x1, blocking collectives: none -> 16.6 us  [per_device(): lax.all_to_all(gram, 'space', split_axis=0, concat_axis=0, tiled=True)]
    ppermute x10 -> x8, waiting for transfers between devices: 7.68 us -> 20.7 us  [the longest x6 20.7 us: shares(): operands.append(lax.ppermute(send, 'block', route))]
    all_to_all x2 -> x0, starting transfers between devices: 12.3 us -> none  [the longest x1 6.33 us: per_device(): lax.all_to_all(velocity, 'block', split_axis=0, concat_axis=0, tiled=True)]
    ppermute x10 -> x8, starting transfers between devices: 16.2 us -> 8.36 us  [the longest x6 7.77 us: shares(): operands.append(lax.ppermute(send, 'block', route))]
    pallas_call x3 -> x5, Pallas kernels: 3.55 us -> 10.6 us  [the longest x2 6.22 us: shares(): pl.pallas_call(dft_kernel, out_shape=[jax.ShapeDtypeStruct((step // 2, PA...]
    broadcast_in_dim x6, local copies, waits for them, and re-layouts: 0.13 us -> 2.78 us  [the longest x4 2.73 us: shares(): jnp.where(row // nq == line, table, 0).reshape(chips, 6 * nq, 12 * local)]
    slice x0 -> x1, local copies, waits for them, and re-layouts: none -> 2.24 us  [shares(): mine = [held[i * step:(i + 1) * step] for i in range(PARTS)]]
  transfers between devices with their start and end apart: 15 -> 11, of which waited for: 8 -> 6; matrix products, arithmetic and copies ran while one was open for 2% -> 5% of each run, Pallas kernels for 0% -> 6%
where the time goes in v2:
time: 105 us; the launch traced here: 104 us
  waiting for transfers between devices  43.2 us (41%)
  starting transfers between devices  23.5 us (22%)
  blocking collectives  16.6 us (16%)
  Pallas kernels  10.6 us (10%)
  local copies, waits for them, and re-layouts  7.83 us (7%)
  other arithmetic  1.42 us (1%)
    ppermute x6, waiting for transfers between devices, shares(): operands.append(lax.ppermute(send, 'block', route))  20.7 us
    all_to_all x1, waiting for transfers between devices, per_device(): lax.all_to_all(velocity, 'space', split_axis=0, concat_axis=0, tiled=True)  19.4 us
    all_to_all x1, blocking collectives, per_device(): lax.all_to_all(gram, 'space', split_axis=0, concat_axis=0, tiled=True)  16.6 us
    all_to_all x1, starting transfers between devices, per_device(): lax.all_to_all(velocity, 'space', split_axis=0, concat_axis=0, tiled=True)  9.75 us
    ppermute x6, starting transfers between devices, shares(): operands.append(lax.ppermute(send, 'block', route))  7.77 us
    pallas_call x2, Pallas kernels, shares(): pl.pallas_call(dft_kernel, out_shape=[jax.ShapeDtypeStruct((step // 2, PA...  6.22 us
    ppermute x1, starting transfers between devices, per_device(): high = lax.ppermute(high, 'space', backward)  3.43 us
    ppermute x1, waiting for transfers between devices, per_device(): low = lax.ppermute(low, 'space', forward)  3.12 us
  transfers between devices with their start and end apart: 11, of which 6 were waited for; matrix products, arithmetic and copies ran while one was open for 5% of the time, Pallas kernels for 6%

profile of v2, /device:TPU:6, one launch (start us, length us, event | category | flops | bytes accessed | tf_op | source)
XLA Modules:
  0.0 104.1 jit_solution(514897635897758318)
XLA Ops:
  0.7 2.2 %fusion.17 = (bf16[16,2,3,32,256]{4,3,2,1,0:T(8,128)(2,1)S(1)}, bf16[16,2,3,32,256]{4,3,2,1,0:T(8,128)(2,1)S(1)}) fusion(bf16[32,2,3,32,256]{4,3,2,1,0:T(8,128)(2,1)} %bitcast.21), kind=kLoop, calls=%fused_computation.58 | loop fusion | bytes 6291456 | tf_op jit(solution)/shard_map/slice | solution.py:176
  3.0 0.5 collective-permute-start
  3.6 0.6 gather_fusion
  4.6 0.3 multiply_convert_fusion.1
  5.1 1.0 broadcast_in_dim.93
  6.1 1.5 %broadcast_in_dim.94 = bf16[4,36,384]{2,0,1:T(4,128)(2,1)S(1)} reshape(bf16[4,36,2,6,32]{4,3,2,0,1:T(8,128)(2,1)} %broadcast_in_dim.93) | data formatting | bytes 221184 | tf_op jit(solution)/shard_map/jit(_where)/broadcast_in_dim | solution.py:192
  7.7 0.1 broadcast_in_dim.87
  7.8 0.1 broadcast_in_dim.88
  8.0 0.1 broadcast_select_fusion
  8.2 3.1 %dft.3 = (f32[8,72,256]{2,1,0:T(8,128)S(1)}, bf16[8,72,256]{2,1,0:T(8,128)(2,1)S(1)}, bf16[8,72,256]{2,1,0:T(8,128)(2,1)}, bf16[8,72,256]{2,1,0:T(8,128)(2,1)}) custom-call(bf16[16,2,3,32,256]{4,3,2,1,0:T(8,128)(2,1)S(1)} %get-tuple-element.34.mine_ref, bf16[16,2,3,32,256]{4,3,2,1,0:T(8,128)(2,1)} %collective-permute-done.4.other_ref, ...), custom_call_target="tpu_custom_call" | custom-call | tf_op jit(solution)/shard_map/dft/pallas_call | solution.py:200
  11.3 0.8 copy-done.1
  12.1 2.2 %collective-permute-start.5 = (bf16[8,72,256]{2,1,0:T(8,128)(2,1)S(1)}, bf16[8,72,256]{2,1,0:T(8,128)(2,1)S(1)}, u32[]{:S(2)}, u32[]{:S(2)}) collective-permute-start(bf16[8,72,256]{2,1,0:T(8,128)(2,1)S(1)} %get-tuple-element.20), channel_id=1, source_target_pairs={{0,64},{32,96},{64,128},{96,160},{128,192},{160,224},{192,0},{224,... | collective-permute-start | bytes 884744 | tf_op jit(solution)/shard_map/ppermute | solution.py:216
  14.3 0.7 collective-permute-start.6
  15.0 0.2 collective-permute-start.7
  15.2 3.1 %dft.2 = (f32[8,72,256]{2,1,0:T(8,128)S(1)}, bf16[8,72,256]{2,1,0:T(8,128)(2,1)}, bf16[8,72,256]{2,1,0:T(8,128)(2,1)}, bf16[8,72,256]{2,1,0:T(8,128)(2,1)}) custom-call(bf16[16,2,3,32,256]{4,3,2,1,0:T(8,128)(2,1)S(1)} %get-tuple-element.35.mine_ref, bf16[16,2,3,32,256]{4,3,2,1,0:T(8,128)(2,1)} %collective-permute-done.other_ref, ...), custom_call_target="tpu_custom_call" | custom-call | tf_op jit(solution)/shard_map/dft/pallas_call | solution.py:200
  18.3 3.1 %collective-permute-start.1 = (bf16[8,72,256]{2,1,0:T(8,128)(2,1)}, bf16[8,72,256]{2,1,0:T(8,128)(2,1)S(1)}, u32[]{:S(2)}, u32[]{:S(2)}) collective-permute-start(bf16[8,72,256]{2,1,0:T(8,128)(2,1)} %get-tuple-element.16), channel_id=1, source_target_pairs={{0,64},{32,96},{64,128},{96,160},{128,192},{160,224},{192,0},{224,... | collective-permute-start | bytes 884744 | tf_op jit(solution)/shard_map/ppermute | solution.py:216
  21.4 1.6 %collective-permute-start.2 = (bf16[8,72,256]{2,1,0:T(8,128)(2,1)}, bf16[8,72,256]{2,1,0:T(8,128)(2,1)S(1)}, u32[]{:S(2)}, u32[]{:S(2)}) collective-permute-start(bf16[8,72,256]{2,1,0:T(8,128)(2,1)} %get-tuple-element.17), channel_id=1, source_target_pairs={{0,128},{32,160},{64,192},{96,224},{128,0},{160,32},{192,64},{224,... | collective-permute-start | bytes 884744 | tf_op jit(solution)/shard_map/ppermute | solution.py:216
  23.0 4.7 %collective-permute-done.5.refs_5_ = bf16[8,72,256]{2,1,0:T(8,128)(2,1)S(1)} collective-permute-done((bf16[8,72,256]{2,1,0:T(8,128)(2,1)S(1)}, bf16[8,72,256]{2,1,0:T(8,128)(2,1)S(1)}, u32[]{:S(2)}, u32[]{:S(2)}) %collective-permute-start.5) | collective-permute-done | bytes 294944 | tf_op jit(solution)/shard_map/ppermute | solution.py:216
  27.7 4.8 %collective-permute-done.7.refs_7_ = bf16[8,72,256]{2,1,0:T(8,128)(2,1)} collective-permute-done((bf16[8,72,256]{2,1,0:T(8,128)(2,1)}, bf16[8,72,256]{2,1,0:T(8,128)(2,1)}, u32[]{:S(2)}, u32[]{:S(2)}) %collective-permute-start.7) | collective-permute-done | bytes 294944 | tf_op jit(solution)/shard_map/ppermute | solution.py:216
  32.4 7.5 %collective-permute-done.1.refs_1_ = bf16[8,72,256]{2,1,0:T(8,128)(2,1)S(1)} collective-permute-done((bf16[8,72,256]{2,1,0:T(8,128)(2,1)}, bf16[8,72,256]{2,1,0:T(8,128)(2,1)S(1)}, u32[]{:S(2)}, u32[]{:S(2)}) %collective-permute-start.1) | collective-permute-done | bytes 294944 | tf_op jit(solution)/shard_map/ppermute | solution.py:216
  39.9 3.8 %collective-permute-done.3.refs_3_ = bf16[8,72,256]{2,1,0:T(8,128)(2,1)S(1)} collective-permute-done((bf16[8,72,256]{2,1,0:T(8,128)(2,1)}, bf16[8,72,256]{2,1,0:T(8,128)(2,1)S(1)}, u32[]{:S(2)}, u32[]{:S(2)}) %collective-permute-start.3) | collective-permute-done | bytes 294944 | tf_op jit(solution)/shard_map/ppermute | solution.py:216
  43.7 2.1 %sum.1 = bf16[32,40,256]{2,1,0:T(8,128)(2,1)} custom-call(f32[8,72,256]{2,1,0:T(8,128)S(1)} %get-tuple-element.15.refs_0_, bf16[8,72,256]{2,1,0:T(8,128)(2,1)S(1)} %collective-permute-done.1.refs_1_, bf16[8,72,256]{2,1,0:T(8,128)(2,1)S(1)} %collective-permute-done.2.refs_2_, bf16[8,72,256]{2,1,0:T(8,128)(2,1)S(1)} %collective-permute-done.3.refs_3_, ...), custom_call_target="tpu_custom_call" | custom-call | tf_op jit(solution)/shard_map/sum/pallas_call | solution.py:217
  45.8 9.8 %all-to-all-start = ((bf16[32,40,256]{2,1,0:T(8,128)(2,1)}), bf16[32,40,256]{2,1,0:T(8,128)(2,1)S(1)}, u32[]{:S(2)}, u32[]{:S(2)}) async-start(bf16[32,40,256]{2,1,0:T(8,128)(2,1)} %sum.1), calls=%async_computation | async-start | bytes 1310720 | tf_op jit(solution)/shard_map/all_to_all | solution.py:244
  56.0 0.4 fusion.place_ref
  56.4 19.4 %all-to-all-done.held_ref = bf16[32,40,256]{2,1,0:T(8,128)(2,1)S(1)} async-done(((bf16[32,40,256]{2,1,0:T(8,128)(2,1)}), bf16[32,40,256]{2,1,0:T(8,128)(2,1)S(1)}, u32[]{:S(2)}, u32[]{:S(2)}) %all-to-all-start) | async-done | bytes 655392 | tf_op jit(solution)/shard_map/all_to_all | solution.py:244
  75.9 0.6 place.1
  76.4 2.0 %collective-permute-start.8 = (bf16[6,3,2,8,256]{4,3,2,1,0:T(8,128)(2,1)S(1)}, bf16[6,3,2,8,256]{4,3,2,1,0:T(8,128)(2,1)S(1)}, u32[]{:S(2)}, u32[]{:S(2)}) collective-permute-start(bf16[6,3,2,8,256]{4,3,2,1,0:T(8,128)(2,1)S(1)} %get-tuple-element.24), channel_id=1, source_target_pairs={{0,1},{1,2},{2,3},{3,4},{4,5},{5,6},{6,7},{7,8},{8,9},{9,10},{10,1... | collective-permute-start | bytes 442376 | tf_op jit(solution)/shard_map/ppermute | solution.py:261
  78.4 3.4 %collective-permute-start.9 = (bf16[6,3,2,8,256]{4,3,2,1,0:T(8,128)(2,1)S(1)}, bf16[6,3,2,8,256]{4,3,2,1,0:T(8,128)(2,1)S(1)}, u32[]{:S(2)}, u32[]{:S(2)}) collective-permute-start(bf16[6,3,2,8,256]{4,3,2,1,0:T(8,128)(2,1)S(1)} %get-tuple-element.25), channel_id=1, source_target_pairs={{1,0},{2,1},{3,2},{4,3},{5,4},{6,5},{7,6},{8,7},{9,8},{10,9},{11,1... | collective-permute-start | bytes 442376 | tf_op jit(solution)/shard_map/ppermute | solution.py:262
  81.8 3.1 %collective-permute-done.8.low_ref = bf16[6,3,2,8,256]{4,3,2,1,0:T(8,128)(2,1)S(1)} collective-permute-done((bf16[6,3,2,8,256]{4,3,2,1,0:T(8,128)(2,1)S(1)}, bf16[6,3,2,8,256]{4,3,2,1,0:T(8,128)(2,1)S(1)}, u32[]{:S(2)}, u32[]{:S(2)}) %collective-permute-start.8) | collective-permute-done | bytes 147488 | tf_op jit(solution)/shard_map/ppermute | solution.py:261
  85.0 1.8 %vorticity.1 = (bf16[3,2,3,4,8,256]{5,4,3,2,1,0:T(8,128)(2,1)}, f32[32,1,128]{2,1,0:T(1,128)S(1)}) custom-call(bf16[6,3,4,8,256]{4,3,2,1,0:T(8,128)(2,1)S(1)} %get-tuple-element.23.own_ref, bf16[6,3,2,8,256]{4,3,2,1,0:T(8,128)(2,1)S(1)} %collective-permute-done.8.low_ref, bf16[6,3,2,8,256]{4,3,2,1,0:T(8,128)(2,1)S(1)} %collective-permute-done.9.high_ref, ...), custom_call_target="tpu_custom_call" | custom-call | tf_op jit(solution)/shard_map/vorticity/pallas_call | solution.py:264
  86.8 16.6 %all_to_all.10 = f32[32,1,128]{2,1,0:T(1,128)S(1)} all-to-all(f32[32,1,128]{2,1,0:T(1,128)S(1)} %get-tuple-element.27), channel_id=1, replica_groups=mesh['block'=8,'space'=32] {'space'}, dimensions={0} | all-to-all | bytes 32768 | tf_op jit(solution)/shard_map/all_to_all | solution.py:276
  103.5 0.6 copy.19
  (50 shorter events, 1.6 us)
Async XLA Ops:
  0.6 54.9 %copy-start = (s32[32,32,2]{1,2,0:T(2,128)S(1)}, s32[32,32,2]{1,2,0:T(2,128)}, u32[]{:S(2)}) copy-start(s32[32,32,2]{1,2,0:T(2,128)} %param.8) | copy-start | bytes 24580
  0.6 2.9 %copy-start.7 = (s32[24]{0:T(128)S(1)}, s32[24]{0:T(128)}, u32[]{:S(2)}) copy-start(s32[24]{0:T(128)} %param.9) | copy-start | bytes 292
  2.9 5.3 %collective-permute-start.4 = (bf16[16,2,3,32,256]{4,3,2,1,0:T(8,128)(2,1)S(1)}, bf16[16,2,3,32,256]{4,3,2,1,0:T(8,128)(2,1)}, u32[]{:S(2)}, u32[]{:S(2)}) collective-permute-start(bf16[16,2,3,32,256]{4,3,2,1,0:T(8,128)(2,1)S(1)} %get-tuple-element.34.mine_ref), channel_id=1, source_target_pairs={{0,32},{32,0},{64,96},{96,64},{128,160},{160,128},{192,224},{224,1... | collective-permute-start | bytes 4718600 | tf_op jit(solution)/shard_map/ppermute | solution.py:177
  3.0 12.2 %collective-permute-start = (bf16[16,2,3,32,256]{4,3,2,1,0:T(8,128)(2,1)S(1)}, bf16[16,2,3,32,256]{4,3,2,1,0:T(8,128)(2,1)}, u32[]{:S(2)}, u32[]{:S(2)}) collective-permute-start(bf16[16,2,3,32,256]{4,3,2,1,0:T(8,128)(2,1)S(1)} %get-tuple-element.35.mine_ref), channel_id=1, source_target_pairs={{0,32},{32,0},{64,96},{96,64},{128,160},{160,128},{192,224},{224,1... | collective-permute-start | bytes 4718600 | tf_op jit(solution)/shard_map/ppermute | solution.py:177
  11.3 0.8 copy-start.1
  12.1 15.6 %collective-permute-start.5 = (bf16[8,72,256]{2,1,0:T(8,128)(2,1)S(1)}, bf16[8,72,256]{2,1,0:T(8,128)(2,1)S(1)}, u32[]{:S(2)}, u32[]{:S(2)}) collective-permute-start(bf16[8,72,256]{2,1,0:T(8,128)(2,1)S(1)} %get-tuple-element.20), channel_id=1, source_target_pairs={{0,64},{32,96},{64,128},{96,160},{128,192},{160,224},{192,0},{224,... | collective-permute-start | bytes 884744 | tf_op jit(solution)/shard_map/ppermute | solution.py:216
  14.3 13.4 %collective-permute-start.6 = (bf16[8,72,256]{2,1,0:T(8,128)(2,1)}, bf16[8,72,256]{2,1,0:T(8,128)(2,1)S(1)}, u32[]{:S(2)}, u32[]{:S(2)}) collective-permute-start(bf16[8,72,256]{2,1,0:T(8,128)(2,1)} %get-tuple-element.21), channel_id=1, source_target_pairs={{0,128},{32,160},{64,192},{96,224},{128,0},{160,32},{192,64},{224,... | collective-permute-start | bytes 884744 | tf_op jit(solution)/shard_map/ppermute | solution.py:216
  15.0 28.7 %copy-start.2 = (f32[8,72,256]{2,1,0:T(8,128)S(1)}, f32[8,72,256]{2,1,0:T(8,128)}, u32[]{:S(2)}) copy-start(f32[8,72,256]{2,1,0:T(8,128)} %copy-done.1) | copy-start | bytes 1769476
  15.0 17.5 %collective-permute-start.7 = (bf16[8,72,256]{2,1,0:T(8,128)(2,1)}, bf16[8,72,256]{2,1,0:T(8,128)(2,1)}, u32[]{:S(2)}, u32[]{:S(2)}) collective-permute-start(bf16[8,72,256]{2,1,0:T(8,128)(2,1)} %get-tuple-element.22), channel_id=1, source_target_pairs={{0,192},{32,224},{64,0},{96,32},{128,64},{160,96},{192,128},{224,1... | collective-permute-start | bytes 884744 | tf_op jit(solution)/shard_map/ppermute | solution.py:216
  18.3 21.6 %collective-permute-start.1 = (bf16[8,72,256]{2,1,0:T(8,128)(2,1)}, bf16[8,72,256]{2,1,0:T(8,128)(2,1)S(1)}, u32[]{:S(2)}, u32[]{:S(2)}) collective-permute-start(bf16[8,72,256]{2,1,0:T(8,128)(2,1)} %get-tuple-element.16), channel_id=1, source_target_pairs={{0,64},{32,96},{64,128},{96,160},{128,192},{160,224},{192,0},{224,... | collective-permute-start | bytes 884744 | tf_op jit(solution)/shard_map/ppermute | solution.py:216
  21.4 18.6 %collective-permute-start.2 = (bf16[8,72,256]{2,1,0:T(8,128)(2,1)}, bf16[8,72,256]{2,1,0:T(8,128)(2,1)S(1)}, u32[]{:S(2)}, u32[]{:S(2)}) collective-permute-start(bf16[8,72,256]{2,1,0:T(8,128)(2,1)} %get-tuple-element.17), channel_id=1, source_target_pairs={{0,128},{32,160},{64,192},{96,224},{128,0},{160,32},{192,64},{224,... | collective-permute-start | bytes 884744 | tf_op jit(solution)/shard_map/ppermute | solution.py:216
  27.7 16.0 %collective-permute-start.3 = (bf16[8,72,256]{2,1,0:T(8,128)(2,1)}, bf16[8,72,256]{2,1,0:T(8,128)(2,1)S(1)}, u32[]{:S(2)}, u32[]{:S(2)}) collective-permute-start(bf16[8,72,256]{2,1,0:T(8,128)(2,1)} %get-tuple-element.18), channel_id=1, source_target_pairs={{0,192},{32,224},{64,0},{96,32},{128,64},{160,96},{192,128},{224,1... | collective-permute-start | bytes 884744 | tf_op jit(solution)/shard_map/ppermute | solution.py:216
  45.8 30.1 %all-to-all-start = ((bf16[32,40,256]{2,1,0:T(8,128)(2,1)}), bf16[32,40,256]{2,1,0:T(8,128)(2,1)S(1)}, u32[]{:S(2)}, u32[]{:S(2)}) async-start(bf16[32,40,256]{2,1,0:T(8,128)(2,1)} %sum.1), calls=%async_computation | async-start | bytes 1310720 | tf_op jit(solution)/shard_map/all_to_all | solution.py:244
  56.0 29.0 %copy-start.3 = (bf16[3,2,2,3,4,8,256]{6,5,4,3,2,1,0:T(8,128)(2,1)S(1)}, bf16[3,2,2,3,4,8,256]{6,5,4,3,2,1,0:T(8,128)(2,1)}, u32[]{:S(2)}) copy-start(bf16[3,2,2,3,4,8,256]{6,5,4,3,2,1,0:T(8,128)(2,1)} %stored_ref.1) | copy-start | bytes 1769476
  56.0 29.0 %copy-start.4 = (bf16[256,256]{1,0:T(8,128)(2,1)S(1)}, bf16[256,256]{1,0:T(8,128)(2,1)}, u32[]{:S(2)}) copy-start(bf16[256,256]{1,0:T(8,128)(2,1)} %constant.144.clone.line_ref) | copy-start | bytes 393220
  56.0 29.0 %copy-start.5 = (f32[4,4,256]{2,1,0:T(4,128)S(1)}, f32[4,4,256]{2,1,0:T(4,128)}, u32[]{:S(2)}) copy-start(f32[4,4,256]{2,1,0:T(4,128)} %metric_ref.1) | copy-start | bytes 49156
  56.0 29.0 %copy-start.6 = (f32[4,256]{1,0:T(4,128)S(1)}, f32[4,256]{1,0:T(4,128)}, u32[]{:S(2)}) copy-start(f32[4,256]{1,0:T(4,128)} %weight_ref.1) | copy-start | bytes 12292
  76.4 8.5 %collective-permute-start.8 = (bf16[6,3,2,8,256]{4,3,2,1,0:T(8,128)(2,1)S(1)}, bf16[6,3,2,8,256]{4,3,2,1,0:T(8,128)(2,1)S(1)}, u32[]{:S(2)}, u32[]{:S(2)}) collective-permute-start(bf16[6,3,2,8,256]{4,3,2,1,0:T(8,128)(2,1)S(1)} %get-tuple-element.24), channel_id=1, source_target_pairs={{0,1},{1,2},{2,3},{3,4},{4,5},{5,6},{6,7},{7,8},{8,9},{9,10},{10,1... | collective-permute-start | bytes 442376 | tf_op jit(solution)/shard_map/ppermute | solution.py:261
  78.4 6.5 %collective-permute-start.9 = (bf16[6,3,2,8,256]{4,3,2,1,0:T(8,128)(2,1)S(1)}, bf16[6,3,2,8,256]{4,3,2,1,0:T(8,128)(2,1)S(1)}, u32[]{:S(2)}, u32[]{:S(2)}) collective-permute-start(bf16[6,3,2,8,256]{4,3,2,1,0:T(8,128)(2,1)S(1)} %get-tuple-element.25), channel_id=1, source_target_pairs={{1,0},{2,1},{3,2},{4,3},{5,4},{6,5},{7,6},{8,7},{9,8},{10,9},{11,1... | collective-permute-start | bytes 442376 | tf_op jit(solution)/shard_map/ppermute | solution.py:262

commit v3 on v2

--- a/solution.py
+++ b/solution.py
@@ -17,20 +17,12 @@
 LD = JD * NK
 ROWS = 40
 PAIR = 72
-PARTS = 2
+PARTS = (16, 16)
+UNROLL = 2
+SHARE_US, JOIN_US = (20, 1), 1
 VMEM = pl.BlockSpec(memory_space=pltpu.VMEM)
-PARAMS = pltpu.CompilerParams(vmem_limit_bytes=32 * 1024 * 1024)
-
-
-def fourier_table(freq_ids, times, total):
-    turns = times[:, None] * freq_ids[None, :] % total
-    theta = 2.0 * math.pi / total * turns.astype(jnp.float32)
-    window = 0.5 - 0.5 * jnp.cos(2.0 * math.pi / total * times.astype(jnp.float32))
-    scale = 1.0 / math.sqrt(0.375 * total)
-    cosine = scale * window[:, None] * jnp.cos(theta)
-    sine = -scale * window[:, None] * jnp.sin(theta)
-    table = jnp.stack([cosine, sine], axis=-1)
-    return table.reshape(times.shape[0], -1).astype(jnp.bfloat16)
+SMEM = pl.BlockSpec(memory_space=pltpu.SMEM)
+PARAMS = pltpu.CompilerParams(vmem_limit_bytes=16 * 1024 * 1024)
 
 
 def line_matrix():
@@ -44,35 +36,91 @@
     return jnp.asarray(d, jnp.bfloat16)
 
 
-def dft_kernel(mine_ref, other_ref, table_ref, own_ref, next_ref, across_ref, last_ref):
-    def share(d):
+def table_kernel(chips, local, block_ref, freq_ref, table_ref):
+    block = block_ref[0]
+    half = 6 * local
+    lane = lax.broadcasted_iota(jnp.int32, (NF, 2 * half), 1)
+    far = (lane >= half).astype(jnp.int32)
+    time = (block ^ far) * local + ((lane - far * half) & (local - 1))
+    row = lax.broadcasted_iota(jnp.int32, (NF, 2 * half), 0)
+    freq = jnp.zeros_like(row)
+    for f in range(NF):
+        freq = jnp.where(row == f, freq_ref[f], freq)
+    theta = 2.0 * math.pi / NT * ((time * freq) & (NT - 1)).astype(jnp.float32)
+    window = 0.5 - 0.5 * jnp.cos(2.0 * math.pi / NT * time.astype(jnp.float32))
+    scale = 1.0 / math.sqrt(0.375 * NT)
+    waves = jnp.concatenate(
+        [scale * window * jnp.cos(theta), -scale * window * jnp.sin(theta)], axis=0
+    ).astype(jnp.bfloat16)
+
+    def line_of(row):
+        return sum((row >= 6 * i).astype(jnp.int32) for i in range(1, 6))
+
+    lane = lax.broadcasted_iota(jnp.int32, (ROWS, 2 * half), 1)
+    lane_line = line_of((lane - jnp.where(lane >= half, half, 0)) * 6 // local)
+    wide = lax.broadcasted_iota(jnp.int32, (ROWS, 2 * half), 0)
+    narrow = lax.broadcasted_iota(jnp.int32, (ROWS, 2 * NF), 0)
+    wave = lax.broadcasted_iota(jnp.int32, (ROWS, 2 * NF), 1)
+    for parity in range(2):
+        row = wide - 4 * parity
+        kept = (line_of(row) == lane_line) & (row >= 0) & (row < 36)
+        row = narrow - 4 * parity
+        real = row - 6 * line_of(row)
+        for k in range(chips):
+            group = ((block >> 1) + k) % chips * 2 + (block & 1)
+            pick = wave == group * 3 + (real >> 1) + NF * (real & 1)
+            pick = pick.astype(jnp.float32).astype(jnp.bfloat16)
+            rows = jnp.dot(pick, waves, preferred_element_type=jnp.float32)
+            rows = jnp.where(kept, rows, 0.0).astype(jnp.bfloat16)
+            table_ref[parity, k * ROWS : (k + 1) * ROWS] = rows
+
+
+def share_kernel(mine_ref, other_ref, table_ref, *out_refs):
+    def share(d, parity):
         lines = jnp.concatenate(
             [mine_ref[d].reshape(-1, P_SIZE), other_ref[d].reshape(-1, P_SIZE)], axis=0
         )
-        return jnp.dot(table_ref[d % 2], lines, preferred_element_type=jnp.float32)
-
-    for pair in range(own_ref.shape[0]):
-        even, odd = share(2 * pair), share(2 * pair + 1)
-        for k, ref in enumerate((own_ref, next_ref, across_ref, last_ref)):
+        return jnp.dot(table_ref[parity], lines, preferred_element_type=jnp.float32)
+
+    def step(pair, carry):
+        even, odd = share(2 * pair, 0), share(2 * pair + 1, 1)
+        for k, ref in enumerate(out_refs):
             first, second = even[k * ROWS : (k + 1) * ROWS], odd[k * ROWS : (k + 1) * ROWS]
             both = jnp.concatenate(
                 [first[: ROWS - 8], first[ROWS - 8 :] + second[:8], second[8:]], axis=0
             )
             ref[pair] = both.astype(ref.dtype)
-
-
-def sum_kernel(parts, *refs):
+        return carry
+
+    lax.fori_loop(0, out_refs[0].shape[0], step, 0, unroll=UNROLL)
+
+
+def join_kernel(kept_ref, passing_ref, out_ref):
+    def step(pair, carry):
+        total = kept_ref[pair] + passing_ref[pair].astype(jnp.float32)
+        out_ref[pair] = total.astype(jnp.bfloat16)
+        return carry
+
+    lax.fori_loop(0, out_ref.shape[0], step, 0, unroll=UNROLL)
+
+
+def sum_kernel(*refs):
     out_ref = refs[-1]
-    pair = 0
-    for part in range(parts):
-        own, a, b, c = refs[4 * part : 4 * part + 4]
-        for i in range(own.shape[0]):
-            total = own[i] + a[i].astype(jnp.float32)
-            total = total + b[i].astype(jnp.float32) + c[i].astype(jnp.float32)
+    start = 0
+    for part in range(len(refs) // 3):
+        own, *rest = refs[3 * part : 3 * part + 3]
+
+        def step(pair, carry, own=own, rest=rest, start=start):
+            total = own[pair]
+            for ref in rest:
+                total = total + ref[pair].astype(jnp.float32)
             total = total.astype(jnp.bfloat16)
-            out_ref[2 * pair] = total[:ROWS]
-            out_ref[2 * pair + 1] = total[PAIR - ROWS :]
-            pair += 1
+            out_ref[start + 2 * pair] = total[:ROWS]
+            out_ref[start + 2 * pair + 1] = total[PAIR - ROWS :]
+            return carry
+
+        lax.fori_loop(0, own.shape[0], step, 0, unroll=UNROLL)
+        start += 2 * own.shape[0]
 
 
 def place_kernel(place_ref, held_ref, own_ref, low_ref, high_ref):
@@ -168,55 +216,75 @@
     gram_ref[...] = jnp.broadcast_to(total[:1].reshape(1, 1, 128), gram_ref.shape)
 
 
+def cost(us):
+    return pl.CostEstimate(flops=int(us * 1e9), bytes_accessed=0, transcendentals=0)
+
+
 def shares(snapshots, freq_ids):
     groups = lax.axis_size("block")
+    chips = groups // 2
     block = lax.axis_index("block")
     held = jnp.transpose(snapshots[0], (0, 1, 3, 2, 4))
-    step = held.shape[0] // PARTS
-    mine = [held[i * step : (i + 1) * step] for i in range(PARTS)]
-    other = [lax.ppermute(v, "block", [(i, i ^ 1) for i in range(groups)]) for v in mine]
-
-    local = held.shape[3]
-    both = jnp.stack([block, block ^ 1])[:, None]
-    times = (both * local + jnp.arange(local, dtype=jnp.int32)).reshape(-1)
-    chips = groups // 2
-    target = (block // 2 + jnp.arange(chips, dtype=jnp.int32)) % chips * 2 + block % 2
-    ids = jnp.take(freq_ids.reshape(groups, -1), target, axis=0).reshape(-1)
-    nq = 2 * NF // groups
-    table = fourier_table(ids, times, NT).reshape(2, local, chips, nq)
-    table = jnp.transpose(table, (2, 3, 0, 1))
-    table = jnp.broadcast_to(table[:, None], (chips, 6, nq, 2, local))
-    table = table.reshape(chips, 6 * nq, 2, 1, local)
-    row = jnp.arange(6 * nq, dtype=jnp.int32)[:, None, None, None]
-    line = jnp.arange(6, dtype=jnp.int32)[:, None]
-    table = jnp.where(row // nq == line, table, 0).reshape(chips, 6 * nq, 12 * local)
-    pad = ROWS - 6 * nq
-    table = jnp.stack(
-        [jnp.pad(table, ((0, 0), (0, pad), (0, 0))), jnp.pad(table, ((0, 0), (pad, 0), (0, 0)))]
-    ).reshape(2, chips * ROWS, 12 * local)
-
-    operands = []
-    for i in range(PARTS):
-        own, *sends = pl.pallas_call(
-            dft_kernel,
+    owners, _, _, local, _ = held.shape
+
+    def along(value, k):
+        route = [(j, (j + 2 * k) % groups) for j in range(groups)]
+        return lax.ppermute(value, "block", route)
+
+    table = pl.pallas_call(
+        functools.partial(table_kernel, chips, local),
+        out_shape=jax.ShapeDtypeStruct((2, chips * ROWS, 12 * local), jnp.bfloat16),
+        in_specs=[SMEM, SMEM],
+        out_specs=VMEM,
+        compiler_params=PARAMS,
+        name="table",
+    )(block.reshape(1), freq_ids)
+    lines, start = [], 0
+    for step in PARTS:
+        mine = held[start : start + step]
+        if start:
+            mine, table = lax.optimization_barrier((mine, table))
+        lines.append((mine, lax.ppermute(mine, "block", [(i, i ^ 1) for i in range(groups)])))
+        start += step
+
+    operands, previous = [], None
+    for part, (mine, other) in enumerate(lines):
+        direct, joined = ((chips - 1, 1), (1, chips - 1))[part]
+        if part:
+            other, previous = lax.optimization_barrier((other, previous))
+        shape = (mine.shape[0] // 2, PAIR, P_SIZE)
+        results = pl.pallas_call(
+            share_kernel,
             out_shape=[
-                jax.ShapeDtypeStruct(
-                    (step // 2, PAIR, P_SIZE), jnp.bfloat16 if k else jnp.float32
-                )
+                jax.ShapeDtypeStruct(shape, jnp.float32 if k in (0, joined) else jnp.bfloat16)
                 for k in range(chips)
             ],
             in_specs=[VMEM] * 3,
             out_specs=[VMEM] * chips,
             compiler_params=PARAMS,
-            name="dft",
-        )(mine[i], other[i], table)
-        operands.append(own)
-        for k, send in enumerate(sends, 1):
-            route = [(j, (j + 2 * k) % groups) for j in range(groups)]
-            operands.append(lax.ppermute(send, "block", route))
+            cost_estimate=cost(SHARE_US[part]),
+            name="share",
+        )(mine, other, table)
+        previous = results[0]
+        passing = along(results[2], joined)
+        sent = along(results[direct], direct)
+        if part:
+            passing, operands[1] = lax.optimization_barrier((passing, operands[1]))
+        else:
+            passing, sent = lax.optimization_barrier((passing, sent))
+        total = pl.pallas_call(
+            join_kernel,
+            out_shape=jax.ShapeDtypeStruct(shape, jnp.bfloat16),
+            in_specs=[VMEM] * 2,
+            out_specs=VMEM,
+            compiler_params=PARAMS,
+            cost_estimate=cost(JOIN_US),
+            name="join",
+        )(results[joined], passing)
+        operands += [results[0], sent, along(total, joined)]
     return pl.pallas_call(
-        functools.partial(sum_kernel, PARTS),
-        out_shape=jax.ShapeDtypeStruct((held.shape[0], ROWS, P_SIZE), jnp.bfloat16),
+        sum_kernel,
+        out_shape=jax.ShapeDtypeStruct((owners, ROWS, P_SIZE), jnp.bfloat16),
         in_specs=[VMEM] * len(operands),
         out_specs=VMEM,
         compiler_params=PARAMS,

time: 105 us -> 96.8 us (0.922)
  local copies, waits for them, and re-layouts: 7.83 us -> 4.09 us
  waiting for transfers between devices: 43.2 us -> 39.6 us
  Pallas kernels: 10.6 us -> 8.65 us
  starting transfers between devices: 23.5 us -> 24.8 us
    broadcast_in_dim x5 -> x0, local copies, waits for them, and re-layouts: 2.78 us -> none  [the longest x4 2.73 us: shares(): jnp.where(row // nq == line, table, 0).reshape(chips, 6 * nq, 12 * local)]
    all_to_all x1, waiting for transfers between devices: 19.4 us -> 17.2 us  [per_device(): lax.all_to_all(velocity, 'space', split_axis=0, concat_axis=0, tiled=True)]
    pallas_call x3 -> x6, Pallas kernels: 8.28 us -> 6.31 us  [the longest x2 4.1 us: shares(): pl.pallas_call(share_kernel, out_shape=[jax.ShapeDtypeStruct(shape, jnp.f...]
    ppermute x8, waiting for transfers between devices: 20.7 us -> 19.2 us  [the longest x6 17.3 us: along(): return lax.ppermute(value, 'block', route)]
    ppermute x8, starting transfers between devices: 8.36 us -> 9.65 us  [the longest x6 8.99 us: along(): return lax.ppermute(value, 'block', route)]
  transfers between devices with their start and end apart: 11 -> 11, of which waited for: 6 -> 7; matrix products, arithmetic and copies ran while one was open for 5% -> 1% of each run, Pallas kernels for 6% -> 5%
where the time goes in v3:
time: 96.8 us; the launch traced here: 95.1 us
  waiting for transfers between devices  39.6 us (41%)
  starting transfers between devices  24.8 us (26%)
  blocking collectives  16.6 us (17%)
  Pallas kernels  8.65 us (9%)
  local copies, waits for them, and re-layouts  4.09 us (4%)
    ppermute x6, waiting for transfers between devices, along(): return lax.ppermute(value, 'block', route)  17.3 us
    all_to_all x1, waiting for transfers between devices, per_device(): lax.all_to_all(velocity, 'space', split_axis=0, concat_axis=0, tiled=True)  17.2 us
    all_to_all x1, blocking collectives, per_device(): lax.all_to_all(gram, 'space', split_axis=0, concat_axis=0, tiled=True)  16.6 us
    all_to_all x1, starting transfers between devices, per_device(): lax.all_to_all(velocity, 'space', split_axis=0, concat_axis=0, tiled=True)  9.75 us
    ppermute x6, starting transfers between devices, along(): return lax.ppermute(value, 'block', route)  8.99 us
    pallas_call x2, Pallas kernels, shares(): pl.pallas_call(share_kernel, out_shape=[jax.ShapeDtypeStruct(shape, jnp.f...  4.1 us
    ppermute x1, waiting for transfers between devices, per_device(): low = lax.ppermute(low, 'space', forward)  3.12 us
    ppermute x1, starting transfers between devices, per_device(): high = lax.ppermute(high, 'space', backward)  3.04 us
  transfers between devices with their start and end apart: 11, of which 7 were waited for; matrix products, arithmetic and copies ran while one was open for 1% of the time, Pallas kernels for 5%

profile of v3, /device:TPU:6, one launch (start us, length us, event | category | flops | bytes accessed | tf_op | source)
XLA Modules:
  0.0 95.1 jit_solution(1699750807527479889)
XLA Ops:
  0.7 2.2 %fusion.7 = (bf16[16,2,3,32,256]{4,3,2,1,0:T(8,128)(2,1)S(1)}, bf16[16,2,3,32,256]{4,3,2,1,0:T(8,128)(2,1)S(1)}) fusion(bf16[32,2,3,32,256]{4,3,2,1,0:T(8,128)(2,1)} %bitcast.10), kind=kLoop, calls=%fused_computation.18 | loop fusion | bytes 6291456 | tf_op jit(solution)/shard_map/slice | solution.py:244
  2.9 0.1 collective-permute-start
  3.0 1.0 %table.1.table_ref = bf16[2,160,384]{2,1,0:T(8,128)(2,1)S(1)} custom-call(s32[1]{0:T(128)} %bitcast.6.block_ref, s32[24]{0:T(128)S(1)} %copy-done.7), custom_call_target="tpu_custom_call" | custom-call | tf_op jit(solution)/shard_map/table/pallas_call | solution.py:234
  4.0 0.6 collective-permute-start.1
  4.6 2.0 %collective-permute-done.other_ref = bf16[16,2,3,32,256]{4,3,2,1,0:T(8,128)(2,1)} collective-permute-done((bf16[16,2,3,32,256]{4,3,2,1,0:T(8,128)(2,1)S(1)}, bf16[16,2,3,32,256]{4,3,2,1,0:T(8,128)(2,1)}, u32[]{:S(2)}, u32[]{:S(2)}) %collective-permute-start) | collective-permute-done | bytes 1572896 | tf_op jit(solution)/shard_map/ppermute | solution.py:247
  6.5 2.8 %share.2 = (f32[8,72,256]{2,1,0:T(8,128)S(1)}, f32[8,72,256]{2,1,0:T(8,128)S(1)}, bf16[8,72,256]{2,1,0:T(8,128)(2,1)S(1)}, bf16[8,72,256]{2,1,0:T(8,128)(2,1)S(1)}) custom-call(bf16[16,2,3,32,256]{4,3,2,1,0:T(8,128)(2,1)S(1)} %get-tuple-element.47.mine_ref, bf16[16,2,3,32,256]{4,3,2,1,0:T(8,128)(2,1)} %collective-permute-done.other_ref, ...), custom_call_target="tpu_custom_call" | custom-call | flops 20000000000 | tf_op jit(solution)/shard_map/share/pallas_call | solution.py:256
  9.3 0.8 copy-done.2
  10.1 2.2 %collective-permute-start.3 = (bf16[8,72,256]{2,1,0:T(8,128)(2,1)S(1)}, bf16[8,72,256]{2,1,0:T(8,128)(2,1)S(1)}, u32[]{:S(2)}, u32[]{:S(2)}) collective-permute-start(bf16[8,72,256]{2,1,0:T(8,128)(2,1)S(1)} %get-tuple-element.27), channel_id=1, source_target_pairs={{0,64},{32,96},{64,128},{96,160},{128,192},{160,224},{192,0},{224,... | collective-permute-start | bytes 884744 | tf_op jit(solution)/shard_map/ppermute | solution.py:232
  12.3 1.3 %share.3 = (f32[8,72,256]{2,1,0:T(8,128)S(1)}, bf16[8,72,256]{2,1,0:T(8,128)(2,1)S(1)}, bf16[8,72,256]{2,1,0:T(8,128)(2,1)S(1)}, f32[8,72,256]{2,1,0:T(8,128)S(1)}) custom-call(bf16[16,2,3,32,256]{4,3,2,1,0:T(8,128)(2,1)S(1)} %get-tuple-element.24.mine_ref, bf16[16,2,3,32,256]{4,3,2,1,0:T(8,128)(2,1)S(1)} %collective-permute-done.1.other_ref, ...), custom_call_target="tpu_custom_call" | custom-call | flops 1000000000 | tf_op jit(solution)/shard_map/share/pallas_call | solution.py:256
  13.7 0.7 collective-permute-start.2
  14.4 2.7 %collective-permute-start.6 = (bf16[8,72,256]{2,1,0:T(8,128)(2,1)S(1)}, bf16[8,72,256]{2,1,0:T(8,128)(2,1)S(1)}, u32[]{:S(2)}, u32[]{:S(2)}) collective-permute-start(bf16[8,72,256]{2,1,0:T(8,128)(2,1)S(1)} %get-tuple-element.34), channel_id=1, source_target_pairs={{0,64},{32,96},{64,128},{96,160},{128,192},{160,224},{192,0},{224,... | collective-permute-start | bytes 884744 | tf_op jit(solution)/shard_map/ppermute | solution.py:232
  17.1 2.9 %collective-permute-done.3.passing_ref = bf16[8,72,256]{2,1,0:T(8,128)(2,1)S(1)} collective-permute-done((bf16[8,72,256]{2,1,0:T(8,128)(2,1)S(1)}, bf16[8,72,256]{2,1,0:T(8,128)(2,1)S(1)}, u32[]{:S(2)}, u32[]{:S(2)}) %collective-permute-start.3) | collective-permute-done | bytes 294944 | tf_op jit(solution)/shard_map/ppermute | solution.py:232
  20.0 3.5 %collective-permute-done.4.refs_1_ = bf16[8,72,256]{2,1,0:T(8,128)(2,1)S(1)} collective-permute-done((bf16[8,72,256]{2,1,0:T(8,128)(2,1)S(1)}, bf16[8,72,256]{2,1,0:T(8,128)(2,1)S(1)}, u32[]{:S(2)}, u32[]{:S(2)}) %collective-permute-start.4) | collective-permute-done | bytes 294944 | tf_op jit(solution)/shard_map/ppermute | solution.py:232
  23.4 5.2 %collective-permute-done.2.passing_ref = bf16[8,72,256]{2,1,0:T(8,128)(2,1)S(1)} collective-permute-done((bf16[8,72,256]{2,1,0:T(8,128)(2,1)S(1)}, bf16[8,72,256]{2,1,0:T(8,128)(2,1)S(1)}, u32[]{:S(2)}, u32[]{:S(2)}) %collective-permute-start.2) | collective-permute-done | bytes 294944 | tf_op jit(solution)/shard_map/ppermute | solution.py:232
  28.7 0.1 collective-permute-start.7
  28.9 3.3 %collective-permute-start.5 = (bf16[8,72,256]{2,1,0:T(8,128)(2,1)S(1)}, bf16[8,72,256]{2,1,0:T(8,128)(2,1)S(1)}, u32[]{:S(2)}, u32[]{:S(2)}) collective-permute-start(bf16[8,72,256]{2,1,0:T(8,128)(2,1)S(1)} %join.2), channel_id=1, source_target_pairs={{0,64},{32,96},{64,128},{96,160},{128,192},{160,224},{192,0},{224,... | collective-permute-start | bytes 884744 | tf_op jit(solution)/shard_map/ppermute | solution.py:232
  32.2 5.7 %collective-permute-done.7.refs_5_ = bf16[8,72,256]{2,1,0:T(8,128)(2,1)S(1)} collective-permute-done((bf16[8,72,256]{2,1,0:T(8,128)(2,1)S(1)}, bf16[8,72,256]{2,1,0:T(8,128)(2,1)S(1)}, u32[]{:S(2)}, u32[]{:S(2)}) %collective-permute-start.7) | collective-permute-done | bytes 294944 | tf_op jit(solution)/shard_map/ppermute | solution.py:232
  37.9 1.1 %sum.1 = bf16[32,40,256]{2,1,0:T(8,128)(2,1)} custom-call(f32[8,72,256]{2,1,0:T(8,128)S(1)} %copy-done.3, bf16[8,72,256]{2,1,0:T(8,128)(2,1)S(1)} %collective-permute-done.4.refs_1_, bf16[8,72,256]{2,1,0:T(8,128)(2,1)S(1)} %collective-permute-done.5.refs_2_, f32[8,72,256]{2,1,0:T(8,128)S(1)} %get-tuple-element.33.refs_3_, ...), custom_call_target="tpu_custom_call" | custom-call | tf_op jit(solution)/shard_map/sum/pallas_call | solution.py:285
  39.0 9.8 %all-to-all-start = ((bf16[32,40,256]{2,1,0:T(8,128)(2,1)}), bf16[32,40,256]{2,1,0:T(8,128)(2,1)S(1)}, u32[]{:S(2)}, u32[]{:S(2)}) async-start(bf16[32,40,256]{2,1,0:T(8,128)(2,1)} %sum.1), calls=%async_computation | async-start | bytes 1310720 | tf_op jit(solution)/shard_map/all_to_all | solution.py:312
  48.8 0.1 constant_dynamic-slice_fusion
  48.9 0.1 copy.11
  49.1 0.1 select_n.65
  49.2 0.4 fusion.place_ref
  49.7 17.2 %all-to-all-done.held_ref = bf16[32,40,256]{2,1,0:T(8,128)(2,1)S(1)} async-done(((bf16[32,40,256]{2,1,0:T(8,128)(2,1)}), bf16[32,40,256]{2,1,0:T(8,128)(2,1)S(1)}, u32[]{:S(2)}, u32[]{:S(2)}) %all-to-all-start) | async-done | bytes 655392 | tf_op jit(solution)/shard_map/all_to_all | solution.py:312
  66.9 0.5 place.1
  67.4 2.4 %collective-permute-start.8 = (bf16[6,3,2,8,256]{4,3,2,1,0:T(8,128)(2,1)S(1)}, bf16[6,3,2,8,256]{4,3,2,1,0:T(8,128)(2,1)S(1)}, u32[]{:S(2)}, u32[]{:S(2)}) collective-permute-start(bf16[6,3,2,8,256]{4,3,2,1,0:T(8,128)(2,1)S(1)} %get-tuple-element.38), channel_id=1, source_target_pairs={{0,1},{1,2},{2,3},{3,4},{4,5},{5,6},{6,7},{7,8},{8,9},{9,10},{10,1... | collective-permute-start | bytes 442376 | tf_op jit(solution)/shard_map/ppermute | solution.py:329
  69.8 3.0 %collective-permute-start.9 = (bf16[6,3,2,8,256]{4,3,2,1,0:T(8,128)(2,1)S(1)}, bf16[6,3,2,8,256]{4,3,2,1,0:T(8,128)(2,1)S(1)}, u32[]{:S(2)}, u32[]{:S(2)}) collective-permute-start(bf16[6,3,2,8,256]{4,3,2,1,0:T(8,128)(2,1)S(1)} %get-tuple-element.39), channel_id=1, source_target_pairs={{1,0},{2,1},{3,2},{4,3},{5,4},{6,5},{7,6},{8,7},{9,8},{10,9},{11,1... | collective-permute-start | bytes 442376 | tf_op jit(solution)/shard_map/ppermute | solution.py:330
  72.9 3.1 %collective-permute-done.8.low_ref = bf16[6,3,2,8,256]{4,3,2,1,0:T(8,128)(2,1)S(1)} collective-permute-done((bf16[6,3,2,8,256]{4,3,2,1,0:T(8,128)(2,1)S(1)}, bf16[6,3,2,8,256]{4,3,2,1,0:T(8,128)(2,1)S(1)}, u32[]{:S(2)}, u32[]{:S(2)}) %collective-permute-start.8) | collective-permute-done | bytes 147488 | tf_op jit(solution)/shard_map/ppermute | solution.py:329
  76.0 1.8 %vorticity.1 = (bf16[3,2,3,4,8,256]{5,4,3,2,1,0:T(8,128)(2,1)}, f32[32,1,128]{2,1,0:T(1,128)S(1)}) custom-call(bf16[6,3,4,8,256]{4,3,2,1,0:T(8,128)(2,1)S(1)} %get-tuple-element.37.own_ref, bf16[6,3,2,8,256]{4,3,2,1,0:T(8,128)(2,1)S(1)} %collective-permute-done.8.low_ref, bf16[6,3,2,8,256]{4,3,2,1,0:T(8,128)(2,1)S(1)} %collective-permute-done.9.high_ref, ...), custom_call_target="tpu_custom_call" | custom-call | tf_op jit(solution)/shard_map/vorticity/pallas_call | solution.py:332
  77.8 16.6 %all_to_all.10 = f32[32,1,128]{2,1,0:T(1,128)S(1)} all-to-all(f32[32,1,128]{2,1,0:T(1,128)S(1)} %get-tuple-element.41), channel_id=1, replica_groups=mesh['block'=8,'space'=32] {'space'}, dimensions={0} | all-to-all | bytes 32768 | tf_op jit(solution)/shard_map/all_to_all | solution.py:344
  94.4 0.1 reshape.89
  94.5 0.6 copy.12
  (27 shorter events, 0.4 us)
Async XLA Ops:
  0.6 48.1 %copy-start = (s32[32,32,2]{1,2,0:T(2,128)S(1)}, s32[32,32,2]{1,2,0:T(2,128)}, u32[]{:S(2)}) copy-start(s32[32,32,2]{1,2,0:T(2,128)} %param.8) | copy-start | bytes 24580
  0.6 2.4 %copy-start.7 = (s32[24]{0:T(128)S(1)}, s32[24]{0:T(128)}, u32[]{:S(2)}) copy-start(s32[24]{0:T(128)} %freq_ref.1) | copy-start | bytes 292
  2.9 3.6 %collective-permute-start = (bf16[16,2,3,32,256]{4,3,2,1,0:T(8,128)(2,1)S(1)}, bf16[16,2,3,32,256]{4,3,2,1,0:T(8,128)(2,1)}, u32[]{:S(2)}, u32[]{:S(2)}) collective-permute-start(bf16[16,2,3,32,256]{4,3,2,1,0:T(8,128)(2,1)S(1)} %get-tuple-element.47.mine_ref), channel_id=1, source_target_pairs={{0,32},{32,0},{64,96},{96,64},{128,160},{160,128},{192,224},{224,1... | collective-permute-start | bytes 4718600 | tf_op jit(solution)/shard_map/ppermute | solution.py:247
  4.0 6.1 %collective-permute-start.1 = (bf16[16,2,3,32,256]{4,3,2,1,0:T(8,128)(2,1)S(1)}, bf16[16,2,3,32,256]{4,3,2,1,0:T(8,128)(2,1)S(1)}, u32[]{:S(2)}, u32[]{:S(2)}) collective-permute-start(bf16[16,2,3,32,256]{4,3,2,1,0:T(8,128)(2,1)S(1)} %get-tuple-element.24.mine_ref), channel_id=1, source_target_pairs={{0,32},{32,0},{64,96},{96,64},{128,160},{160,128},{192,224},{224,1... | collective-permute-start | bytes 4718600 | tf_op jit(solution)/shard_map/ppermute | solution.py:247
  9.3 0.8 copy-start.2
  10.1 9.9 %collective-permute-start.3 = (bf16[8,72,256]{2,1,0:T(8,128)(2,1)S(1)}, bf16[8,72,256]{2,1,0:T(8,128)(2,1)S(1)}, u32[]{:S(2)}, u32[]{:S(2)}) collective-permute-start(bf16[8,72,256]{2,1,0:T(8,128)(2,1)S(1)} %get-tuple-element.27), channel_id=1, source_target_pairs={{0,64},{32,96},{64,128},{96,160},{128,192},{160,224},{192,0},{224,... | collective-permute-start | bytes 884744 | tf_op jit(solution)/shard_map/ppermute | solution.py:232
  12.3 11.1 %collective-permute-start.4 = (bf16[8,72,256]{2,1,0:T(8,128)(2,1)S(1)}, bf16[8,72,256]{2,1,0:T(8,128)(2,1)S(1)}, u32[]{:S(2)}, u32[]{:S(2)}) collective-permute-start(bf16[8,72,256]{2,1,0:T(8,128)(2,1)S(1)} %get-tuple-element.28), channel_id=1, source_target_pairs={{0,192},{32,224},{64,0},{96,32},{128,64},{160,96},{192,128},{224,1... | collective-permute-start | bytes 884744 | tf_op jit(solution)/shard_map/ppermute | solution.py:232
  13.7 14.9 %collective-permute-start.2 = (bf16[8,72,256]{2,1,0:T(8,128)(2,1)S(1)}, bf16[8,72,256]{2,1,0:T(8,128)(2,1)S(1)}, u32[]{:S(2)}, u32[]{:S(2)}) collective-permute-start(bf16[8,72,256]{2,1,0:T(8,128)(2,1)S(1)} %get-tuple-element.26), channel_id=1, source_target_pairs={{0,192},{32,224},{64,0},{96,32},{128,64},{160,96},{192,128},{224,1... | collective-permute-start | bytes 884744 | tf_op jit(solution)/shard_map/ppermute | solution.py:232
  14.4 17.8 %collective-permute-start.6 = (bf16[8,72,256]{2,1,0:T(8,128)(2,1)S(1)}, bf16[8,72,256]{2,1,0:T(8,128)(2,1)S(1)}, u32[]{:S(2)}, u32[]{:S(2)}) collective-permute-start(bf16[8,72,256]{2,1,0:T(8,128)(2,1)S(1)} %get-tuple-element.34), channel_id=1, source_target_pairs={{0,64},{32,96},{64,128},{96,160},{128,192},{160,224},{192,0},{224,... | collective-permute-start | bytes 884744 | tf_op jit(solution)/shard_map/ppermute | solution.py:232
  28.7 9.2 %collective-permute-start.7 = (bf16[8,72,256]{2,1,0:T(8,128)(2,1)S(1)}, bf16[8,72,256]{2,1,0:T(8,128)(2,1)S(1)}, u32[]{:S(2)}, u32[]{:S(2)}) collective-permute-start(bf16[8,72,256]{2,1,0:T(8,128)(2,1)S(1)} %join.3), channel_id=1, source_target_pairs={{0,192},{32,224},{64,0},{96,32},{128,64},{160,96},{192,128},{224,1... | collective-permute-start | bytes 884744 | tf_op jit(solution)/shard_map/ppermute | solution.py:232
  28.8 9.1 %copy-start.3 = (f32[8,72,256]{2,1,0:T(8,128)S(1)}, f32[8,72,256]{2,1,0:T(8,128)}, u32[]{:S(2)}) copy-start(f32[8,72,256]{2,1,0:T(8,128)} %copy-done.2) | copy-start | bytes 1769476
  28.9 9.0 %collective-permute-start.5 = (bf16[8,72,256]{2,1,0:T(8,128)(2,1)S(1)}, bf16[8,72,256]{2,1,0:T(8,128)(2,1)S(1)}, u32[]{:S(2)}, u32[]{:S(2)}) collective-permute-start(bf16[8,72,256]{2,1,0:T(8,128)(2,1)S(1)} %join.2), channel_id=1, source_target_pairs={{0,64},{32,96},{64,128},{96,160},{128,192},{160,224},{192,0},{224,... | collective-permute-start | bytes 884744 | tf_op jit(solution)/shard_map/ppermute | solution.py:232
  39.0 27.9 %all-to-all-start = ((bf16[32,40,256]{2,1,0:T(8,128)(2,1)}), bf16[32,40,256]{2,1,0:T(8,128)(2,1)S(1)}, u32[]{:S(2)}, u32[]{:S(2)}) async-start(bf16[32,40,256]{2,1,0:T(8,128)(2,1)} %sum.1), calls=%async_computation | async-start | bytes 1310720 | tf_op jit(solution)/shard_map/all_to_all | solution.py:312
  49.2 26.8 %copy-start.1 = (bf16[3,2,2,3,4,8,256]{6,5,4,3,2,1,0:T(8,128)(2,1)S(1)}, bf16[3,2,2,3,4,8,256]{6,5,4,3,2,1,0:T(8,128)(2,1)}, u32[]{:S(2)}) copy-start(bf16[3,2,2,3,4,8,256]{6,5,4,3,2,1,0:T(8,128)(2,1)} %stored_ref.1) | copy-start | bytes 1769476
  49.2 26.8 %copy-start.4 = (bf16[256,256]{1,0:T(8,128)(2,1)S(1)}, bf16[256,256]{1,0:T(8,128)(2,1)}, u32[]{:S(2)}) copy-start(bf16[256,256]{1,0:T(8,128)(2,1)} %constant.68.clone.line_ref) | copy-start | bytes 393220
  49.2 26.8 %copy-start.5 = (f32[4,4,256]{2,1,0:T(4,128)S(1)}, f32[4,4,256]{2,1,0:T(4,128)}, u32[]{:S(2)}) copy-start(f32[4,4,256]{2,1,0:T(4,128)} %metric_ref.1) | copy-start | bytes 49156
  49.2 26.8 %copy-start.6 = (f32[4,256]{1,0:T(4,128)S(1)}, f32[4,256]{1,0:T(4,128)}, u32[]{:S(2)}) copy-start(f32[4,256]{1,0:T(4,128)} %weight_ref.1) | copy-start | bytes 12292
  67.4 8.5 %collective-permute-start.8 = (bf16[6,3,2,8,256]{4,3,2,1,0:T(8,128)(2,1)S(1)}, bf16[6,3,2,8,256]{4,3,2,1,0:T(8,128)(2,1)S(1)}, u32[]{:S(2)}, u32[]{:S(2)}) collective-permute-start(bf16[6,3,2,8,256]{4,3,2,1,0:T(8,128)(2,1)S(1)} %get-tuple-element.38), channel_id=1, source_target_pairs={{0,1},{1,2},{2,3},{3,4},{4,5},{5,6},{6,7},{7,8},{8,9},{9,10},{10,1... | collective-permute-start | bytes 442376 | tf_op jit(solution)/shard_map/ppermute | solution.py:329
  69.8 6.2 %collective-permute-start.9 = (bf16[6,3,2,8,256]{4,3,2,1,0:T(8,128)(2,1)S(1)}, bf16[6,3,2,8,256]{4,3,2,1,0:T(8,128)(2,1)S(1)}, u32[]{:S(2)}, u32[]{:S(2)}) collective-permute-start(bf16[6,3,2,8,256]{4,3,2,1,0:T(8,128)(2,1)S(1)} %get-tuple-element.39), channel_id=1, source_target_pairs={{1,0},{2,1},{3,2},{4,3},{5,4},{6,5},{7,6},{8,7},{9,8},{10,9},{11,1... | collective-permute-start | bytes 442376 | tf_op jit(solution)/shard_map/ppermute | solution.py:330

commit v4 on v3

--- a/solution.py
+++ b/solution.py
@@ -18,10 +18,12 @@
 ROWS = 40
 PAIR = 72
 PARTS = (16, 16)
-UNROLL = 2
-SHARE_US, JOIN_US = (20, 1), 1
+SHARE_US, JOIN_US, SUM_US = (20, 1), 1, (20, 1)
 VMEM = pl.BlockSpec(memory_space=pltpu.VMEM)
 SMEM = pl.BlockSpec(memory_space=pltpu.SMEM)
+ANY = pl.BlockSpec(memory_space=pl.ANY)
+HBM = pl.BlockSpec(memory_space=pltpu.HBM)
+FETCHES = 4
 PARAMS = pltpu.CompilerParams(vmem_limit_bytes=16 * 1024 * 1024)
 
 
@@ -75,10 +77,12 @@
             table_ref[parity, k * ROWS : (k + 1) * ROWS] = rows
 
 
-def share_kernel(mine_ref, other_ref, table_ref, *out_refs):
+def share_kernel(mine_ref, other_ref, table_ref, *refs):
+    *out_refs, fetched_ref, sems = refs
+
     def share(d, parity):
         lines = jnp.concatenate(
-            [mine_ref[d].reshape(-1, P_SIZE), other_ref[d].reshape(-1, P_SIZE)], axis=0
+            [mine_ref[d].reshape(-1, P_SIZE), fetched_ref[d].reshape(-1, P_SIZE)], axis=0
         )
         return jnp.dot(table_ref[parity], lines, preferred_element_type=jnp.float32)
 
@@ -92,35 +96,46 @@
             ref[pair] = both.astype(ref.dtype)
         return carry
 
-    lax.fori_loop(0, out_refs[0].shape[0], step, 0, unroll=UNROLL)
-
-
-def join_kernel(kept_ref, passing_ref, out_ref):
+    pairs = out_refs[0].shape[0]
+    ends = [pairs * (i + 1) // FETCHES for i in range(FETCHES)]
+    copies = []
+    for i, (start, end) in enumerate(zip([0] + ends, ends)):
+        owners = pl.ds(2 * start, 2 * (end - start))
+        copies.append(
+            pltpu.make_async_copy(other_ref.at[owners], fetched_ref.at[owners], sems.at[i])
+        )
+        copies[-1].start()
+    for copy, start, end in zip(copies, [0] + ends, ends):
+        copy.wait()
+        lax.fori_loop(start, end, step, 0, unroll=2)
+
+
+def join_kernel(kept_ref, passing_ref, *refs):
+    out_ref = refs[-1]
+
     def step(pair, carry):
         total = kept_ref[pair] + passing_ref[pair].astype(jnp.float32)
         out_ref[pair] = total.astype(jnp.bfloat16)
         return carry
 
-    lax.fori_loop(0, out_ref.shape[0], step, 0, unroll=UNROLL)
-
-
-def sum_kernel(*refs):
-    out_ref = refs[-1]
+    lax.fori_loop(0, out_ref.shape[0], step, 0)
+
+
+def sum_kernel(own_ref, sent_ref, joined_ref, *refs):
+    *before_refs, out_ref = refs
     start = 0
-    for part in range(len(refs) // 3):
-        own, *rest = refs[3 * part : 3 * part + 3]
-
-        def step(pair, carry, own=own, rest=rest, start=start):
-            total = own[pair]
-            for ref in rest:
-                total = total + ref[pair].astype(jnp.float32)
-            total = total.astype(jnp.bfloat16)
-            out_ref[start + 2 * pair] = total[:ROWS]
-            out_ref[start + 2 * pair + 1] = total[PAIR - ROWS :]
-            return carry
-
-        lax.fori_loop(0, own.shape[0], step, 0, unroll=UNROLL)
-        start += 2 * own.shape[0]
+    for before_ref in before_refs:
+        start = before_ref.shape[0]
+        out_ref[:start] = before_ref[...]
+
+    def step(pair, carry):
+        total = own_ref[pair] + sent_ref[pair].astype(jnp.float32)
+        total = (total + joined_ref[pair].astype(jnp.float32)).astype(jnp.bfloat16)
+        out_ref[start + 2 * pair] = total[:ROWS]
+        out_ref[start + 2 * pair + 1] = total[PAIR - ROWS :]
+        return carry
+
+    lax.fori_loop(0, own_ref.shape[0], step, 0)
 
 
 def place_kernel(place_ref, held_ref, own_ref, low_ref, high_ref):
@@ -132,79 +147,100 @@
     high_ref[...] = rows[:, :, :2]
 
 
+def add_products(sums_ref, f, a, b, left, right):
+    def put(part, value):
+        total = jnp.sum(value, axis=(0, 1, 2)).reshape(1, P_SIZE)
+        total = total[:, :128] + total[:, 128:]
+        row = ((f * 2 + part) * 3 + a) * 3 + b
+        sums_ref[row : row + 1, :] = total
+        if a != b:
+            row = ((f * 2 + part) * 3 + b) * 3 + a
+            sums_ref[row : row + 1, :] = total if part == 0 else -total
+
+    put(0, left[0] * right[0] + left[1] * right[1])
+    if a != b:
+        put(1, left[0] * right[1] - left[1] * right[0])
+
+
+def column(ref, f, a):
+    return tuple(ref[f, a, r].astype(jnp.float32) for r in range(2))
+
+
+def stored_kernel(weight_ref, stored_ref, sums_ref):
+    sums_ref[...] = jnp.zeros_like(sums_ref)
+    weight = weight_ref[...].reshape(1, JD, 1, P_SIZE)
+    for f in range(stored_ref.shape[0]):
+        columns = [column(stored_ref, f, a) for a in range(2)]
+        for a in range(2):
+            left = tuple(weight * v for v in columns[a])
+            for b in range(a, 2):
+                add_products(sums_ref, f, a + 1, b + 1, left, columns[b])
+
+
+def within_kernel(own_ref, line_ref, metric_ref, base_ref):
+    xi_x, xi_y = (metric_ref[i].reshape(JD, 1, P_SIZE) for i in range(2))
+    twelfth = 1.0 / 12.0
+    for q in range(own_ref.shape[0]):
+        along, span = [], []
+        for c in range(3):
+            line = own_ref[q, c].reshape(LD, P_SIZE)
+            value = jnp.dot(line, line_ref[...], preferred_element_type=jnp.float32)
+            along.append((value * twelfth).reshape(JD, NK, P_SIZE))
+        for c in range(2):
+            center = own_ref[q, c].astype(jnp.float32)
+            value = (
+                pltpu.roll(center, 2, 1)
+                - 8.0 * pltpu.roll(center, 1, 1)
+                + 8.0 * pltpu.roll(center, NK - 1, 1)
+                - pltpu.roll(center, NK - 2, 1)
+            )
+            span.append(value * twelfth)
+        base_ref[q, 0] = xi_y * along[2] - span[1]
+        base_ref[q, 1] = span[0] - xi_x * along[2]
+        base_ref[q, 2] = xi_x * along[1] - xi_y * along[0]
+
+
 def vorticity_kernel(
     scale,
     own_ref,
     low_ref,
     high_ref,
-    line_ref,
+    base_ref,
     metric_ref,
     weight_ref,
     stored_ref,
+    before_ref,
     spectra_ref,
     gram_ref,
     sums_ref,
 ):
-    sums_ref[...] = jnp.zeros_like(sums_ref)
-    nf = stored_ref.shape[0]
-    xi_x, xi_y, eta_x, eta_y = (metric_ref[i].reshape(JD, 1, P_SIZE) for i in range(4))
+    sums_ref[...] = before_ref[...]
+    eta_x, eta_y = (metric_ref[i].reshape(JD, 1, P_SIZE) * (1.0 / 12.0) for i in (2, 3))
     weight = weight_ref[...].reshape(1, JD, 1, P_SIZE)
-    twelfth = 1.0 / 12.0
-
-    for f in range(nf):
+    for f in range(stored_ref.shape[0]):
         new = []
         for r in range(2):
             q = 2 * f + r
-            d_x, d_y, d_z = [], [], []
+            pitch = []
             for c in range(3):
-                line = own_ref[q, c].reshape(LD, P_SIZE)
-                along = jnp.dot(line, line_ref[...], preferred_element_type=jnp.float32)
-                along = (along * twelfth).reshape(JD, NK, P_SIZE)
-                center = own_ref[q, c].astype(jnp.float32)
                 padded = jnp.concatenate(
-                    [
-                        low_ref[q, c].astype(jnp.float32),
-                        center,
-                        high_ref[q, c].astype(jnp.float32),
-                    ],
+                    [ref[q, c].astype(jnp.float32) for ref in (low_ref, own_ref, high_ref)],
                     axis=0,
                 )
-                pitch = (
-                    padded[:-4] - 8.0 * padded[1:-3] + 8.0 * padded[3:-1] - padded[4:]
-                ) * twelfth
-                span = (
-                    pltpu.roll(center, 2, 1)
-                    - 8.0 * pltpu.roll(center, 1, 1)
-                    + 8.0 * pltpu.roll(center, NK - 1, 1)
-                    - pltpu.roll(center, NK - 2, 1)
-                ) * twelfth
-                d_x.append(xi_x * along + eta_x * pitch)
-                d_y.append(xi_y * along + eta_y * pitch)
-                d_z.append(span)
-            vort = [d_y[2] - d_z[1], d_z[0] - d_x[2], d_x[1] - d_y[0]]
+                pitch.append(padded[:-4] - 8.0 * padded[1:-3] + 8.0 * padded[3:-1] - padded[4:])
+            vort = [
+                base_ref[q, 0] + eta_y * pitch[2],
+                base_ref[q, 1] - eta_x * pitch[2],
+                base_ref[q, 2] + eta_x * pitch[1] - eta_y * pitch[0],
+            ]
             vort = [v.astype(jnp.bfloat16) for v in vort]
             for c in range(3):
                 spectra_ref[f, r, c] = vort[c]
             new.append(jnp.stack([v.astype(jnp.float32) for v in vort], axis=0))
-        columns = [tuple(new)] + [
-            tuple(stored_ref[f, a, r].astype(jnp.float32) for r in range(2)) for a in range(2)
-        ]
-
-        def put(part, a, b, value):
-            total = jnp.sum(value, axis=(0, 1, 2)).reshape(1, P_SIZE)
-            total = total[:, :128] + total[:, 128:]
-            row = ((f * 2 + part) * 3 + a) * 3 + b
-            sums_ref[row : row + 1, :] = total
-            if a != b:
-                row = ((f * 2 + part) * 3 + b) * 3 + a
-                sums_ref[row : row + 1, :] = total if part == 0 else -total
-
-        for a in range(3):
-            real, imag = (weight * v for v in columns[a])
-            for b in range(a, 3):
-                put(0, a, b, real * columns[b][0] + imag * columns[b][1])
-                if a != b:
-                    put(1, a, b, real * columns[b][1] - imag * columns[b][0])
+        left = tuple(weight * v for v in new)
+        add_products(sums_ref, f, 0, 0, left, new)
+        for a in range(2):
+            add_products(sums_ref, f, 0, a + 1, left, column(stored_ref, f, a))
 
     total = lax.dot_general(
         jnp.full((8, 128), scale, jnp.float32),
@@ -241,13 +277,13 @@
     )(block.reshape(1), freq_ids)
     lines, start = [], 0
     for step in PARTS:
+        if start:
+            held, table = lax.optimization_barrier((held, table))
         mine = held[start : start + step]
-        if start:
-            mine, table = lax.optimization_barrier((mine, table))
         lines.append((mine, lax.ppermute(mine, "block", [(i, i ^ 1) for i in range(groups)])))
         start += step
 
-    operands, previous = [], None
+    total, previous, passed = None, None, []
     for part, (mine, other) in enumerate(lines):
         direct, joined = ((chips - 1, 1), (1, chips - 1))[part]
         if part:
@@ -259,8 +295,12 @@
                 jax.ShapeDtypeStruct(shape, jnp.float32 if k in (0, joined) else jnp.bfloat16)
                 for k in range(chips)
             ],
-            in_specs=[VMEM] * 3,
+            in_specs=[VMEM, HBM, VMEM],
             out_specs=[VMEM] * chips,
+            scratch_shapes=[
+                pltpu.VMEM(mine.shape, jnp.bfloat16),
+                pltpu.SemaphoreType.DMA((FETCHES,)),
+            ],
             compiler_params=PARAMS,
             cost_estimate=cost(SHARE_US[part]),
             name="share",
@@ -269,27 +309,36 @@
         passing = along(results[2], joined)
         sent = along(results[direct], direct)
         if part:
-            passing, operands[1] = lax.optimization_barrier((passing, operands[1]))
+            earlier = [total]
         else:
-            passing, sent = lax.optimization_barrier((passing, sent))
+            earlier = []
+        passing, sent = lax.optimization_barrier((passing, sent))
         total = pl.pallas_call(
             join_kernel,
             out_shape=jax.ShapeDtypeStruct(shape, jnp.bfloat16),
-            in_specs=[VMEM] * 2,
+            in_specs=[VMEM] * 2 + [ANY] * len(earlier),
             out_specs=VMEM,
             compiler_params=PARAMS,
             cost_estimate=cost(JOIN_US),
             name="join",
-        )(results[joined], passing)
-        operands += [results[0], sent, along(total, joined)]
-    return pl.pallas_call(
-        sum_kernel,
-        out_shape=jax.ShapeDtypeStruct((owners, ROWS, P_SIZE), jnp.bfloat16),
-        in_specs=[VMEM] * len(operands),
-        out_specs=VMEM,
-        compiler_params=PARAMS,
-        name="sum",
-    )(*operands)
+        )(results[joined], passing, *earlier)
+        passed.append((results[0], sent, along(total, joined)))
+    velocity = []
+    for part, operands in enumerate(passed):
+        velocity = [
+            pl.pallas_call(
+                sum_kernel,
+                out_shape=jax.ShapeDtypeStruct(
+                    (sum(PARTS[: part + 1]), ROWS, P_SIZE), jnp.bfloat16
+                ),
+                in_specs=[VMEM] * (3 + part),
+                out_specs=VMEM,
+                compiler_params=PARAMS,
+                cost_estimate=cost(SUM_US[part]),
+                name="sum",
+            )(*operands, *velocity)
+        ]
+    return velocity[0]
 
 
 def placing(slot_line):
@@ -328,6 +377,24 @@
     backward = [(target, source) for source, target in forward]
     low = lax.ppermute(low, "space", forward)
     high = lax.ppermute(high, "space", backward)
+    base = pl.pallas_call(
+        within_kernel,
+        out_shape=jax.ShapeDtypeStruct((2 * nf, 3, JD, NK, P_SIZE), jnp.float32),
+        in_specs=[VMEM] * 3,
+        out_specs=VMEM,
+        compiler_params=PARAMS,
+        cost_estimate=cost(5),
+        name="within",
+    )(own, line_matrix(), metrics)
+    before = pl.pallas_call(
+        stored_kernel,
+        out_shape=jax.ShapeDtypeStruct((128, 128), jnp.float32),
+        in_specs=[VMEM] * 2,
+        out_specs=VMEM,
+        compiler_params=PARAMS,
+        cost_estimate=cost(1),
+        name="stored",
+    )(weights, stored_spectra)
 
     spectra, gram = pl.pallas_call(
         functools.partial(vorticity_kernel, 1.0 / (3.0 * JD * holders * NK * P_SIZE)),
@@ -335,12 +402,12 @@
             jax.ShapeDtypeStruct((nf, 2, 3, JD, NK, P_SIZE), jnp.bfloat16),
             jax.ShapeDtypeStruct((holders, 1, 128), jnp.float32),
         ],
-        in_specs=[VMEM] * 7,
+        in_specs=[VMEM] * 8,
         out_specs=[VMEM, VMEM],
         scratch_shapes=[pltpu.VMEM((128, 128), jnp.float32)],
         compiler_params=PARAMS,
         name="vorticity",
-    )(own, low, high, line_matrix(), metrics, weights, stored_spectra)
+    )(own, low, high, base, metrics, weights, stored_spectra, before)
     gram = lax.all_to_all(gram, "space", split_axis=0, concat_axis=0, tiled=True)
     gram = jnp.sum(gram, axis=(0, 1))[: nf * 18].reshape(nf, 2, 3, 3)
     return (spectra, gram)

time: 96.8 us -> 92.7 us (0.958); the launches traced: 95.1 us -> 92.4 us
  starting transfers between devices: 24.8 us -> 21.7 us
    ppermute x6, starting transfers between devices: 8.99 us -> 5.86 us  [along(): return lax.ppermute(value, 'block', route)]
    ppermute x6, waiting for transfers between devices: 17.3 us -> 19.3 us  [along(): return lax.ppermute(value, 'block', route)]
    ppermute x2, waiting for transfers between devices: 1.96 us -> 0.27 us  [shares(): lax.ppermute(mine, 'block', [(i, i ^ 1) for i in range(groups)])]
    pallas_call x1 -> x4, Pallas kernels: 1.09 us -> 2 us  [the longest x2 1.15 us: shares(): pl.pallas_call(sum_kernel, out_shape=jax.ShapeDtypeStruct((sum(PARTS[:par...]
    slice x1 -> x2, local copies, waits for them, and re-layouts: 2.24 us -> 3.12 us  [shares(): mine = held[start:start + step]]
  transfers between devices with their start and end apart: 11 -> 11, of which waited for: 7 -> 8; matrix products, arithmetic and copies ran while one was open for 1% -> 3% of each run, Pallas kernels for 5% -> 7%
where the time goes in v4:
time: 92.7 us; the launch traced here: 92.4 us
  waiting for transfers between devices  39.3 us (42%)
  starting transfers between devices  21.7 us (23%)
  blocking collectives  16.6 us (18%)
  Pallas kernels  9.24 us (10%)
  local copies, waits for them, and re-layouts  4.14 us (4%)
    ppermute x6, waiting for transfers between devices, along(): return lax.ppermute(value, 'block', route)  19.3 us
    all_to_all x1, waiting for transfers between devices, per_device(): lax.all_to_all(velocity, 'space', split_axis=0, concat_axis=0, tiled=True)  17.1 us
    all_to_all x1, blocking collectives, per_device(): lax.all_to_all(gram, 'space', split_axis=0, concat_axis=0, tiled=True)  16.6 us
    all_to_all x1, starting transfers between devices, per_device(): lax.all_to_all(velocity, 'space', split_axis=0, concat_axis=0, tiled=True)  9.77 us
    ppermute x6, starting transfers between devices, along(): return lax.ppermute(value, 'block', route)  5.86 us
    pallas_call x2, Pallas kernels, shares(): pl.pallas_call(share_kernel, out_shape=[jax.ShapeDtypeStruct(shape, jnp.f...  4.25 us
    slice x2, local copies, waits for them, and re-layouts, shares(): mine = held[start:start + step]  3.12 us
    ppermute x1, starting transfers between devices, per_device(): high = lax.ppermute(high, 'space', backward)  3.02 us
  transfers between devices with their start and end apart: 11, of which 8 were waited for; matrix products, arithmetic and copies ran while one was open for 3% of the time, Pallas kernels for 7%

profile of v4, /device:TPU:6, one launch (start us, length us, event | category | flops | bytes accessed | tf_op | source)
XLA Modules:
  0.0 92.4 jit_solution(2788882412602548210)
XLA Ops:
  0.7 1.6 %slice.20.mine_ref = bf16[16,2,3,32,256]{4,3,2,1,0:T(8,128)(2,1)S(1)} slice(bf16[32,2,3,32,256]{4,3,2,1,0:T(8,128)(2,1)} %bitcast.10), slice={[0:16], [0:2], [0:3], [0:32], [0:256]} | slice | bytes 3145728 | tf_op jit(solution)/shard_map/slice | solution.py:282
  2.2 0.1 collective-permute-start.1
  2.3 1.0 %table.1.table_ref = bf16[2,160,384]{2,1,0:T(8,128)(2,1)S(1)} custom-call(s32[1]{0:T(128)} %bitcast.5.block_ref, s32[24]{0:T(128)S(1)} %copy-done.4), custom_call_target="tpu_custom_call" | custom-call | tf_op jit(solution)/shard_map/table/pallas_call | solution.py:270
  3.3 1.6 %slice.17.mine_ref = bf16[16,2,3,32,256]{4,3,2,1,0:T(8,128)(2,1)S(1)} slice(bf16[32,2,3,32,256]{4,3,2,1,0:T(8,128)(2,1)} %bitcast.11), slice={[16:32], [0:2], [0:3], [0:32], [0:256]} | slice | bytes 3145728 | tf_op jit(solution)/shard_map/slice | solution.py:282
  4.9 0.6 collective-permute-start
  5.5 0.3 collective-permute-done.1.other_ref
  5.7 2.1 %share.2 = (f32[8,72,256]{2,1,0:T(8,128)S(1)}, f32[8,72,256]{2,1,0:T(8,128)S(1)}, bf16[8,72,256]{2,1,0:T(8,128)(2,1)S(1)}, bf16[8,72,256]{2,1,0:T(8,128)(2,1)S(1)}) custom-call(bf16[16,2,3,32,256]{4,3,2,1,0:T(8,128)(2,1)S(1)} %slice.20.mine_ref, bf16[16,2,3,32,256]{4,3,2,1,0:T(8,128)(2,1)S(1)} %collective-permute-done.1.other_ref, ...), custom_call_target="tpu_custom_call" | custom-call | flops 20000000000 | tf_op jit(solution)/shard_map/share/pallas_call | solution.py:292
  7.9 2.3 %collective-permute-start.4 = (bf16[8,72,256]{2,1,0:T(8,128)(2,1)S(1)}, bf16[8,72,256]{2,1,0:T(8,128)(2,1)S(1)}, u32[]{:S(2)}, u32[]{:S(2)}) collective-permute-start(bf16[8,72,256]{2,1,0:T(8,128)(2,1)S(1)} %get-tuple-element.33), channel_id=1, source_target_pairs={{0,64},{32,96},{64,128},{96,160},{128,192},{160,224},{192,0},{224,... | collective-permute-start | bytes 884744 | tf_op jit(solution)/shard_map/ppermute | solution.py:268
  10.2 2.1 %share.3 = (f32[8,72,256]{2,1,0:T(8,128)S(1)}, bf16[8,72,256]{2,1,0:T(8,128)(2,1)S(1)}, bf16[8,72,256]{2,1,0:T(8,128)(2,1)S(1)}, f32[8,72,256]{2,1,0:T(8,128)S(1)}) custom-call(bf16[16,2,3,32,256]{4,3,2,1,0:T(8,128)(2,1)S(1)} %slice.17.mine_ref, bf16[16,2,3,32,256]{4,3,2,1,0:T(8,128)(2,1)S(1)} %collective-permute-done.other_ref, ...), custom_call_target="tpu_custom_call" | custom-call | flops 1000000000 | tf_op jit(solution)/shard_map/share/pallas_call | solution.py:292
  12.3 0.7 collective-permute-start.2
  13.0 2.7 %collective-permute-start.3 = (bf16[8,72,256]{2,1,0:T(8,128)(2,1)S(1)}, bf16[8,72,256]{2,1,0:T(8,128)(2,1)S(1)}, u32[]{:S(2)}, u32[]{:S(2)}) collective-permute-start(bf16[8,72,256]{2,1,0:T(8,128)(2,1)S(1)} %get-tuple-element.28), channel_id=1, source_target_pairs={{0,64},{32,96},{64,128},{96,160},{128,192},{160,224},{192,0},{224,... | collective-permute-start | bytes 884744 | tf_op jit(solution)/shard_map/ppermute | solution.py:268
  15.7 2.1 %collective-permute-done.4.passing_ref = bf16[8,72,256]{2,1,0:T(8,128)(2,1)S(1)} collective-permute-done((bf16[8,72,256]{2,1,0:T(8,128)(2,1)S(1)}, bf16[8,72,256]{2,1,0:T(8,128)(2,1)S(1)}, u32[]{:S(2)}, u32[]{:S(2)}) %collective-permute-start.4) | collective-permute-done | bytes 294944 | tf_op jit(solution)/shard_map/ppermute | solution.py:268
  17.8 3.5 %collective-permute-done.5.sent_ref = bf16[8,72,256]{2,1,0:T(8,128)(2,1)S(1)} collective-permute-done((bf16[8,72,256]{2,1,0:T(8,128)(2,1)S(1)}, bf16[8,72,256]{2,1,0:T(8,128)(2,1)S(1)}, u32[]{:S(2)}, u32[]{:S(2)}) %collective-permute-start.5) | collective-permute-done | bytes 294944 | tf_op jit(solution)/shard_map/ppermute | solution.py:268
  21.5 0.1 constant_dynamic-slice_fusion
  21.7 4.8 %collective-permute-done.2.passing_ref = bf16[8,72,256]{2,1,0:T(8,128)(2,1)S(1)} collective-permute-done((bf16[8,72,256]{2,1,0:T(8,128)(2,1)S(1)}, bf16[8,72,256]{2,1,0:T(8,128)(2,1)S(1)}, u32[]{:S(2)}, u32[]{:S(2)}) %collective-permute-start.2) | collective-permute-done | bytes 294944 | tf_op jit(solution)/shard_map/ppermute | solution.py:268
  26.6 3.0 %collective-permute-done.7.joined_ref = bf16[8,72,256]{2,1,0:T(8,128)(2,1)S(1)} collective-permute-done((bf16[8,72,256]{2,1,0:T(8,128)(2,1)S(1)}, bf16[8,72,256]{2,1,0:T(8,128)(2,1)S(1)}, u32[]{:S(2)}, u32[]{:S(2)}) %collective-permute-start.7) | collective-permute-done | bytes 294944 | tf_op jit(solution)/shard_map/ppermute | solution.py:268
  29.6 0.1 sum.2.refs_0_
  29.8 6.0 %collective-permute-done.6.joined_ref = bf16[8,72,256]{2,1,0:T(8,128)(2,1)S(1)} collective-permute-done((bf16[8,72,256]{2,1,0:T(8,128)(2,1)S(1)}, bf16[8,72,256]{2,1,0:T(8,128)(2,1)S(1)}, u32[]{:S(2)}, u32[]{:S(2)}) %collective-permute-start.6) | collective-permute-done | bytes 294944 | tf_op jit(solution)/shard_map/ppermute | solution.py:268
  35.7 1.0 %sum.3 = bf16[32,40,256]{2,1,0:T(8,128)(2,1)} custom-call(f32[8,72,256]{2,1,0:T(8,128)S(1)} %get-tuple-element.26.own_ref, bf16[8,72,256]{2,1,0:T(8,128)(2,1)S(1)} %collective-permute-done.3.sent_ref, bf16[8,72,256]{2,1,0:T(8,128)(2,1)S(1)} %collective-permute-done.6.joined_ref, bf16[16,40,256]{2,1,0:T(8,128)(2,1)S(1)} %sum.2.refs_0_), custom_call_target="tpu_custom_call" | custom-call | flops 1000000000 | tf_op jit(solution)/shard_map/sum/pallas_call | solution.py:329
  36.8 9.8 %all-to-all-start = ((bf16[32,40,256]{2,1,0:T(8,128)(2,1)}), bf16[32,40,256]{2,1,0:T(8,128)(2,1)S(1)}, u32[]{:S(2)}, u32[]{:S(2)}) async-start(bf16[32,40,256]{2,1,0:T(8,128)(2,1)} %sum.3), calls=%async_computation | async-start | bytes 1310720 | tf_op jit(solution)/shard_map/all_to_all | solution.py:361
  46.8 0.3 stored.1.before_ref
  47.1 0.4 fusion.place_ref
  47.6 17.1 %all-to-all-done.held_ref = bf16[32,40,256]{2,1,0:T(8,128)(2,1)S(1)} async-done(((bf16[32,40,256]{2,1,0:T(8,128)(2,1)}), bf16[32,40,256]{2,1,0:T(8,128)(2,1)S(1)}, u32[]{:S(2)}, u32[]{:S(2)}) %all-to-all-start) | async-done | bytes 655392 | tf_op jit(solution)/shard_map/all_to_all | solution.py:361
  64.7 0.5 place.1
  65.2 2.4 %collective-permute-start.8 = (bf16[6,3,2,8,256]{4,3,2,1,0:T(8,128)(2,1)S(1)}, bf16[6,3,2,8,256]{4,3,2,1,0:T(8,128)(2,1)S(1)}, u32[]{:S(2)}, u32[]{:S(2)}) collective-permute-start(bf16[6,3,2,8,256]{4,3,2,1,0:T(8,128)(2,1)S(1)} %get-tuple-element.38), channel_id=1, source_target_pairs={{0,1},{1,2},{2,3},{3,4},{4,5},{5,6},{6,7},{7,8},{8,9},{9,10},{10,1... | collective-permute-start | bytes 442376 | tf_op jit(solution)/shard_map/ppermute | solution.py:378
  67.6 3.0 %collective-permute-start.9 = (bf16[6,3,2,8,256]{4,3,2,1,0:T(8,128)(2,1)S(1)}, bf16[6,3,2,8,256]{4,3,2,1,0:T(8,128)(2,1)S(1)}, u32[]{:S(2)}, u32[]{:S(2)}) collective-permute-start(bf16[6,3,2,8,256]{4,3,2,1,0:T(8,128)(2,1)S(1)} %get-tuple-element.39), channel_id=1, source_target_pairs={{1,0},{2,1},{3,2},{4,3},{5,4},{6,5},{7,6},{8,7},{9,8},{10,9},{11,1... | collective-permute-start | bytes 442376 | tf_op jit(solution)/shard_map/ppermute | solution.py:379
  70.7 0.5 within.1.base_ref
  71.2 2.6 %collective-permute-done.8.low_ref = bf16[6,3,2,8,256]{4,3,2,1,0:T(8,128)(2,1)S(1)} collective-permute-done((bf16[6,3,2,8,256]{4,3,2,1,0:T(8,128)(2,1)S(1)}, bf16[6,3,2,8,256]{4,3,2,1,0:T(8,128)(2,1)S(1)}, u32[]{:S(2)}, u32[]{:S(2)}) %collective-permute-start.8) | collective-permute-done | bytes 147488 | tf_op jit(solution)/shard_map/ppermute | solution.py:378
  73.8 1.3 %vorticity.1 = (bf16[3,2,3,4,8,256]{5,4,3,2,1,0:T(8,128)(2,1)}, f32[32,1,128]{2,1,0:T(1,128)S(1)}) custom-call(bf16[6,3,4,8,256]{4,3,2,1,0:T(8,128)(2,1)S(1)} %get-tuple-element.37.own_ref, bf16[6,3,2,8,256]{4,3,2,1,0:T(8,128)(2,1)S(1)} %collective-permute-done.8.low_ref, bf16[6,3,2,8,256]{4,3,2,1,0:T(8,128)(2,1)S(1)} %collective-permute-done.9.high_ref, ...), custom_call_target="tpu_custom_call" | custom-call | tf_op jit(solution)/shard_map/vorticity/pallas_call | solution.py:399
  75.1 16.6 %all_to_all.10 = f32[32,1,128]{2,1,0:T(1,128)S(1)} all-to-all(f32[32,1,128]{2,1,0:T(1,128)S(1)} %get-tuple-element.41), channel_id=1, replica_groups=mesh['block'=8,'space'=32] {'space'}, dimensions={0} | all-to-all | bytes 32768 | tf_op jit(solution)/shard_map/all_to_all | solution.py:411
  91.7 0.1 reshape.89
  91.8 0.6 copy.12
  (31 shorter events, 0.7 us)
Async XLA Ops:
  0.6 20.8 %copy-start = (s32[32,32,2]{1,2,0:T(2,128)S(1)}, s32[32,32,2]{1,2,0:T(2,128)}, u32[]{:S(2)}) copy-start(s32[32,32,2]{1,2,0:T(2,128)} %param.8) | copy-start | bytes 24580
  0.6 1.7 %copy-start.4 = (s32[24]{0:T(128)S(1)}, s32[24]{0:T(128)}, u32[]{:S(2)}) copy-start(s32[24]{0:T(128)} %freq_ref.1) | copy-start | bytes 292
  2.2 3.5 %collective-permute-start.1 = (bf16[16,2,3,32,256]{4,3,2,1,0:T(8,128)(2,1)S(1)}, bf16[16,2,3,32,256]{4,3,2,1,0:T(8,128)(2,1)S(1)}, u32[]{:S(2)}, u32[]{:S(2)}) collective-permute-start(bf16[16,2,3,32,256]{4,3,2,1,0:T(8,128)(2,1)S(1)} %slice.20.mine_ref), channel_id=1, source_target_pairs={{0,32},{32,0},{64,96},{96,64},{128,160},{160,128},{192,224},{224,1... | collective-permute-start | bytes 4718600 | tf_op jit(solution)/shard_map/ppermute | solution.py:283
  4.9 5.3 %collective-permute-start = (bf16[16,2,3,32,256]{4,3,2,1,0:T(8,128)(2,1)S(1)}, bf16[16,2,3,32,256]{4,3,2,1,0:T(8,128)(2,1)S(1)}, u32[]{:S(2)}, u32[]{:S(2)}) collective-permute-start(bf16[16,2,3,32,256]{4,3,2,1,0:T(8,128)(2,1)S(1)} %slice.17.mine_ref), channel_id=1, source_target_pairs={{0,32},{32,0},{64,96},{96,64},{128,160},{160,128},{192,224},{224,1... | collective-permute-start | bytes 4718600 | tf_op jit(solution)/shard_map/ppermute | solution.py:283
  7.9 4.4 %copy-start.6 = (f32[8,72,256]{2,1,0:T(8,128)}, f32[8,72,256]{2,1,0:T(8,128)S(1)}, u32[]{:S(2)}) copy-start(f32[8,72,256]{2,1,0:T(8,128)S(1)} %get-tuple-element.24.own_ref) | copy-start | bytes 1769476
  7.9 9.9 %collective-permute-start.4 = (bf16[8,72,256]{2,1,0:T(8,128)(2,1)S(1)}, bf16[8,72,256]{2,1,0:T(8,128)(2,1)S(1)}, u32[]{:S(2)}, u32[]{:S(2)}) collective-permute-start(bf16[8,72,256]{2,1,0:T(8,128)(2,1)S(1)} %get-tuple-element.33), channel_id=1, source_target_pairs={{0,64},{32,96},{64,128},{96,160},{128,192},{160,224},{192,0},{224,... | collective-permute-start | bytes 884744 | tf_op jit(solution)/shard_map/ppermute | solution.py:268
  10.2 11.1 %collective-permute-start.5 = (bf16[8,72,256]{2,1,0:T(8,128)(2,1)S(1)}, bf16[8,72,256]{2,1,0:T(8,128)(2,1)S(1)}, u32[]{:S(2)}, u32[]{:S(2)}) collective-permute-start(bf16[8,72,256]{2,1,0:T(8,128)(2,1)S(1)} %get-tuple-element.34), channel_id=1, source_target_pairs={{0,192},{32,224},{64,0},{96,32},{128,64},{160,96},{192,128},{224,1... | collective-permute-start | bytes 884744 | tf_op jit(solution)/shard_map/ppermute | solution.py:268
  12.3 14.2 %collective-permute-start.2 = (bf16[8,72,256]{2,1,0:T(8,128)(2,1)S(1)}, bf16[8,72,256]{2,1,0:T(8,128)(2,1)S(1)}, u32[]{:S(2)}, u32[]{:S(2)}) collective-permute-start(bf16[8,72,256]{2,1,0:T(8,128)(2,1)S(1)} %get-tuple-element.27), channel_id=1, source_target_pairs={{0,192},{32,224},{64,0},{96,32},{128,64},{160,96},{192,128},{224,1... | collective-permute-start | bytes 884744 | tf_op jit(solution)/shard_map/ppermute | solution.py:268
  13.0 13.4 %collective-permute-start.3 = (bf16[8,72,256]{2,1,0:T(8,128)(2,1)S(1)}, bf16[8,72,256]{2,1,0:T(8,128)(2,1)S(1)}, u32[]{:S(2)}, u32[]{:S(2)}) collective-permute-start(bf16[8,72,256]{2,1,0:T(8,128)(2,1)S(1)} %get-tuple-element.28), channel_id=1, source_target_pairs={{0,64},{32,96},{64,128},{96,160},{128,192},{160,224},{192,0},{224,... | collective-permute-start | bytes 884744 | tf_op jit(solution)/shard_map/ppermute | solution.py:268
  21.4 8.3 %collective-permute-start.7 = (bf16[8,72,256]{2,1,0:T(8,128)(2,1)S(1)}, bf16[8,72,256]{2,1,0:T(8,128)(2,1)S(1)}, u32[]{:S(2)}, u32[]{:S(2)}) collective-permute-start(bf16[8,72,256]{2,1,0:T(8,128)(2,1)S(1)} %join.2.refs_0_), channel_id=1, source_target_pairs={{0,64},{32,96},{64,128},{96,160},{128,192},{160,224},{192,0},{224,... | collective-permute-start | bytes 884744 | tf_op jit(solution)/shard_map/ppermute | solution.py:268
  26.5 3.2 %copy-start.7 = (f32[8,72,256]{2,1,0:T(8,128)S(1)}, f32[8,72,256]{2,1,0:T(8,128)}, u32[]{:S(2)}) copy-start(f32[8,72,256]{2,1,0:T(8,128)} %copy-done.6) | copy-start | bytes 1769476
  26.6 9.2 %collective-permute-start.6 = (bf16[8,72,256]{2,1,0:T(8,128)(2,1)S(1)}, bf16[8,72,256]{2,1,0:T(8,128)(2,1)S(1)}, u32[]{:S(2)}, u32[]{:S(2)}) collective-permute-start(bf16[8,72,256]{2,1,0:T(8,128)(2,1)S(1)} %join.3), channel_id=1, source_target_pairs={{0,192},{32,224},{64,0},{96,32},{128,64},{160,96},{192,128},{224,1... | collective-permute-start | bytes 884744 | tf_op jit(solution)/shard_map/ppermute | solution.py:268
  35.7 11.0 %copy-start.1 = (bf16[3,2,2,3,4,8,256]{6,5,4,3,2,1,0:T(8,128)(2,1)S(1)}, bf16[3,2,2,3,4,8,256]{6,5,4,3,2,1,0:T(8,128)(2,1)}, u32[]{:S(2)}) copy-start(bf16[3,2,2,3,4,8,256]{6,5,4,3,2,1,0:T(8,128)(2,1)} %stored_ref.3) | copy-start | bytes 1769476
  35.7 11.0 %copy-start.3 = (f32[4,256]{1,0:T(4,128)S(1)}, f32[4,256]{1,0:T(4,128)}, u32[]{:S(2)}) copy-start(f32[4,256]{1,0:T(4,128)} %weight_ref.3) | copy-start | bytes 12292
  36.8 27.9 %all-to-all-start = ((bf16[32,40,256]{2,1,0:T(8,128)(2,1)}), bf16[32,40,256]{2,1,0:T(8,128)(2,1)S(1)}, u32[]{:S(2)}, u32[]{:S(2)}) async-start(bf16[32,40,256]{2,1,0:T(8,128)(2,1)} %sum.3), calls=%async_computation | async-start | bytes 1310720 | tf_op jit(solution)/shard_map/all_to_all | solution.py:361
  47.1 23.5 %copy-start.2 = (f32[4,4,256]{2,1,0:T(4,128)S(1)}, f32[4,4,256]{2,1,0:T(4,128)}, u32[]{:S(2)}) copy-start(f32[4,4,256]{2,1,0:T(4,128)} %metric_ref.3) | copy-start | bytes 49156
  47.1 23.5 %copy-start.5 = (bf16[256,256]{1,0:T(8,128)(2,1)S(1)}, bf16[256,256]{1,0:T(8,128)(2,1)}, u32[]{:S(2)}) copy-start(bf16[256,256]{1,0:T(8,128)(2,1)} %constant.68.clone.line_ref) | copy-start | bytes 393220
  65.2 8.5 %collective-permute-start.8 = (bf16[6,3,2,8,256]{4,3,2,1,0:T(8,128)(2,1)S(1)}, bf16[6,3,2,8,256]{4,3,2,1,0:T(8,128)(2,1)S(1)}, u32[]{:S(2)}, u32[]{:S(2)}) collective-permute-start(bf16[6,3,2,8,256]{4,3,2,1,0:T(8,128)(2,1)S(1)} %get-tuple-element.38), channel_id=1, source_target_pairs={{0,1},{1,2},{2,3},{3,4},{4,5},{5,6},{6,7},{7,8},{8,9},{9,10},{10,1... | collective-permute-start | bytes 442376 | tf_op jit(solution)/shard_map/ppermute | solution.py:378
  67.6 6.1 %collective-permute-start.9 = (bf16[6,3,2,8,256]{4,3,2,1,0:T(8,128)(2,1)S(1)}, bf16[6,3,2,8,256]{4,3,2,1,0:T(8,128)(2,1)S(1)}, u32[]{:S(2)}, u32[]{:S(2)}) collective-permute-start(bf16[6,3,2,8,256]{4,3,2,1,0:T(8,128)(2,1)S(1)} %get-tuple-element.39), channel_id=1, source_target_pairs={{1,0},{2,1},{3,2},{4,3},{5,4},{6,5},{7,6},{8,7},{9,8},{10,9},{11,1... | collective-permute-start | bytes 442376 | tf_op jit(solution)/shard_map/ppermute | solution.py:379

commit v5 on v4

--- a/solution.py
+++ b/solution.py
@@ -17,7 +17,7 @@
 LD = JD * NK
 ROWS = 40
 PAIR = 72
-PARTS = (16, 16)
+PARTS = (18, 14)
 SHARE_US, JOIN_US, SUM_US = (20, 1), 1, (20, 1)
 VMEM = pl.BlockSpec(memory_space=pltpu.VMEM)
 SMEM = pl.BlockSpec(memory_space=pltpu.SMEM)
@@ -127,18 +127,32 @@
     for before_ref in before_refs:
         start = before_ref.shape[0]
         out_ref[:start] = before_ref[...]
+    low = lax.broadcasted_iota(jnp.int32, (8, 128), 0) < 4
 
     def step(pair, carry):
         total = own_ref[pair] + sent_ref[pair].astype(jnp.float32)
-        total = (total + joined_ref[pair].astype(jnp.float32)).astype(jnp.bfloat16)
-        out_ref[start + 2 * pair] = total[:ROWS]
-        out_ref[start + 2 * pair + 1] = total[PAIR - ROWS :]
+        total = total + joined_ref[pair].astype(jnp.float32)
+        left, right = total[:, :128], total[:, 128:]
+        middle = slice(32, 40)
+        even = jnp.where(low, left[middle], pltpu.roll(right[middle], 4, 0))
+        odd = jnp.where(low, pltpu.roll(left[middle], 4, 0), right[middle])
+        for i, mixed, rows in ((0, even, slice(0, 32)), (1, odd, slice(40, 72))):
+            block = jnp.concatenate([left[rows], mixed, right[rows]], axis=0)
+            out_ref[start + 2 * pair + i] = block.astype(jnp.bfloat16)
         return carry
 
     lax.fori_loop(0, own_ref.shape[0], step, 0)
 
 
-def place_kernel(place_ref, held_ref, own_ref, low_ref, high_ref):
+def place_kernel(place_ref, packed_ref, own_ref, low_ref, high_ref, held_ref):
+    def unpack(h, carry):
+        mixed = packed_ref[h, 32:40].astype(jnp.float32)
+        turned = pltpu.roll(mixed, 4, 0).astype(jnp.bfloat16)
+        held_ref[h, :, :128] = packed_ref[h, :40]
+        held_ref[h, :, 128:] = jnp.concatenate([packed_ref[h, 40:], turned], axis=0)
+        return carry
+
+    lax.fori_loop(0, packed_ref.shape[0], unpack, 0, unroll=2)
     held = held_ref[...].reshape(-1, P_SIZE)
     rows = jnp.dot(place_ref[...], held, preferred_element_type=jnp.float32)
     rows = rows.astype(jnp.bfloat16).reshape(own_ref.shape)
@@ -328,9 +342,7 @@
         velocity = [
             pl.pallas_call(
                 sum_kernel,
-                out_shape=jax.ShapeDtypeStruct(
-                    (sum(PARTS[: part + 1]), ROWS, P_SIZE), jnp.bfloat16
-                ),
+                out_shape=jax.ShapeDtypeStruct((sum(PARTS[: part + 1]), PAIR, 128), jnp.bfloat16),
                 in_specs=[VMEM] * (3 + part),
                 out_specs=VMEM,
                 compiler_params=PARAMS,
@@ -344,11 +356,12 @@
 def placing(slot_line):
     me = lax.axis_index("space")
     ids = lax.dynamic_index_in_dim(slot_line, me, 1, keepdims=False)
-    in_row = jnp.arange(ROWS, dtype=jnp.int32) - (ROWS - 36) * (me % 2)
+    place = jnp.arange(ROWS, dtype=jnp.int32)
+    in_row = jnp.where(me % 2 == 0, place, jnp.where(place < 32, place + 4, place - 32))
     held = jnp.where(in_row[None, :] < 18, ids[:, 0:1], ids[:, 1:2])
     inner = in_row % 18
     source = (inner % 6 * 3 + inner // 6)[None, :] * LD + held
-    real = (in_row >= 0) & (in_row < 36)
+    real = place < 36
     source = jnp.where((held >= 0) & real[None, :], source, -1).reshape(1, -1)
     target = jnp.arange(18 * LD, dtype=jnp.int32)[:, None]
     return (source == target).astype(jnp.bfloat16)
@@ -370,6 +383,7 @@
         ],
         in_specs=[VMEM, VMEM],
         out_specs=[VMEM, VMEM, VMEM],
+        scratch_shapes=[pltpu.VMEM((holders, ROWS, P_SIZE), jnp.bfloat16)],
         compiler_params=PARAMS,
         name="place",
     )(placing(slot_line), velocity)

time: 92.7 us -> 91.5 us (0.987)
  waiting for transfers between devices: 39.3 us -> 37.6 us
    all_to_all x1, waiting for transfers between devices: 17.1 us -> 15.7 us  [per_device(): lax.all_to_all(velocity, 'space', split_axis=0, concat_axis=0, tiled=True)]
  transfers between devices with their start and end apart: 11 -> 11, of which waited for: 8 -> 8; matrix products, arithmetic and copies ran while one was open for 3% -> 2% of each run, Pallas kernels for 7% -> 7%
where the time goes in v5:
time: 91.5 us; the launch traced here: 91.2 us
  waiting for transfers between devices  37.6 us (41%)
  starting transfers between devices  21.7 us (24%)
  blocking collectives  16.6 us (18%)
  Pallas kernels  9.78 us (11%)
  local copies, waits for them, and re-layouts  4.12 us (5%)
    ppermute x6, waiting for transfers between devices, along(): return lax.ppermute(value, 'block', route)  18.5 us
    all_to_all x1, blocking collectives, per_device(): lax.all_to_all(gram, 'space', split_axis=0, concat_axis=0, tiled=True)  16.6 us
    all_to_all x1, waiting for transfers between devices, per_device(): lax.all_to_all(velocity, 'space', split_axis=0, concat_axis=0, tiled=True)  15.7 us
    all_to_all x1, starting transfers between devices, per_device(): lax.all_to_all(velocity, 'space', split_axis=0, concat_axis=0, tiled=True)  9.76 us
    ppermute x6, starting transfers between devices, along(): return lax.ppermute(value, 'block', route)  5.83 us
    pallas_call x2, Pallas kernels, shares(): pl.pallas_call(share_kernel, out_shape=[jax.ShapeDtypeStruct(shape, jnp.f...  4.61 us
    slice x2, local copies, waits for them, and re-layouts, shares(): mine = held[start:start + step]  3.1 us
    ppermute x1, starting transfers between devices, per_device(): high = lax.ppermute(high, 'space', backward)  3.07 us
  transfers between devices with their start and end apart: 11, of which 8 were waited for; matrix products, arithmetic and copies ran while one was open for 2% of the time, Pallas kernels for 7%

profile of v5, /device:TPU:6, one launch (start us, length us, event | category | flops | bytes accessed | tf_op | source)
XLA Modules:
  0.0 91.2 jit_solution(6523990831285193796)
XLA Ops:
  0.7 1.7 %slice.20.mine_ref = bf16[18,2,3,32,256]{4,3,2,1,0:T(8,128)(2,1)S(1)} slice(bf16[32,2,3,32,256]{4,3,2,1,0:T(8,128)(2,1)} %bitcast.10), slice={[0:18], [0:2], [0:3], [0:32], [0:256]} | slice | bytes 3538944 | tf_op jit(solution)/shard_map/slice | solution.py:296
  2.3 0.1 collective-permute-start.1
  2.4 1.0 %table.1.table_ref = bf16[2,160,384]{2,1,0:T(8,128)(2,1)S(1)} custom-call(s32[1]{0:T(128)} %bitcast.5.block_ref, s32[24]{0:T(128)S(1)} %copy-done.4), custom_call_target="tpu_custom_call" | custom-call | tf_op jit(solution)/shard_map/table/pallas_call | solution.py:284
  3.4 1.4 %slice.17.mine_ref = bf16[14,2,3,32,256]{4,3,2,1,0:T(8,128)(2,1)S(1)} slice(bf16[32,2,3,32,256]{4,3,2,1,0:T(8,128)(2,1)} %bitcast.11), slice={[18:32], [0:2], [0:3], [0:32], [0:256]} | slice | bytes 2752512 | tf_op jit(solution)/shard_map/slice | solution.py:296
  4.9 0.6 collective-permute-start
  5.4 0.8 collective-permute-done.1.other_ref
  6.2 2.5 %share.2 = (f32[9,72,256]{2,1,0:T(8,128)S(1)}, f32[9,72,256]{2,1,0:T(8,128)S(1)}, bf16[9,72,256]{2,1,0:T(8,128)(2,1)S(1)}, bf16[9,72,256]{2,1,0:T(8,128)(2,1)S(1)}) custom-call(bf16[18,2,3,32,256]{4,3,2,1,0:T(8,128)(2,1)S(1)} %slice.20.mine_ref, bf16[18,2,3,32,256]{4,3,2,1,0:T(8,128)(2,1)} %collective-permute-done.1.other_ref, ...), custom_call_target="tpu_custom_call" | custom-call | flops 20000000000 | tf_op jit(solution)/shard_map/share/pallas_call | solution.py:306
  8.7 2.3 %collective-permute-start.4 = (bf16[9,72,256]{2,1,0:T(8,128)(2,1)S(1)}, bf16[9,72,256]{2,1,0:T(8,128)(2,1)S(1)}, u32[]{:S(2)}, u32[]{:S(2)}) collective-permute-start(bf16[9,72,256]{2,1,0:T(8,128)(2,1)S(1)} %get-tuple-element.33), channel_id=1, source_target_pairs={{0,64},{32,96},{64,128},{96,160},{128,192},{160,224},{192,0},{224,... | collective-permute-start | bytes 995336 | tf_op jit(solution)/shard_map/ppermute | solution.py:282
  11.0 2.1 %share.3 = (f32[7,72,256]{2,1,0:T(8,128)S(1)}, bf16[7,72,256]{2,1,0:T(8,128)(2,1)S(1)}, bf16[7,72,256]{2,1,0:T(8,128)(2,1)S(1)}, f32[7,72,256]{2,1,0:T(8,128)S(1)}) custom-call(bf16[14,2,3,32,256]{4,3,2,1,0:T(8,128)(2,1)S(1)} %slice.17.mine_ref, bf16[14,2,3,32,256]{4,3,2,1,0:T(8,128)(2,1)S(1)} %collective-permute-done.other_ref, ...), custom_call_target="tpu_custom_call" | custom-call | flops 1000000000 | tf_op jit(solution)/shard_map/share/pallas_call | solution.py:306
  13.2 0.7 collective-permute-start.2
  13.9 2.7 %collective-permute-start.3 = (bf16[7,72,256]{2,1,0:T(8,128)(2,1)S(1)}, bf16[7,72,256]{2,1,0:T(8,128)(2,1)S(1)}, u32[]{:S(2)}, u32[]{:S(2)}) collective-permute-start(bf16[7,72,256]{2,1,0:T(8,128)(2,1)S(1)} %get-tuple-element.28), channel_id=1, source_target_pairs={{0,64},{32,96},{64,128},{96,160},{128,192},{160,224},{192,0},{224,... | collective-permute-start | bytes 774152 | tf_op jit(solution)/shard_map/ppermute | solution.py:282
  16.5 2.9 %collective-permute-done.4.passing_ref = bf16[9,72,256]{2,1,0:T(8,128)(2,1)S(1)} collective-permute-done((bf16[9,72,256]{2,1,0:T(8,128)(2,1)S(1)}, bf16[9,72,256]{2,1,0:T(8,128)(2,1)S(1)}, u32[]{:S(2)}, u32[]{:S(2)}) %collective-permute-start.4) | collective-permute-done | bytes 331808 | tf_op jit(solution)/shard_map/ppermute | solution.py:282
  19.5 3.5 %collective-permute-done.5.sent_ref = bf16[9,72,256]{2,1,0:T(8,128)(2,1)S(1)} collective-permute-done((bf16[9,72,256]{2,1,0:T(8,128)(2,1)S(1)}, bf16[9,72,256]{2,1,0:T(8,128)(2,1)S(1)}, u32[]{:S(2)}, u32[]{:S(2)}) %collective-permute-start.5) | collective-permute-done | bytes 331808 | tf_op jit(solution)/shard_map/ppermute | solution.py:282
  22.9 0.1 join.2.refs_0_
  23.3 4.0 %collective-permute-done.2.passing_ref = bf16[7,72,256]{2,1,0:T(8,128)(2,1)S(1)} collective-permute-done((bf16[7,72,256]{2,1,0:T(8,128)(2,1)S(1)}, bf16[7,72,256]{2,1,0:T(8,128)(2,1)S(1)}, u32[]{:S(2)}, u32[]{:S(2)}) %collective-permute-start.2) | collective-permute-done | bytes 258080 | tf_op jit(solution)/shard_map/ppermute | solution.py:282
  27.5 3.8 %collective-permute-done.7.joined_ref = bf16[9,72,256]{2,1,0:T(8,128)(2,1)S(1)} collective-permute-done((bf16[9,72,256]{2,1,0:T(8,128)(2,1)S(1)}, bf16[9,72,256]{2,1,0:T(8,128)(2,1)S(1)}, u32[]{:S(2)}, u32[]{:S(2)}) %collective-permute-start.7) | collective-permute-done | bytes 331808 | tf_op jit(solution)/shard_map/ppermute | solution.py:282
  31.3 0.2 sum.2.refs_0_
  31.5 4.3 %collective-permute-done.6.joined_ref = bf16[7,72,256]{2,1,0:T(8,128)(2,1)S(1)} collective-permute-done((bf16[7,72,256]{2,1,0:T(8,128)(2,1)S(1)}, bf16[7,72,256]{2,1,0:T(8,128)(2,1)S(1)}, u32[]{:S(2)}, u32[]{:S(2)}) %collective-permute-start.6) | collective-permute-done | bytes 258080 | tf_op jit(solution)/shard_map/ppermute | solution.py:282
  35.8 1.0 %sum.3 = bf16[32,72,128]{2,1,0:T(8,128)(2,1)} custom-call(f32[7,72,256]{2,1,0:T(8,128)S(1)} %get-tuple-element.26.own_ref, bf16[7,72,256]{2,1,0:T(8,128)(2,1)S(1)} %collective-permute-done.3.sent_ref, bf16[7,72,256]{2,1,0:T(8,128)(2,1)S(1)} %collective-permute-done.6.joined_ref, bf16[18,72,128]{2,1,0:T(8,128)(2,1)S(1)} %sum.2.refs_0_), custom_call_target="tpu_custom_call" | custom-call | flops 1000000000 | tf_op jit(solution)/shard_map/sum/pallas_call | solution.py:343
  36.8 9.8 %all-to-all-start = ((bf16[32,72,128]{2,1,0:T(8,128)(2,1)}), bf16[32,72,128]{2,1,0:T(8,128)(2,1)S(1)}, u32[]{:S(2)}, u32[]{:S(2)}) async-start(bf16[32,72,128]{2,1,0:T(8,128)(2,1)} %sum.3), calls=%async_computation | async-start | bytes 1179648 | tf_op jit(solution)/shard_map/all_to_all | solution.py:374
  46.8 0.3 stored.1.before_ref
  47.1 0.4 fusion.place_ref
  47.6 15.7 %all-to-all-done.packed_ref = bf16[32,72,128]{2,1,0:T(8,128)(2,1)S(1)} async-done(((bf16[32,72,128]{2,1,0:T(8,128)(2,1)}), bf16[32,72,128]{2,1,0:T(8,128)(2,1)S(1)}, u32[]{:S(2)}, u32[]{:S(2)}) %all-to-all-start) | async-done | bytes 589856 | tf_op jit(solution)/shard_map/all_to_all | solution.py:374
  63.3 0.7 place.1
  64.0 2.4 %collective-permute-start.8 = (bf16[6,3,2,8,256]{4,3,2,1,0:T(8,128)(2,1)S(1)}, bf16[6,3,2,8,256]{4,3,2,1,0:T(8,128)(2,1)S(1)}, u32[]{:S(2)}, u32[]{:S(2)}) collective-permute-start(bf16[6,3,2,8,256]{4,3,2,1,0:T(8,128)(2,1)S(1)} %get-tuple-element.38), channel_id=1, source_target_pairs={{0,1},{1,2},{2,3},{3,4},{4,5},{5,6},{6,7},{7,8},{8,9},{9,10},{10,1... | collective-permute-start | bytes 442376 | tf_op jit(solution)/shard_map/ppermute | solution.py:392
  66.4 3.1 %collective-permute-start.9 = (bf16[6,3,2,8,256]{4,3,2,1,0:T(8,128)(2,1)S(1)}, bf16[6,3,2,8,256]{4,3,2,1,0:T(8,128)(2,1)S(1)}, u32[]{:S(2)}, u32[]{:S(2)}) collective-permute-start(bf16[6,3,2,8,256]{4,3,2,1,0:T(8,128)(2,1)S(1)} %get-tuple-element.39), channel_id=1, source_target_pairs={{1,0},{2,1},{3,2},{4,3},{5,4},{6,5},{7,6},{8,7},{9,8},{10,9},{11,1... | collective-permute-start | bytes 442376 | tf_op jit(solution)/shard_map/ppermute | solution.py:393
  69.4 0.5 within.1.base_ref
  70.0 2.6 %collective-permute-done.8.low_ref = bf16[6,3,2,8,256]{4,3,2,1,0:T(8,128)(2,1)S(1)} collective-permute-done((bf16[6,3,2,8,256]{4,3,2,1,0:T(8,128)(2,1)S(1)}, bf16[6,3,2,8,256]{4,3,2,1,0:T(8,128)(2,1)S(1)}, u32[]{:S(2)}, u32[]{:S(2)}) %collective-permute-start.8) | collective-permute-done | bytes 147488 | tf_op jit(solution)/shard_map/ppermute | solution.py:392
  72.5 1.3 %vorticity.1 = (bf16[3,2,3,4,8,256]{5,4,3,2,1,0:T(8,128)(2,1)}, f32[32,1,128]{2,1,0:T(1,128)S(1)}) custom-call(bf16[6,3,4,8,256]{4,3,2,1,0:T(8,128)(2,1)S(1)} %get-tuple-element.37.own_ref, bf16[6,3,2,8,256]{4,3,2,1,0:T(8,128)(2,1)S(1)} %collective-permute-done.8.low_ref, bf16[6,3,2,8,256]{4,3,2,1,0:T(8,128)(2,1)S(1)} %collective-permute-done.9.high_ref, ...), custom_call_target="tpu_custom_call" | custom-call | tf_op jit(solution)/shard_map/vorticity/pallas_call | solution.py:413
  73.8 16.6 %all_to_all.10 = f32[32,1,128]{2,1,0:T(1,128)S(1)} all-to-all(f32[32,1,128]{2,1,0:T(1,128)S(1)} %get-tuple-element.41), channel_id=1, replica_groups=mesh['block'=8,'space'=32] {'space'}, dimensions={0} | all-to-all | bytes 32768 | tf_op jit(solution)/shard_map/all_to_all | solution.py:425
  90.5 0.1 reshape.95
  90.6 0.6 copy.12
  (31 shorter events, 0.7 us)
Async XLA Ops:
  0.6 22.5 %copy-start = (s32[32,32,2]{1,2,0:T(2,128)S(1)}, s32[32,32,2]{1,2,0:T(2,128)}, u32[]{:S(2)}) copy-start(s32[32,32,2]{1,2,0:T(2,128)} %param.8) | copy-start | bytes 24580
  0.6 1.8 %copy-start.4 = (s32[24]{0:T(128)S(1)}, s32[24]{0:T(128)}, u32[]{:S(2)}) copy-start(s32[24]{0:T(128)} %freq_ref.1) | copy-start | bytes 292
  2.3 3.9 %collective-permute-start.1 = (bf16[18,2,3,32,256]{4,3,2,1,0:T(8,128)(2,1)S(1)}, bf16[18,2,3,32,256]{4,3,2,1,0:T(8,128)(2,1)}, u32[]{:S(2)}, u32[]{:S(2)}) collective-permute-start(bf16[18,2,3,32,256]{4,3,2,1,0:T(8,128)(2,1)S(1)} %slice.20.mine_ref), channel_id=1, source_target_pairs={{0,32},{32,0},{64,96},{96,64},{128,160},{160,128},{192,224},{224,1... | collective-permute-start | bytes 5308424 | tf_op jit(solution)/shard_map/ppermute | solution.py:297
  4.9 6.2 %collective-permute-start = (bf16[14,2,3,32,256]{4,3,2,1,0:T(8,128)(2,1)S(1)}, bf16[14,2,3,32,256]{4,3,2,1,0:T(8,128)(2,1)S(1)}, u32[]{:S(2)}, u32[]{:S(2)}) collective-permute-start(bf16[14,2,3,32,256]{4,3,2,1,0:T(8,128)(2,1)S(1)} %slice.17.mine_ref), channel_id=1, source_target_pairs={{0,32},{32,0},{64,96},{96,64},{128,160},{160,128},{192,224},{224,1... | collective-permute-start | bytes 4128776 | tf_op jit(solution)/shard_map/ppermute | solution.py:297
  8.7 4.4 %copy-start.6 = (f32[9,72,256]{2,1,0:T(8,128)}, f32[9,72,256]{2,1,0:T(8,128)S(1)}, u32[]{:S(2)}) copy-start(f32[9,72,256]{2,1,0:T(8,128)S(1)} %get-tuple-element.24.own_ref) | copy-start | bytes 1990660
  8.7 10.7 %collective-permute-start.4 = (bf16[9,72,256]{2,1,0:T(8,128)(2,1)S(1)}, bf16[9,72,256]{2,1,0:T(8,128)(2,1)S(1)}, u32[]{:S(2)}, u32[]{:S(2)}) collective-permute-start(bf16[9,72,256]{2,1,0:T(8,128)(2,1)S(1)} %get-tuple-element.33), channel_id=1, source_target_pairs={{0,64},{32,96},{64,128},{96,160},{128,192},{160,224},{192,0},{224,... | collective-permute-start | bytes 995336 | tf_op jit(solution)/shard_map/ppermute | solution.py:282
  11.0 11.9 %collective-permute-start.5 = (bf16[9,72,256]{2,1,0:T(8,128)(2,1)S(1)}, bf16[9,72,256]{2,1,0:T(8,128)(2,1)S(1)}, u32[]{:S(2)}, u32[]{:S(2)}) collective-permute-start(bf16[9,72,256]{2,1,0:T(8,128)(2,1)S(1)} %get-tuple-element.34), channel_id=1, source_target_pairs={{0,192},{32,224},{64,0},{96,32},{128,64},{160,96},{192,128},{224,1... | collective-permute-start | bytes 995336 | tf_op jit(solution)/shard_map/ppermute | solution.py:282
  13.2 14.2 %collective-permute-start.2 = (bf16[7,72,256]{2,1,0:T(8,128)(2,1)S(1)}, bf16[7,72,256]{2,1,0:T(8,128)(2,1)S(1)}, u32[]{:S(2)}, u32[]{:S(2)}) collective-permute-start(bf16[7,72,256]{2,1,0:T(8,128)(2,1)S(1)} %get-tuple-element.27), channel_id=1, source_target_pairs={{0,192},{32,224},{64,0},{96,32},{128,64},{160,96},{192,128},{224,1... | collective-permute-start | bytes 774152 | tf_op jit(solution)/shard_map/ppermute | solution.py:282
  13.9 13.5 %collective-permute-start.3 = (bf16[7,72,256]{2,1,0:T(8,128)(2,1)S(1)}, bf16[7,72,256]{2,1,0:T(8,128)(2,1)S(1)}, u32[]{:S(2)}, u32[]{:S(2)}) collective-permute-start(bf16[7,72,256]{2,1,0:T(8,128)(2,1)S(1)} %get-tuple-element.28), channel_id=1, source_target_pairs={{0,64},{32,96},{64,128},{96,160},{128,192},{160,224},{192,0},{224,... | collective-permute-start | bytes 774152 | tf_op jit(solution)/shard_map/ppermute | solution.py:282
  23.0 8.3 %collective-permute-start.7 = (bf16[9,72,256]{2,1,0:T(8,128)(2,1)S(1)}, bf16[9,72,256]{2,1,0:T(8,128)(2,1)S(1)}, u32[]{:S(2)}, u32[]{:S(2)}) collective-permute-start(bf16[9,72,256]{2,1,0:T(8,128)(2,1)S(1)} %join.2.refs_0_), channel_id=1, source_target_pairs={{0,64},{32,96},{64,128},{96,160},{128,192},{160,224},{192,0},{224,... | collective-permute-start | bytes 995336 | tf_op jit(solution)/shard_map/ppermute | solution.py:282
  27.3 4.0 %copy-start.7 = (f32[9,72,256]{2,1,0:T(8,128)S(1)}, f32[9,72,256]{2,1,0:T(8,128)}, u32[]{:S(2)}) copy-start(f32[9,72,256]{2,1,0:T(8,128)} %copy-done.6) | copy-start | bytes 1990660
  27.4 8.4 %collective-permute-start.6 = (bf16[7,72,256]{2,1,0:T(8,128)(2,1)S(1)}, bf16[7,72,256]{2,1,0:T(8,128)(2,1)S(1)}, u32[]{:S(2)}, u32[]{:S(2)}) collective-permute-start(bf16[7,72,256]{2,1,0:T(8,128)(2,1)S(1)} %join.3), channel_id=1, source_target_pairs={{0,192},{32,224},{64,0},{96,32},{128,64},{160,96},{192,128},{224,1... | collective-permute-start | bytes 774152 | tf_op jit(solution)/shard_map/ppermute | solution.py:282
  35.8 11.0 %copy-start.1 = (bf16[3,2,2,3,4,8,256]{6,5,4,3,2,1,0:T(8,128)(2,1)S(1)}, bf16[3,2,2,3,4,8,256]{6,5,4,3,2,1,0:T(8,128)(2,1)}, u32[]{:S(2)}) copy-start(bf16[3,2,2,3,4,8,256]{6,5,4,3,2,1,0:T(8,128)(2,1)} %stored_ref.3) | copy-start | bytes 1769476
  35.8 11.0 %copy-start.3 = (f32[4,256]{1,0:T(4,128)S(1)}, f32[4,256]{1,0:T(4,128)}, u32[]{:S(2)}) copy-start(f32[4,256]{1,0:T(4,128)} %weight_ref.3) | copy-start | bytes 12292
  36.8 26.5 %all-to-all-start = ((bf16[32,72,128]{2,1,0:T(8,128)(2,1)}), bf16[32,72,128]{2,1,0:T(8,128)(2,1)S(1)}, u32[]{:S(2)}, u32[]{:S(2)}) async-start(bf16[32,72,128]{2,1,0:T(8,128)(2,1)} %sum.3), calls=%async_computation | async-start | bytes 1179648 | tf_op jit(solution)/shard_map/all_to_all | solution.py:374
  47.1 22.3 %copy-start.2 = (f32[4,4,256]{2,1,0:T(4,128)S(1)}, f32[4,4,256]{2,1,0:T(4,128)}, u32[]{:S(2)}) copy-start(f32[4,4,256]{2,1,0:T(4,128)} %metric_ref.3) | copy-start | bytes 49156
  47.1 22.3 %copy-start.5 = (bf16[256,256]{1,0:T(8,128)(2,1)S(1)}, bf16[256,256]{1,0:T(8,128)(2,1)}, u32[]{:S(2)}) copy-start(bf16[256,256]{1,0:T(8,128)(2,1)} %constant.71.clone.line_ref) | copy-start | bytes 393220
  64.0 8.5 %collective-permute-start.8 = (bf16[6,3,2,8,256]{4,3,2,1,0:T(8,128)(2,1)S(1)}, bf16[6,3,2,8,256]{4,3,2,1,0:T(8,128)(2,1)S(1)}, u32[]{:S(2)}, u32[]{:S(2)}) collective-permute-start(bf16[6,3,2,8,256]{4,3,2,1,0:T(8,128)(2,1)S(1)} %get-tuple-element.38), channel_id=1, source_target_pairs={{0,1},{1,2},{2,3},{3,4},{4,5},{5,6},{6,7},{7,8},{8,9},{9,10},{10,1... | collective-permute-start | bytes 442376 | tf_op jit(solution)/shard_map/ppermute | solution.py:392
  66.4 6.2 %collective-permute-start.9 = (bf16[6,3,2,8,256]{4,3,2,1,0:T(8,128)(2,1)S(1)}, bf16[6,3,2,8,256]{4,3,2,1,0:T(8,128)(2,1)S(1)}, u32[]{:S(2)}, u32[]{:S(2)}) collective-permute-start(bf16[6,3,2,8,256]{4,3,2,1,0:T(8,128)(2,1)S(1)} %get-tuple-element.39), channel_id=1, source_target_pairs={{1,0},{2,1},{3,2},{4,3},{5,4},{6,5},{7,6},{8,7},{9,8},{10,9},{11,1... | collective-permute-start | bytes 442376 | tf_op jit(solution)/shard_map/ppermute | solution.py:393

commit v6 on v5

--- a/solution.py
+++ b/solution.py
@@ -166,10 +166,10 @@
         total = jnp.sum(value, axis=(0, 1, 2)).reshape(1, P_SIZE)
         total = total[:, :128] + total[:, 128:]
         row = ((f * 2 + part) * 3 + a) * 3 + b
-        sums_ref[row : row + 1, :] = total
+        sums_ref[pl.ds(row, 1), :] = total
         if a != b:
             row = ((f * 2 + part) * 3 + b) * 3 + a
-            sums_ref[row : row + 1, :] = total if part == 0 else -total
+            sums_ref[pl.ds(row, 1), :] = total if part == 0 else -total
 
     put(0, left[0] * right[0] + left[1] * right[1])
     if a != b:
@@ -231,7 +231,8 @@
     sums_ref[...] = before_ref[...]
     eta_x, eta_y = (metric_ref[i].reshape(JD, 1, P_SIZE) * (1.0 / 12.0) for i in (2, 3))
     weight = weight_ref[...].reshape(1, JD, 1, P_SIZE)
-    for f in range(stored_ref.shape[0]):
+
+    def step(f, carry):
         new = []
         for r in range(2):
             q = 2 * f + r
@@ -255,6 +256,9 @@
         add_products(sums_ref, f, 0, 0, left, new)
         for a in range(2):
             add_products(sums_ref, f, 0, a + 1, left, column(stored_ref, f, a))
+        return carry
+
+    lax.fori_loop(0, stored_ref.shape[0], step, 0)
 
     total = lax.dot_general(
         jnp.full((8, 128), scale, jnp.float32),

time: 91.5 us -> 91.5 us (level)
  no operation moved by 1% of the time
where the time goes in v6:
time: 91.5 us; the launch traced here: 91.2 us
  waiting for transfers between devices  37.6 us (41%)
  starting transfers between devices  21.7 us (24%)
  blocking collectives  16.6 us (18%)
  Pallas kernels  9.8 us (11%)
  local copies, waits for them, and re-layouts  4.12 us (5%)
    ppermute x6, waiting for transfers between devices, along(): return lax.ppermute(value, 'block', route)  18.5 us
    all_to_all x1, blocking collectives, per_device(): lax.all_to_all(gram, 'space', split_axis=0, concat_axis=0, tiled=True)  16.6 us
    all_to_all x1, waiting for transfers between devices, per_device(): lax.all_to_all(velocity, 'space', split_axis=0, concat_axis=0, tiled=True)  15.7 us
    all_to_all x1, starting transfers between devices, per_device(): lax.all_to_all(velocity, 'space', split_axis=0, concat_axis=0, tiled=True)  9.76 us
    ppermute x6, starting transfers between devices, along(): return lax.ppermute(value, 'block', route)  5.83 us
    pallas_call x2, Pallas kernels, shares(): pl.pallas_call(share_kernel, out_shape=[jax.ShapeDtypeStruct(shape, jnp.f...  4.61 us
    slice x2, local copies, waits for them, and re-layouts, shares(): mine = held[start:start + step]  3.1 us
    ppermute x1, starting transfers between devices, per_device(): high = lax.ppermute(high, 'space', backward)  3.07 us
  transfers between devices with their start and end apart: 11, of which 8 were waited for; matrix products, arithmetic and copies ran while one was open for 2% of the time, Pallas kernels for 7%

profile of v6, /device:TPU:6, one launch (start us, length us, event | category | flops | bytes accessed | tf_op | source)
XLA Modules:
  0.0 91.2 jit_solution(16835907635155060751)
XLA Ops:
  0.7 1.7 %slice.20.mine_ref = bf16[18,2,3,32,256]{4,3,2,1,0:T(8,128)(2,1)S(1)} slice(bf16[32,2,3,32,256]{4,3,2,1,0:T(8,128)(2,1)} %bitcast.10), slice={[0:18], [0:2], [0:3], [0:32], [0:256]} | slice | bytes 3538944 | tf_op jit(solution)/shard_map/slice | solution.py:300
  2.3 0.1 collective-permute-start.1
  2.4 1.0 %table.1.table_ref = bf16[2,160,384]{2,1,0:T(8,128)(2,1)S(1)} custom-call(s32[1]{0:T(128)} %bitcast.5.block_ref, s32[24]{0:T(128)S(1)} %copy-done.4), custom_call_target="tpu_custom_call" | custom-call | tf_op jit(solution)/shard_map/table/pallas_call | solution.py:288
  3.4 1.4 %slice.17.mine_ref = bf16[14,2,3,32,256]{4,3,2,1,0:T(8,128)(2,1)S(1)} slice(bf16[32,2,3,32,256]{4,3,2,1,0:T(8,128)(2,1)} %bitcast.11), slice={[18:32], [0:2], [0:3], [0:32], [0:256]} | slice | bytes 2752512 | tf_op jit(solution)/shard_map/slice | solution.py:300
  4.9 0.6 collective-permute-start
  5.4 0.8 collective-permute-done.1.other_ref
  6.2 2.5 %share.2 = (f32[9,72,256]{2,1,0:T(8,128)S(1)}, f32[9,72,256]{2,1,0:T(8,128)S(1)}, bf16[9,72,256]{2,1,0:T(8,128)(2,1)S(1)}, bf16[9,72,256]{2,1,0:T(8,128)(2,1)S(1)}) custom-call(bf16[18,2,3,32,256]{4,3,2,1,0:T(8,128)(2,1)S(1)} %slice.20.mine_ref, bf16[18,2,3,32,256]{4,3,2,1,0:T(8,128)(2,1)} %collective-permute-done.1.other_ref, ...), custom_call_target="tpu_custom_call" | custom-call | flops 20000000000 | tf_op jit(solution)/shard_map/share/pallas_call | solution.py:310
  8.7 2.3 %collective-permute-start.4 = (bf16[9,72,256]{2,1,0:T(8,128)(2,1)S(1)}, bf16[9,72,256]{2,1,0:T(8,128)(2,1)S(1)}, u32[]{:S(2)}, u32[]{:S(2)}) collective-permute-start(bf16[9,72,256]{2,1,0:T(8,128)(2,1)S(1)} %get-tuple-element.33), channel_id=1, source_target_pairs={{0,64},{32,96},{64,128},{96,160},{128,192},{160,224},{192,0},{224,... | collective-permute-start | bytes 995336 | tf_op jit(solution)/shard_map/ppermute | solution.py:286
  11.0 2.1 %share.3 = (f32[7,72,256]{2,1,0:T(8,128)S(1)}, bf16[7,72,256]{2,1,0:T(8,128)(2,1)S(1)}, bf16[7,72,256]{2,1,0:T(8,128)(2,1)S(1)}, f32[7,72,256]{2,1,0:T(8,128)S(1)}) custom-call(bf16[14,2,3,32,256]{4,3,2,1,0:T(8,128)(2,1)S(1)} %slice.17.mine_ref, bf16[14,2,3,32,256]{4,3,2,1,0:T(8,128)(2,1)S(1)} %collective-permute-done.other_ref, ...), custom_call_target="tpu_custom_call" | custom-call | flops 1000000000 | tf_op jit(solution)/shard_map/share/pallas_call | solution.py:310
  13.2 0.7 collective-permute-start.2
  13.9 2.7 %collective-permute-start.3 = (bf16[7,72,256]{2,1,0:T(8,128)(2,1)S(1)}, bf16[7,72,256]{2,1,0:T(8,128)(2,1)S(1)}, u32[]{:S(2)}, u32[]{:S(2)}) collective-permute-start(bf16[7,72,256]{2,1,0:T(8,128)(2,1)S(1)} %get-tuple-element.28), channel_id=1, source_target_pairs={{0,64},{32,96},{64,128},{96,160},{128,192},{160,224},{192,0},{224,... | collective-permute-start | bytes 774152 | tf_op jit(solution)/shard_map/ppermute | solution.py:286
  16.5 2.9 %collective-permute-done.4.passing_ref = bf16[9,72,256]{2,1,0:T(8,128)(2,1)S(1)} collective-permute-done((bf16[9,72,256]{2,1,0:T(8,128)(2,1)S(1)}, bf16[9,72,256]{2,1,0:T(8,128)(2,1)S(1)}, u32[]{:S(2)}, u32[]{:S(2)}) %collective-permute-start.4) | collective-permute-done | bytes 331808 | tf_op jit(solution)/shard_map/ppermute | solution.py:286
  19.5 3.5 %collective-permute-done.5.sent_ref = bf16[9,72,256]{2,1,0:T(8,128)(2,1)S(1)} collective-permute-done((bf16[9,72,256]{2,1,0:T(8,128)(2,1)S(1)}, bf16[9,72,256]{2,1,0:T(8,128)(2,1)S(1)}, u32[]{:S(2)}, u32[]{:S(2)}) %collective-permute-start.5) | collective-permute-done | bytes 331808 | tf_op jit(solution)/shard_map/ppermute | solution.py:286
  22.9 0.1 join.2.refs_0_
  23.3 4.0 %collective-permute-done.2.passing_ref = bf16[7,72,256]{2,1,0:T(8,128)(2,1)S(1)} collective-permute-done((bf16[7,72,256]{2,1,0:T(8,128)(2,1)S(1)}, bf16[7,72,256]{2,1,0:T(8,128)(2,1)S(1)}, u32[]{:S(2)}, u32[]{:S(2)}) %collective-permute-start.2) | collective-permute-done | bytes 258080 | tf_op jit(solution)/shard_map/ppermute | solution.py:286
  27.5 3.8 %collective-permute-done.7.joined_ref = bf16[9,72,256]{2,1,0:T(8,128)(2,1)S(1)} collective-permute-done((bf16[9,72,256]{2,1,0:T(8,128)(2,1)S(1)}, bf16[9,72,256]{2,1,0:T(8,128)(2,1)S(1)}, u32[]{:S(2)}, u32[]{:S(2)}) %collective-permute-start.7) | collective-permute-done | bytes 331808 | tf_op jit(solution)/shard_map/ppermute | solution.py:286
  31.3 0.2 sum.2.refs_0_
  31.5 4.3 %collective-permute-done.6.joined_ref = bf16[7,72,256]{2,1,0:T(8,128)(2,1)S(1)} collective-permute-done((bf16[7,72,256]{2,1,0:T(8,128)(2,1)S(1)}, bf16[7,72,256]{2,1,0:T(8,128)(2,1)S(1)}, u32[]{:S(2)}, u32[]{:S(2)}) %collective-permute-start.6) | collective-permute-done | bytes 258080 | tf_op jit(solution)/shard_map/ppermute | solution.py:286
  35.8 1.0 %sum.3 = bf16[32,72,128]{2,1,0:T(8,128)(2,1)} custom-call(f32[7,72,256]{2,1,0:T(8,128)S(1)} %get-tuple-element.26.own_ref, bf16[7,72,256]{2,1,0:T(8,128)(2,1)S(1)} %collective-permute-done.3.sent_ref, bf16[7,72,256]{2,1,0:T(8,128)(2,1)S(1)} %collective-permute-done.6.joined_ref, bf16[18,72,128]{2,1,0:T(8,128)(2,1)S(1)} %sum.2.refs_0_), custom_call_target="tpu_custom_call" | custom-call | flops 1000000000 | tf_op jit(solution)/shard_map/sum/pallas_call | solution.py:347
  36.8 9.8 %all-to-all-start = ((bf16[32,72,128]{2,1,0:T(8,128)(2,1)}), bf16[32,72,128]{2,1,0:T(8,128)(2,1)S(1)}, u32[]{:S(2)}, u32[]{:S(2)}) async-start(bf16[32,72,128]{2,1,0:T(8,128)(2,1)} %sum.3), calls=%async_computation | async-start | bytes 1179648 | tf_op jit(solution)/shard_map/all_to_all | solution.py:378
  46.8 0.3 stored.1.before_ref
  47.1 0.4 fusion.place_ref
  47.6 15.7 %all-to-all-done.packed_ref = bf16[32,72,128]{2,1,0:T(8,128)(2,1)S(1)} async-done(((bf16[32,72,128]{2,1,0:T(8,128)(2,1)}), bf16[32,72,128]{2,1,0:T(8,128)(2,1)S(1)}, u32[]{:S(2)}, u32[]{:S(2)}) %all-to-all-start) | async-done | bytes 589856 | tf_op jit(solution)/shard_map/all_to_all | solution.py:378
  63.3 0.7 place.1
  64.0 2.4 %collective-permute-start.8 = (bf16[6,3,2,8,256]{4,3,2,1,0:T(8,128)(2,1)S(1)}, bf16[6,3,2,8,256]{4,3,2,1,0:T(8,128)(2,1)S(1)}, u32[]{:S(2)}, u32[]{:S(2)}) collective-permute-start(bf16[6,3,2,8,256]{4,3,2,1,0:T(8,128)(2,1)S(1)} %get-tuple-element.38), channel_id=1, source_target_pairs={{0,1},{1,2},{2,3},{3,4},{4,5},{5,6},{6,7},{7,8},{8,9},{9,10},{10,1... | collective-permute-start | bytes 442376 | tf_op jit(solution)/shard_map/ppermute | solution.py:396
  66.4 3.1 %collective-permute-start.9 = (bf16[6,3,2,8,256]{4,3,2,1,0:T(8,128)(2,1)S(1)}, bf16[6,3,2,8,256]{4,3,2,1,0:T(8,128)(2,1)S(1)}, u32[]{:S(2)}, u32[]{:S(2)}) collective-permute-start(bf16[6,3,2,8,256]{4,3,2,1,0:T(8,128)(2,1)S(1)} %get-tuple-element.39), channel_id=1, source_target_pairs={{1,0},{2,1},{3,2},{4,3},{5,4},{6,5},{7,6},{8,7},{9,8},{10,9},{11,1... | collective-permute-start | bytes 442376 | tf_op jit(solution)/shard_map/ppermute | solution.py:397
  69.4 0.5 within.1.base_ref
  70.0 2.6 %collective-permute-done.8.low_ref = bf16[6,3,2,8,256]{4,3,2,1,0:T(8,128)(2,1)S(1)} collective-permute-done((bf16[6,3,2,8,256]{4,3,2,1,0:T(8,128)(2,1)S(1)}, bf16[6,3,2,8,256]{4,3,2,1,0:T(8,128)(2,1)S(1)}, u32[]{:S(2)}, u32[]{:S(2)}) %collective-permute-start.8) | collective-permute-done | bytes 147488 | tf_op jit(solution)/shard_map/ppermute | solution.py:396
  72.5 1.3 %vorticity.1 = (bf16[3,2,3,4,8,256]{5,4,3,2,1,0:T(8,128)(2,1)}, f32[32,1,128]{2,1,0:T(1,128)S(1)}) custom-call(bf16[6,3,4,8,256]{4,3,2,1,0:T(8,128)(2,1)S(1)} %get-tuple-element.37.own_ref, bf16[6,3,2,8,256]{4,3,2,1,0:T(8,128)(2,1)S(1)} %collective-permute-done.8.low_ref, bf16[6,3,2,8,256]{4,3,2,1,0:T(8,128)(2,1)S(1)} %collective-permute-done.9.high_ref, ...), custom_call_target="tpu_custom_call" | custom-call | tf_op jit(solution)/shard_map/vorticity/pallas_call | solution.py:417
  73.8 16.6 %all_to_all.10 = f32[32,1,128]{2,1,0:T(1,128)S(1)} all-to-all(f32[32,1,128]{2,1,0:T(1,128)S(1)} %get-tuple-element.41), channel_id=1, replica_groups=mesh['block'=8,'space'=32] {'space'}, dimensions={0} | all-to-all | bytes 32768 | tf_op jit(solution)/shard_map/all_to_all | solution.py:429
  90.5 0.1 reshape.95
  90.6 0.6 copy.12
  (31 shorter events, 0.7 us)
Async XLA Ops:
  0.6 22.5 %copy-start = (s32[32,32,2]{1,2,0:T(2,128)S(1)}, s32[32,32,2]{1,2,0:T(2,128)}, u32[]{:S(2)}) copy-start(s32[32,32,2]{1,2,0:T(2,128)} %param.8) | copy-start | bytes 24580
  0.6 1.8 %copy-start.4 = (s32[24]{0:T(128)S(1)}, s32[24]{0:T(128)}, u32[]{:S(2)}) copy-start(s32[24]{0:T(128)} %freq_ref.1) | copy-start | bytes 292
  2.3 3.9 %collective-permute-start.1 = (bf16[18,2,3,32,256]{4,3,2,1,0:T(8,128)(2,1)S(1)}, bf16[18,2,3,32,256]{4,3,2,1,0:T(8,128)(2,1)}, u32[]{:S(2)}, u32[]{:S(2)}) collective-permute-start(bf16[18,2,3,32,256]{4,3,2,1,0:T(8,128)(2,1)S(1)} %slice.20.mine_ref), channel_id=1, source_target_pairs={{0,32},{32,0},{64,96},{96,64},{128,160},{160,128},{192,224},{224,1... | collective-permute-start | bytes 5308424 | tf_op jit(solution)/shard_map/ppermute | solution.py:301
  4.9 6.2 %collective-permute-start = (bf16[14,2,3,32,256]{4,3,2,1,0:T(8,128)(2,1)S(1)}, bf16[14,2,3,32,256]{4,3,2,1,0:T(8,128)(2,1)S(1)}, u32[]{:S(2)}, u32[]{:S(2)}) collective-permute-start(bf16[14,2,3,32,256]{4,3,2,1,0:T(8,128)(2,1)S(1)} %slice.17.mine_ref), channel_id=1, source_target_pairs={{0,32},{32,0},{64,96},{96,64},{128,160},{160,128},{192,224},{224,1... | collective-permute-start | bytes 4128776 | tf_op jit(solution)/shard_map/ppermute | solution.py:301
  8.7 4.4 %copy-start.6 = (f32[9,72,256]{2,1,0:T(8,128)}, f32[9,72,256]{2,1,0:T(8,128)S(1)}, u32[]{:S(2)}) copy-start(f32[9,72,256]{2,1,0:T(8,128)S(1)} %get-tuple-element.24.own_ref) | copy-start | bytes 1990660
  8.7 10.7 %collective-permute-start.4 = (bf16[9,72,256]{2,1,0:T(8,128)(2,1)S(1)}, bf16[9,72,256]{2,1,0:T(8,128)(2,1)S(1)}, u32[]{:S(2)}, u32[]{:S(2)}) collective-permute-start(bf16[9,72,256]{2,1,0:T(8,128)(2,1)S(1)} %get-tuple-element.33), channel_id=1, source_target_pairs={{0,64},{32,96},{64,128},{96,160},{128,192},{160,224},{192,0},{224,... | collective-permute-start | bytes 995336 | tf_op jit(solution)/shard_map/ppermute | solution.py:286
  11.0 11.9 %collective-permute-start.5 = (bf16[9,72,256]{2,1,0:T(8,128)(2,1)S(1)}, bf16[9,72,256]{2,1,0:T(8,128)(2,1)S(1)}, u32[]{:S(2)}, u32[]{:S(2)}) collective-permute-start(bf16[9,72,256]{2,1,0:T(8,128)(2,1)S(1)} %get-tuple-element.34), channel_id=1, source_target_pairs={{0,192},{32,224},{64,0},{96,32},{128,64},{160,96},{192,128},{224,1... | collective-permute-start | bytes 995336 | tf_op jit(solution)/shard_map/ppermute | solution.py:286
  13.2 14.2 %collective-permute-start.2 = (bf16[7,72,256]{2,1,0:T(8,128)(2,1)S(1)}, bf16[7,72,256]{2,1,0:T(8,128)(2,1)S(1)}, u32[]{:S(2)}, u32[]{:S(2)}) collective-permute-start(bf16[7,72,256]{2,1,0:T(8,128)(2,1)S(1)} %get-tuple-element.27), channel_id=1, source_target_pairs={{0,192},{32,224},{64,0},{96,32},{128,64},{160,96},{192,128},{224,1... | collective-permute-start | bytes 774152 | tf_op jit(solution)/shard_map/ppermute | solution.py:286
  13.9 13.5 %collective-permute-start.3 = (bf16[7,72,256]{2,1,0:T(8,128)(2,1)S(1)}, bf16[7,72,256]{2,1,0:T(8,128)(2,1)S(1)}, u32[]{:S(2)}, u32[]{:S(2)}) collective-permute-start(bf16[7,72,256]{2,1,0:T(8,128)(2,1)S(1)} %get-tuple-element.28), channel_id=1, source_target_pairs={{0,64},{32,96},{64,128},{96,160},{128,192},{160,224},{192,0},{224,... | collective-permute-start | bytes 774152 | tf_op jit(solution)/shard_map/ppermute | solution.py:286
  23.0 8.3 %collective-permute-start.7 = (bf16[9,72,256]{2,1,0:T(8,128)(2,1)S(1)}, bf16[9,72,256]{2,1,0:T(8,128)(2,1)S(1)}, u32[]{:S(2)}, u32[]{:S(2)}) collective-permute-start(bf16[9,72,256]{2,1,0:T(8,128)(2,1)S(1)} %join.2.refs_0_), channel_id=1, source_target_pairs={{0,64},{32,96},{64,128},{96,160},{128,192},{160,224},{192,0},{224,... | collective-permute-start | bytes 995336 | tf_op jit(solution)/shard_map/ppermute | solution.py:286
  27.3 4.0 %copy-start.7 = (f32[9,72,256]{2,1,0:T(8,128)S(1)}, f32[9,72,256]{2,1,0:T(8,128)}, u32[]{:S(2)}) copy-start(f32[9,72,256]{2,1,0:T(8,128)} %copy-done.6) | copy-start | bytes 1990660
  27.4 8.4 %collective-permute-start.6 = (bf16[7,72,256]{2,1,0:T(8,128)(2,1)S(1)}, bf16[7,72,256]{2,1,0:T(8,128)(2,1)S(1)}, u32[]{:S(2)}, u32[]{:S(2)}) collective-permute-start(bf16[7,72,256]{2,1,0:T(8,128)(2,1)S(1)} %join.3), channel_id=1, source_target_pairs={{0,192},{32,224},{64,0},{96,32},{128,64},{160,96},{192,128},{224,1... | collective-permute-start | bytes 774152 | tf_op jit(solution)/shard_map/ppermute | solution.py:286
  35.8 11.0 %copy-start.1 = (bf16[3,2,2,3,4,8,256]{6,5,4,3,2,1,0:T(8,128)(2,1)S(1)}, bf16[3,2,2,3,4,8,256]{6,5,4,3,2,1,0:T(8,128)(2,1)}, u32[]{:S(2)}) copy-start(bf16[3,2,2,3,4,8,256]{6,5,4,3,2,1,0:T(8,128)(2,1)} %stored_ref.3) | copy-start | bytes 1769476
  35.8 11.0 %copy-start.3 = (f32[4,256]{1,0:T(4,128)S(1)}, f32[4,256]{1,0:T(4,128)}, u32[]{:S(2)}) copy-start(f32[4,256]{1,0:T(4,128)} %weight_ref.3) | copy-start | bytes 12292
  36.8 26.5 %all-to-all-start = ((bf16[32,72,128]{2,1,0:T(8,128)(2,1)}), bf16[32,72,128]{2,1,0:T(8,128)(2,1)S(1)}, u32[]{:S(2)}, u32[]{:S(2)}) async-start(bf16[32,72,128]{2,1,0:T(8,128)(2,1)} %sum.3), calls=%async_computation | async-start | bytes 1179648 | tf_op jit(solution)/shard_map/all_to_all | solution.py:378
  47.1 22.3 %copy-start.2 = (f32[4,4,256]{2,1,0:T(4,128)S(1)}, f32[4,4,256]{2,1,0:T(4,128)}, u32[]{:S(2)}) copy-start(f32[4,4,256]{2,1,0:T(4,128)} %metric_ref.3) | copy-start | bytes 49156
  47.1 22.3 %copy-start.5 = (bf16[256,256]{1,0:T(8,128)(2,1)S(1)}, bf16[256,256]{1,0:T(8,128)(2,1)}, u32[]{:S(2)}) copy-start(bf16[256,256]{1,0:T(8,128)(2,1)} %constant.71.clone.line_ref) | copy-start | bytes 393220
  64.0 8.5 %collective-permute-start.8 = (bf16[6,3,2,8,256]{4,3,2,1,0:T(8,128)(2,1)S(1)}, bf16[6,3,2,8,256]{4,3,2,1,0:T(8,128)(2,1)S(1)}, u32[]{:S(2)}, u32[]{:S(2)}) collective-permute-start(bf16[6,3,2,8,256]{4,3,2,1,0:T(8,128)(2,1)S(1)} %get-tuple-element.38), channel_id=1, source_target_pairs={{0,1},{1,2},{2,3},{3,4},{4,5},{5,6},{6,7},{7,8},{8,9},{9,10},{10,1... | collective-permute-start | bytes 442376 | tf_op jit(solution)/shard_map/ppermute | solution.py:396
  66.4 6.2 %collective-permute-start.9 = (bf16[6,3,2,8,256]{4,3,2,1,0:T(8,128)(2,1)S(1)}, bf16[6,3,2,8,256]{4,3,2,1,0:T(8,128)(2,1)S(1)}, u32[]{:S(2)}, u32[]{:S(2)}) collective-permute-start(bf16[6,3,2,8,256]{4,3,2,1,0:T(8,128)(2,1)S(1)} %get-tuple-element.39), channel_id=1, source_target_pairs={{1,0},{2,1},{3,2},{4,3},{5,4},{6,5},{7,6},{8,7},{9,8},{10,9},{11,1... | collective-permute-start | bytes 442376 | tf_op jit(solution)/shard_map/ppermute | solution.py:397
